TPU v7x, 256 devices: a whole 4x4x8 slice. The times are simulated.
256 devices in a mesh: row: 32 (over x, z_lo, core), col: 8 (over y, z_hi).
Axes of the slice: x: 4, y: 4, z: 8 (z_hi: 2, z_lo: 4; z = z_hi * 4 + z_lo), core: 2. Of those that a mesh axis runs over, the one named last changes fastest.
Arguments:
- embed: bfloat16 [2048, 512], P(('row', 'col')), may hold values from -6 to 6
- left_proj: bfloat16 [512, 32], replicated, may hold values from -0.25 to 0.25
- right_proj: bfloat16 [512, 32], replicated, may hold values from -0.25 to 0.25
- conv_w: bfloat16 [9, 32, 32], replicated, may hold values from -0.375 to 0.375
- cotangent: bfloat16 [32, 2048, 2048], P(None, 'row', 'col'), may hold values from -0.1796875 to 0.1796875
Outputs:
- pair_out: bfloat16 [32, 2048, 2048], P(None, 'row', 'col')
- conv_grad: float32 [9, 32, 32], replicated
- left_grad: float32 [512, 32], replicated
- right_grad: float32 [512, 32], replicated
- embed_grad: float32 [2048, 512], P(('row', 'col'))
All inputs are finite; a program needn't handle non-finite values.
Results may differ from a plain program's by a relative error of at most 0.0057.
Values may be sent and summed in bfloat16 or wider, within the bound.
A program may use at most 128 MiB of HBM per device.

v0:
```python
import jax
import jax.numpy as jnp
from jax import lax
from jax.sharding import PartitionSpec as P

DILATION_STEP = 4


def with_halo(shard, sides, width):
    for axis, dim in sides:
        count, length = (lax.axis_size(axis), shard.shape[dim])
        up = [(i, (i + 1) % count) for i in range(count - 1)]
        down = [(j, i) for i, j in up]
        last = lax.slice_in_dim(shard, length - width, length, axis=dim)
        initial = lax.slice_in_dim(shard, 0, width, axis=dim)
        before = lax.ppermute(last, axis, up)
        after = lax.ppermute(initial, axis, down)
        shard = jnp.concatenate([before, shard, after], axis=dim)
    return shard


def shards(embed, left_proj, right_proj, conv_w, cotangent):
    n_rowdev = lax.axis_size("row")
    n_coldev = lax.axis_size("col")
    bin_count = embed.shape[0]
    total_bins = bin_count * n_rowdev * n_coldev
    channels, row_bins, col_bins = cotangent.shape
    dilation_rate = DILATION_STEP
    row_index = lax.axis_index("row")
    col_index = lax.axis_index("col")
    row_first = row_index * row_bins
    col_first = col_index * col_bins
    whole = lax.all_gather(embed, ("row", "col"), axis=0, tiled=True)
    whole_pad = jnp.pad(whole, ((dilation_rate, dilation_rate), (0, 0)))
    row_embed = lax.dynamic_slice_in_dim(whole_pad, row_first, row_bins + 2 * dilation_rate, 0)
    col_embed = lax.dynamic_slice_in_dim(whole_pad, col_first, col_bins + 2 * dilation_rate, 0)
    left_widened = jnp.dot(row_embed, left_proj, preferred_element_type=jnp.float32).astype(
        jnp.bfloat16
    )
    right_wide = jnp.dot(col_embed, right_proj, preferred_element_type=jnp.float32).astype(
        jnp.bfloat16
    )
    left_table = left_widened.astype(jnp.float32).T
    right_table = right_wide.astype(jnp.float32).T
    left_mid = left_table[:, dilation_rate : dilation_rate + row_bins]
    right_mid = right_table[:, dilation_rate : dilation_rate + col_bins]
    summed_mid = left_mid[:, :, None] + right_mid[:, None, :]
    active_taps = jax.nn.softplus(summed_mid).astype(jnp.bfloat16)
    slope = jax.nn.sigmoid(summed_mid)
    padded_input = with_halo(active_taps, (("row", 1), ("col", 2)), DILATION_STEP)
    rows_global = row_first + jnp.arange(row_bins, dtype=jnp.int32)
    cols_global = col_first + jnp.arange(col_bins, dtype=jnp.int32)
    upper_mask = cols_global[None, :] >= rows_global[:, None]
    masked_pairs = jnp.where(upper_mask[None], cotangent, jnp.zeros((), jnp.bfloat16))
    padded_gradient = with_halo(masked_pairs, (("row", 1), ("col", 2)), DILATION_STEP)
    conv_out = jnp.zeros((channels, row_bins, col_bins), jnp.float32)
    input_grad = jnp.zeros((channels, row_bins, col_bins), jnp.float32)
    tap_grads = []
    for tap_row in range(3):
        for tap_col in range(3):
            tap = 3 * tap_row + tap_col
            window = padded_input[
                :,
                dilation_rate * tap_row : dilation_rate * tap_row + row_bins,
                dilation_rate * tap_col : dilation_rate * tap_col + col_bins,
            ]
            conv_out = conv_out + jnp.einsum(
                "oc,cij->oij", conv_w[tap], window, preferred_element_type=jnp.float32
            )
            shifted = padded_gradient[
                :,
                dilation_rate * (2 - tap_row) : dilation_rate * (2 - tap_row) + row_bins,
                dilation_rate * (2 - tap_col) : dilation_rate * (2 - tap_col) + col_bins,
            ]
            input_grad = input_grad + jnp.einsum(
                "oc,oij->cij", conv_w[tap], shifted, preferred_element_type=jnp.float32
            )
            tap_grads.append(
                jnp.einsum("oij,cij->oc", masked_pairs, window, preferred_element_type=jnp.float32)
            )
    pair_out = jnp.where(upper_mask[None], conv_out, 0.0).astype(jnp.bfloat16)
    pre_grad = input_grad * slope
    row_part = pre_grad.sum(2).T
    col_part = pre_grad.sum(1).T
    col_placed = lax.dynamic_update_slice_in_dim(
        jnp.zeros((total_bins, channels), jnp.float32), col_part, col_first, 0
    )
    row_grad = lax.psum_scatter(row_part, "col", scatter_dimension=0, tiled=True)
    col_grad = lax.psum_scatter(col_placed, ("row", "col"), scatter_dimension=0, tiled=True)
    highest = lax.Precision.HIGHEST
    embed_grad = jnp.dot(row_grad, left_proj.astype(jnp.float32).T, precision=highest) + jnp.dot(
        col_grad, right_proj.astype(jnp.float32).T, precision=highest
    )
    embed_local = embed.astype(jnp.float32)
    left_part = jnp.dot(embed_local.T, row_grad, precision=highest)
    right_part = jnp.dot(embed_local.T, col_grad, precision=highest)
    conv_sum, left_sum, right_sum = lax.psum(
        (jnp.stack(tap_grads), left_part, right_part), ("row", "col")
    )
    grad_scale = 32.0 / total_bins
    return (
        pair_out,
        conv_sum * grad_scale,
        left_sum * grad_scale,
        right_sum * grad_scale,
        embed_grad,
    )


def solution(mesh):
    in_specs = (P(("row", "col"), None), P(), P(), P(), P(None, "row", "col"))
    out_specs = (P(None, "row", "col"), P(), P(), P(), P(("row", "col"), None))
    return jax.shard_map(shards, mesh=mesh, in_specs=in_specs, out_specs=out_specs, check_vma=False)
```

profile of v0, /device:TPU:1, one launch (start us, length us, event | category | flops | bytes accessed | tf_op | source)
XLA Modules:
  0.0 1290.9 jit_solution(6177599002654644845)
XLA Ops:
  8.1 1.9 copy_select_fusion
  10.0 4.9 collective-permute-start.4
  14.9 1.9 collective-permute-start.5
  16.8 2.6 fusion.79
  21.8 1.3 collective-permute-start.6
  23.8 8.6 collective-permute-start.7
  32.4 2.5 fusion.13
  34.9 2.5 fusion.9
  38.5 1.8 copy.33
  40.2 2.5 maximum_maximum_fusion.1
  42.8 1.9 fusion.32
  44.6 1.9 fusion.36
  46.6 1.8 fusion.34
  48.4 1.8 fusion.38
  50.2 1.9 fusion.40
  52.1 656.7 %all-gather.2.cloned.1.call-done = bf16[2048,512]{1,0:T(8,128)(2,1)} async-done(((bf16[8,512]{1,0:T(8,128)(2,1)}), bf16[2048,512]{1,0:T(8,128)(2,1)}) %all-gather.2.cloned.1.call-update) | async-done | bytes 2097168 | tf_op jit(solution)/shard_map/all_gather | solution.py:33
  708.8 1.3 fusion.17
  710.8 6.8 fusion.126
  717.7 46.9 %all-reduce.1 = f32[64,32]{0,1:T(8,128)S(1)} all-reduce(f32[64,32]{0,1:T(8,128)S(1)} %copy.41), channel_id=2, replica_groups=mesh['row'=32,'col'=8] {'col'}, use_global_device_ids=true, to_apply=%region_2.3.clone | all-reduce | flops 2048 | bytes 16384
  765.7 1.3 fusion.8
  767.0 2.8 fusion.66
  770.6 8.1 collective-permute-start
  778.7 2.1 collective-permute-start.1
  782.0 2.5 collective-permute-done.1
  784.9 1.3 copy.23
  786.2 1.8 collective-permute-start.2
  788.8 1.3 collective-permute-start.3
  790.1 1.7 fusion.63
  791.8 1.7 fusion.64
  794.6 3.3 collective-permute-done.3
  797.8 1.8 copy.26
  799.6 1.5 pad_maximum_fusion
  801.2 1.2 fusion.26
  802.3 1.7 fusion.49
  804.1 1.8 fusion.55
  805.9 1.9 fusion.52
  807.8 1.9 fusion.58
  809.6 1.7 fusion.61
  814.6 2.0 fusion.22
  819.8 1.2 fusion.18
  821.0 83.3 %psum.21 = f32[9,32,32]{2,1,0:T(8,128)S(1)} all-reduce(f32[9,32,32]{2,1,0:T(8,128)} %fusion.18), channel_id=1, replica_groups=mesh['row'=32,'col'=8] {'row','col'}, use_global_device_ids=true, to_apply=%region_0.1 | all-reduce | flops 9216 | bytes 73728 | tf_op jit(solution)/shard_map/psum | solution.py:97
  904.3 7.0 fusion.42
  911.3 1.6 copy.43
  913.6 121.0 %all-reduce.7.cloned.1.call-done = f32[2048,32]{1,0:T(8,128)} async-done(((f32[2048,32]{1,0:T(8,128)}), f32[2048,32]{1,0:T(8,128)}) %all-reduce.7.cloned.1.call-update) | async-done | bytes 262160
  1034.6 1.5 convolution_bitcast_fusion
  1036.1 1.4 convolution_add_fusion
  1037.6 245.3 %all-reduce.9.cloned.1.call-done = (f32[512,32]{0,1:T(8,128)}, f32[512,32]{0,1:T(8,128)}) async-done(((f32[512,32]{0,1:T(8,128)}, f32[512,32]{0,1:T(8,128)}), (f32[512,32]{0,1:T(8,128)}, f32[512,32]{0,1:T(8,128)})) %all-reduce.9.cloned.1.call-update) | async-done | bytes 131088 | tf_op jit(solution)/shard_map/psum | solution.py:97
  1282.8 1.5 broadcast_multiply_fusion.1
  (74 shorter events, 17.4 us)
Async XLA Ops:
  7.2 701.6 %copy-start = (bf16[512,32]{0,1:T(8,128)(2,1)S(1)}, bf16[512,32]{0,1:T(8,128)(2,1)}, u32[]{:S(2)}) copy-start(bf16[512,32]{0,1:T(8,128)(2,1)} %param.7) | copy-start | bytes 98308
  7.2 701.6 %all-gather.2.cloned.1.call-start = ((), (), s32[]{:S(2)}) async-start(), calls=%async_computation | async-start | bytes 2105344 | tf_op jit(solution)/shard_map/all_gather | solution.py:33
  7.9 1026.7 %all-reduce.7.cloned.1.call-start = ((), (), s32[]{:S(2)}) async-start(), calls=%async_computation.1 | async-start | bytes 2097152
  9.9 9.5 copy-start.14
  10.0 10.7 collective-permute-start.4
  14.9 5.7 collective-permute-start.5
  20.7 14.2 %copy-start.5 = (bf16[32,4,256]{2,0,1:T(8,128)(2,1)}, bf16[32,4,256]{2,0,1:T(8,128)(2,1)S(1)}, u32[]{:S(2)}) copy-start(bf16[32,4,256]{2,0,1:T(8,128)(2,1)S(1)} %collective-permute-done.5) | copy-start | bytes 196612
  21.8 15.6 %collective-permute-start.6 = (bf16[32,72,4]{1,0,2:T(8,128)(2,1)S(1)}, bf16[32,72,4]{1,0,2:T(8,128)(2,1)S(1)}, u32[]{:S(2)}, u32[]{:S(2)}) collective-permute-start(bf16[32,72,4]{1,0,2:T(8,128)(2,1)S(1)} %copy.28), channel_id=1, source_target_pairs={{1,0},{2,1},{3,2},{4,3},{5,4},{6,5},{7,6},{9,8},{10,9},{11,10},{12... | collective-permute-start | bytes 55304 | tf_op jit(solution)/shard_map/ppermute | solution.py:17
  23.8 14.6 %collective-permute-start.7 = (bf16[32,72,4]{1,0,2:T(8,128)(2,1)S(1)}, bf16[32,72,4]{1,0,2:T(8,128)(2,1)S(1)}, u32[]{:S(2)}, u32[]{:S(2)}) collective-permute-start(bf16[32,72,4]{1,0,2:T(8,128)(2,1)S(1)} %copy.32), channel_id=1, source_target_pairs={{0,1},{1,2},{2,3},{3,4},{4,5},{5,6},{6,7},{8,9},{9,10},{10,11},{11... | collective-permute-start | bytes 55304 | tf_op jit(solution)/shard_map/ppermute | solution.py:16
  40.2 2.5 copy-start.6
  50.2 659.9 %copy-start.8 = (bf16[512,32]{0,1:T(8,128)(2,1)S(1)}, bf16[512,32]{0,1:T(8,128)(2,1)}, u32[]{:S(2)}) copy-start(bf16[512,32]{0,1:T(8,128)(2,1)} %param.6) | copy-start | bytes 98308
  52.1 658.7 %copy-start.7 = (bf16[9,32,32]{2,1,0:T(8,128)(2,1)S(1)}, bf16[9,32,32]{2,1,0:T(8,128)(2,1)}, u32[]{:S(2)}) copy-start(bf16[9,32,32]{2,1,0:T(8,128)(2,1)} %param.8) | copy-start | bytes 55300
  708.8 1.7 copy-start.3
  710.5 56.5 %copy-start.9 = (f32[32,256]{1,0:T(8,128)}, f32[32,256]{1,0:T(8,128)S(1)}, u32[]{:S(2)}) copy-start(f32[32,256]{1,0:T(8,128)S(1)} %slice_convert_fusion) | copy-start | bytes 98308
  710.8 56.2 %copy-start.11 = (f32[32,64]{0,1:T(8,128)}, f32[32,64]{0,1:T(8,128)S(1)}, u32[]{:S(2)}) copy-start(f32[32,64]{0,1:T(8,128)S(1)} %copy.22) | copy-start | bytes 24580
  710.8 54.1 %copy-start.13 = (bf16[8,512]{1,0:T(8,128)(2,1)S(1)}, bf16[8,512]{1,0:T(8,128)(2,1)}, u32[]{:S(2)}) copy-start(bf16[8,512]{1,0:T(8,128)(2,1)} %param.5) | copy-start | bytes 24580
  770.6 11.4 collective-permute-start
  778.7 5.8 collective-permute-start.1
  780.9 1.0 copy-start.4
  781.9 500.9 %all-reduce.9.cloned.1.call-start = ((), (), s32[]{:S(2)}) async-start(), calls=%async_computation.2 | async-start | bytes 262144 | tf_op jit(solution)/shard_map/psum | solution.py:97
  786.2 7.3 collective-permute-start.2
  788.8 9.0 collective-permute-start.3
  801.2 18.6 %copy-start.1 = (bf16[32,72,260]{2,0,1:T(8,128)(2,1)}, bf16[32,72,260]{2,0,1:T(8,128)(2,1)S(1)}, u32[]{:S(2)}) copy-start(bf16[32,72,260]{2,0,1:T(8,128)(2,1)S(1)} %get-tuple-element.23) | copy-start | bytes 3594244
  812.4 2.2 copy-start.10
  812.4 2.2 copy-start.12
  819.8 84.5 %copy-start.2 = (f32[64,256,32]{1,2,0:T(8,128)S(1)}, f32[64,256,32]{1,2,0:T(8,128)}, u32[]{:S(2)}) copy-start(f32[64,256,32]{1,2,0:T(8,128)} %fusion.63) | copy-start | bytes 6291460
Sparse Core Ops, SparseCore 0:
  9.9 698.8 all-gather.1
  782.0 252.4 all-reduce.6
  1041.7 241.0 all-reduce.8
where the time goes:
time: 1290 us
  waiting for transfers between devices  1030 us (80%)
  blocking collectives  130 us (10%)
  matrix products  62.3 us (5%)
  starting transfers between devices  30.1 us (2%)
  between operations  14.8 us (1%)
  local copies, waits for them, and re-layouts  14 us (1%)
    all_gather x1, waiting for transfers between devices, shards(): whole = lax.all_gather(embed, ('row', 'col'), axis=0, tiled=True)  657 us
    psum x1, waiting for transfers between devices, shards(): lax.psum((jnp.stack(tap_grads), left_part, right_part), ('row', 'col'))  245 us
    unnamed x4, waiting for transfers between devices  122 us
    psum x1, blocking collectives, shards(): lax.psum((jnp.stack(tap_grads), left_part, right_part), ('row', 'col'))  83.3 us
    unnamed x1, blocking collectives  46.9 us
  transfers between devices with their start and end apart: 11, of which 5 were waited for; matrix products, arithmetic and copies ran while one was open for 5% of the time, Pallas kernels for 0%

commit v1 on v0

v1 whole, which is shorter than its diff:
```python
import functools

import jax
import jax.numpy as jnp
from jax import lax
from jax.experimental import pallas as pl
from jax.experimental.pallas import tpu as pltpu
from jax.sharding import PartitionSpec as P

MESH = pl.DeviceIdType.MESH
STEP = 4
OUTSIDE = -1e30
F32 = jnp.float32
BF16 = jnp.bfloat16
VMEM = pl.BlockSpec(memory_space=pltpu.VMEM)


def iota(shape, dim):
    return lax.broadcasted_iota(jnp.int32, shape, dim)


def one_hot(cond):
    return jnp.where(cond, 1.0, 0.0).astype(BF16)


def dot(a, b):
    return jnp.dot(a, b, preferred_element_type=F32)


def dot_nt(a, b):
    return lax.dot_general(a, b, (((1,), (1,)), ((), ())), preferred_element_type=F32)


def dot_tn(a, b):
    return lax.dot_general(a, b, (((0,), (0,)), ((), ())), preferred_element_type=F32)


def halves(x):
    high = x.astype(BF16)
    return high, (x - high.astype(F32)).astype(BF16)


def loop(n, f):
    def body(k, _):
        f(k)
        return 0

    lax.fori_loop(0, n, body, 0)


def wait_bytes(ref, sem):
    pltpu.make_async_copy(ref, ref, sem).wait()


def gather_kernel(nr, nc, e_ref, lp_ref, rp_ref, lf_ref, rf_ref, proj, src, fill, rl, rr, sem_l, sem_r, send):
    r, c = lax.axis_index("row"), lax.axis_index("col")
    per = nr // nc
    me_b = r * nc + c
    ct, q = r // per, me_b % (per * nc)
    n_right = per * nc
    last = rr.shape[0] - 1
    barrier = pltpu.get_barrier_semaphore()

    def greet(dst_r, dst_c):
        pl.semaphore_signal(barrier, inc=1, device_id=(dst_r, dst_c), device_id_type=MESH)

    loop(nc, lambda k: pl.when(k != c)(lambda: greet(r, k)))
    pl.when(r > 0)(lambda: greet(r - 1, nc - 1))
    pl.when(r < nr - 1)(lambda: greet(r + 1, 0))

    def greet_other(a, b):
        pl.when((a != r) | (b != c))(lambda: greet(a, b))

    loop(n_right, lambda k: greet_other(per * c + k // nc, k % nc))

    low_self = (per * c - 1 == r) & (c == nc - 1)
    high_self = (per * c + per == r) & (c == 0)
    pl.when((c > 0) & jnp.logical_not(low_self))(lambda: greet(per * c - 1, nc - 1))
    pl.when((c < nc - 1) & jnp.logical_not(high_self))(lambda: greet(per * c + per, 0))

    proj[...] = jnp.zeros_like(proj)
    proj[:, 0:32] = lp_ref[...]
    proj[:, 32:64] = rp_ref[...]
    src[...] = dot(e_ref[...], proj[...]).astype(BF16).astype(F32)
    fill[...] = jnp.full_like(fill, OUTSIDE)
    rr[n_right + 1 : last] = jnp.zeros_like(rr[n_right + 1 : last])

    own = (c == ct).astype(jnp.int32)
    up_l = (c == nc - 1) & (r < nr - 1)
    down_l = (c == 0) & (r > 0)
    up_r = (q == n_right - 1) & (ct < nc - 1)
    down_r = (q == 0) & (ct > 0)
    own_up = (c == ct + 1).astype(jnp.int32)
    own_down = (c == ct - 1).astype(jnp.int32)
    n_sends = nc - 1 + n_right - own
    n_sends += jnp.where(up_l, nc, 0) + jnp.where(down_l, nc, 0)
    n_sends += jnp.where(up_r, n_right - own_up, 0) + jnp.where(down_r, n_right - own_down, 0)
    pl.semaphore_wait(barrier, n_sends)

    def put(dst_r, dst_c, dst, sem, cls):
        mine = (dst_r == r) & (dst_c == c)

        @pl.when(mine)
        def _():
            pltpu.make_async_copy(src, dst, sem).start()

        @pl.when(jnp.logical_not(mine))
        def _():
            pltpu.make_async_remote_copy(
                src, dst, send.at[cls], sem, device_id=(dst_r, dst_c), device_id_type=MESH
            ).start()

    loop(nc, lambda k: put(r, k, rl.at[c + 1], sem_l, 0))
    loop(n_right, lambda k: put(k, ct, rr.at[q], sem_r, 1))
    pl.when(up_l)(lambda: loop(nc, lambda k: put(r + 1, k, rl.at[0], sem_l, 2)))
    pl.when(down_l)(lambda: loop(nc, lambda k: put(r - 1, k, rl.at[nc + 1], sem_l, 3)))
    pl.when(up_r)(lambda: loop(n_right, lambda k: put(k, ct + 1, rr.at[last], sem_r, 4)))
    pl.when(down_r)(lambda: loop(n_right, lambda k: put(k, ct - 1, rr.at[n_right], sem_r, 5)))

    def outside(cond, dst, sem):
        pl.when(cond)(lambda: pltpu.make_async_copy(fill, dst, sem).start())

    outside(r == 0, rl.at[0], sem_l)
    outside(r == nr - 1, rl.at[nc + 1], sem_l)
    outside(c == 0, rr.at[last], sem_r)
    outside(c == nc - 1, rr.at[n_right], sem_r)

    wait_bytes(rl, sem_l)
    lf_ref[...] = rl[...].reshape(rl.shape[0] * 8, 128)[STEP : STEP + lf_ref.shape[0]]
    wait_bytes(rr.at[0 : n_right + 2], sem_r)
    rf_ref[...] = rr[...].reshape(rr.shape[0] * 8, 128).T[32:64]

    wait_bytes(rr.at[0 : nc - 1], send.at[0])
    pl.when(own == 1)(lambda: wait_bytes(rr.at[0 : n_right - 1], send.at[1]))
    pl.when(own == 0)(lambda: wait_bytes(rr.at[0:n_right], send.at[1]))
    pl.when(up_l)(lambda: wait_bytes(rr.at[0:nc], send.at[2]))
    pl.when(down_l)(lambda: wait_bytes(rr.at[0:nc], send.at[3]))
    for cond, mine, sem in ((up_r, own_up, send.at[4]), (down_r, own_down, send.at[5])):
        pl.when(cond & (mine == 1))(lambda s=sem: wait_bytes(rr.at[0 : n_right - 1], s))
        pl.when(cond & (mine == 0))(lambda s=sem: wait_bytes(rr.at[0:n_right], s))


def build_taps(w_ref, tf, tb):
    spread = one_hot(iota((256, 32), 0) // 8 == iota((256, 32), 1))
    widen = one_hot(iota((32, 256), 1) // 8 == iota((32, 256), 0))
    s0, s1 = iota((256, 256), 0) % 8, iota((256, 256), 1) % 8
    same, above, below = s1 == s0, s1 == s0 + 4, s1 == s0 - 4

    def expand(x):
        return dot(spread, x.astype(BF16))

    for b in range(3):
        x = [expand(dot(w_ref[3 * a + b], widen)) for a in range(3)]
        tf[:, 256 * b : 256 * b + 256] = jnp.where(same, x[0], jnp.where(above, x[1], 0.0)).astype(BF16)
        tf[:, 768 + 256 * b : 1024 + 256 * b] = jnp.where(same, x[2], jnp.where(below, x[1], 0.0)).astype(BF16)
        y = [expand(dot_tn(w_ref[3 * a + b], widen)) for a in range(3)]
        rows = slice(256 * b, 256 * b + 256)
        tb[rows, 0:256] = jnp.where(same, y[2], jnp.where(above, y[1], 0.0)).astype(BF16)
        tb[rows, 256:512] = jnp.where(same, y[0], jnp.where(below, y[1], 0.0)).astype(BF16)


def mask_cotangent(r, c, cot_ref, m2):
    zero = jnp.zeros((256, 256), BF16)
    m2[:, 0:256] = zero
    m2[:, 2304:2560] = zero
    for k in range(4):
        x = cot_ref[:, 16 * k : 16 * k + 16, :].astype(F32)
        row = r * 64 + 16 * k + iota((16, 256), 0)
        col = c * 256 + iota((16, 256), 1)
        x = jnp.where((col >= row)[None], x, 0.0)
        m2[:, 256 * (2 * k + 1) : 256 * (2 * k + 2)] = x[:, 0:8].reshape(256, 256).astype(BF16)
        m2[:, 256 * (2 * k + 2) : 256 * (2 * k + 3)] = x[:, 8:16].reshape(256, 256).astype(BF16)


def lanes(h):
    return pl.ds(pl.multiple_of(h * 256, 256), 256)


def input_gradient(m2, tb, z):
    def body(h, _):
        pair = jnp.concatenate([m2[:, lanes(h)], m2[:, lanes(h + 1)]], axis=0)
        z[h] = dot(tb[...], pair)
        return 0

    lax.fori_loop(0, 9, body, 0)


def elementwise(lf, rf, z, a2, cacc, rowp):
    cacc[...] = jnp.zeros_like(cacc)
    rowp[...] = jnp.zeros_like(rowp)
    lane = iota((8, 128), 1)

    def body(h, _):
        base = pl.multiple_of(h * 8, 8)
        left = lf[pl.ds(base, 8), :]
        row = jnp.zeros((8, 128), F32)
        for pair in range(16):
            acts = []
            for c in (2 * pair, 2 * pair + 1):
                s = left[:, c : c + 1] + rf[c : c + 1, :]
                t = jnp.exp(-jnp.abs(s))
                act = jnp.maximum(s, 0.0) + jnp.log1p(t)
                slope = jnp.where(s >= 0, 1.0, t) / (1.0 + t)
                acts.append(act)
                total = jnp.zeros((8, 128), F32)
                for b, shift in enumerate((4, 0, 380)):
                    moved = pltpu.roll(slope, shift, 1) if shift else slope
                    p = z[h, pl.ds(256 * b + 8 * c, 8), :] * moved[:, 0:256]
                    cacc[b, 8 * c : 8 * c + 8, :] += p
                    total += p[:, 0:128] + p[:, 128:256]
                row = jnp.where(lane == c, jnp.sum(total, axis=1, keepdims=True), row)
            for b, shift in enumerate((4, 0, 380)):
                both = [(pltpu.roll(x, shift, 1) if shift else x)[:, 0:256] for x in acts]
                a2[b, 16 * pair : 16 * pair + 16, lanes(h)] = jnp.concatenate(both, axis=0).astype(BF16)
        rowp[pl.ds(base + 4, 8), :] = row
        return 0

    lax.fori_loop(0, 9, body, 0)


def column_sums(cacc, colp):
    pick = one_hot(iota((256, 128), 0) // 8 + 32 == iota((256, 128), 1))
    colp[...] = jnp.zeros_like(colp)
    for b in range(3):
        high, low = halves(cacc[b])
        colp[4 + 4 * b : 260 + 4 * b, :] += dot_tn(high, pick) + dot_tn(low, pick)


def convolve(r, c, a2, tf, out_ref):
    def body(k, _):
        parts = []
        for g in (2 * k, 2 * k + 1):
            stack = [a2[b, :, lanes(g + u)] for u in range(2) for b in range(3)]
            y = dot(tf[...], jnp.concatenate(stack, axis=0))
            parts.append(y.reshape(32, 8, 256))
        y = jnp.concatenate(parts, axis=1)
        row = r * 64 + 16 * k + iota((16, 256), 0)
        col = c * 256 + iota((16, 256), 1)
        y = jnp.where((col >= row)[None], y, 0.0).astype(BF16)
        out_ref[:, pl.ds(pl.multiple_of(16 * k, 16), 16), :] = y
        return 0

    lax.fori_loop(0, 4, body, 0)


def tap_gradient(m2, a2, taps):
    s0, s1 = iota((256, 256), 0) % 8, iota((256, 256), 1) % 8
    same, above, below = s1 == s0, s1 == s0 + 4, s1 == s0 - 4
    gather_rows = one_hot(iota((32, 256), 1) // 8 == iota((32, 256), 0))
    taps[...] = jnp.zeros_like(taps)
    for b in range(3):
        g0 = dot_nt(m2[:, 256:2304], a2[b, :, 0:2048])
        g1 = dot_nt(m2[:, 256:2304], a2[b, :, 256:2304])
        ys = (
            jnp.where(same, g0, 0.0),
            jnp.where(above, g0, jnp.where(below, g1, 0.0)),
            jnp.where(same, g1, 0.0),
        )
        for a in range(3):
            q, k = divmod(3 * a + b, 4)
            pick = one_hot(iota((256, 128), 0) // 8 + 32 * k == iota((256, 128), 1))
            high, low = halves(ys[a])
            rows = dot(gather_rows, high) + dot(gather_rows, low)
            high, low = halves(rows)
            taps[32 * q : 32 * q + 32, :] += dot(high, pick) + dot(low, pick)


def compute_kernel(lf, rf, cot_ref, w_ref, out_ref, taps, rowp, colp, m2, a2, z, tf, tb, cacc):
    r, c = lax.axis_index("row"), lax.axis_index("col")
    build_taps(w_ref, tf, tb)
    mask_cotangent(r, c, cot_ref, m2)
    input_gradient(m2, tb, z)
    elementwise(lf, rf, z, a2, cacc, rowp)
    column_sums(cacc, colp)
    convolve(r, c, a2, tf, out_ref)
    tap_gradient(m2, a2, taps)


def reduce_kernel(
    nr, nc, e_ref, lp_ref, rp_ref, rowp, colp, taps,
    sums_ref, eg_ref,
    proj, rrow, rrow2, rcol, rcol2, buf, r1, r2, r3, mid, fin, recv, send,
):
    r, c = lax.axis_index("row"), lax.axis_index("col")
    per = nr // nc
    n_right = per * nc
    me_b = r * nc + c
    ct, q = r // per, me_b % n_right
    k1 = (r % 8) * 2 + c % 2
    k2 = (r // 8) * 4 + c // 2

    def member1(k):
        return r // 8 * 8 + k // 2, c // 2 * 2 + k % 2

    def member2(k):
        return k // 4 * 8 + r % 8, k % 4 * 2 + c % 2

    barrier = pltpu.get_barrier_semaphore()

    def greet(dst_r, dst_c):
        pl.semaphore_signal(barrier, inc=1, device_id=(dst_r, dst_c), device_id_type=MESH)

    up_l = (c == nc - 1) & (r < nr - 1)
    down_l = (c == 0) & (r > 0)
    up_r = (q == n_right - 1) & (ct < nc - 1)
    down_r = (q == 0) & (ct > 0)

    def greet_other(a, b):
        pl.when((a != r) | (b != c))(lambda: greet(a, b))

    loop(nc, lambda k: greet_other(r, k))
    loop(nr, lambda k: greet_other(k, ct))
    pl.when(up_l)(lambda: loop(nc, lambda k: greet(r + 1, k)))
    pl.when(down_l)(lambda: loop(nc, lambda k: greet(r - 1, k)))
    pl.when(up_r)(lambda: loop(nr, lambda k: greet_other(k, ct + 1)))
    pl.when(down_r)(lambda: loop(nr, lambda k: greet_other(k, ct - 1)))
    loop(16, lambda k: greet_other(*member1(k)))
    loop(16, lambda k: greet_other(*member2(k)))

    own = (c == ct).astype(jnp.int32)
    low_self = (per * c - 1 == r) & (c == nc - 1)
    high_self = (per * c + per == r) & (c == 0)
    n_sends = nc - 1 + n_right - own + 30
    n_sends += jnp.where(r > 0, 1, 0) + jnp.where(r < nr - 1, 1, 0)
    n_sends += jnp.where((c > 0) & jnp.logical_not(low_self), 1, 0)
    n_sends += jnp.where((c < nc - 1) & jnp.logical_not(high_self), 1, 0)
    pl.semaphore_wait(barrier, n_sends)

    def put(src, dst_r, dst_c, dst, sem, cls):
        mine = (dst_r == r) & (dst_c == c)

        @pl.when(mine)
        def _():
            pltpu.make_async_copy(src, dst, recv.at[sem]).start()

        @pl.when(jnp.logical_not(mine))
        def _():
            pltpu.make_async_remote_copy(
                src, dst, send.at[cls], recv.at[sem], device_id=(dst_r, dst_c), device_id_type=MESH
            ).start()

    loop(n_right, lambda k: put(colp.at[k + 1], per * c + k // nc, k % nc, rcol.at[r], 0, 0))
    loop(nc, lambda k: put(rowp.at[k + 1], r, k, rrow.at[c], 1, 1))
    pl.when(c > 0)(lambda: put(colp.at[0], per * c - 1, nc - 1, rcol2.at[r], 2, 2))
    pl.when(c < nc - 1)(lambda: put(colp.at[n_right + 1], per * c + per, 0, rcol2.at[r], 2, 3))
    pl.when(r > 0)(lambda: put(rowp.at[0], r - 1, nc - 1, rrow2.at[c], 3, 4))
    pl.when(r < nr - 1)(lambda: put(rowp.at[nc + 1], r + 1, 0, rrow2.at[c], 3, 5))

    proj[...] = jnp.zeros_like(proj)
    proj[:, 0:32] = lp_ref[...]
    proj[:, 32:64] = rp_ref[...]
    buf[...] = jnp.zeros_like(buf)
    for k in range(taps.shape[0] // 8):
        buf[k, :, 256:384] = taps[8 * k : 8 * k + 8, :]

    rrow2_wanted = up_l | down_l
    rcol2_wanted = up_r | down_r
    pl.when(jnp.logical_not(rrow2_wanted))(lambda: rrow2.__setitem__(..., jnp.zeros(rrow2.shape, F32)))
    pl.when(jnp.logical_not(rcol2_wanted))(lambda: rcol2.__setitem__(..., jnp.zeros(rcol2.shape, F32)))
    wait_bytes(rrow, recv.at[1])
    wait_bytes(rcol, recv.at[0])
    pl.when(rcol2_wanted)(lambda: wait_bytes(rcol2, recv.at[2]))
    pl.when(rrow2_wanted)(lambda: wait_bytes(rrow2, recv.at[3]))
    grads = jnp.sum(rrow[...], axis=0) + jnp.sum(rcol[...], axis=0)
    grads += jnp.sum(rrow2[...], axis=0) + jnp.sum(rcol2[...], axis=0)
    high, low = halves(grads)
    lr = dot_tn(high, e_ref[...]) + dot_tn(low, e_ref[...])
    for k in range(16):
        buf[k, :, 0:256] = lr[8 * (k // 2) : 8 * (k // 2) + 8, 256 * (k % 2) : 256 * (k % 2) + 256]

    loop(16, lambda k: put(buf.at[k], *member1(k), r1.at[k1], 4, 6))
    eg_ref[...] = dot_nt(high, proj[...]) + dot_nt(low, proj[...])
    wait_bytes(r1, recv.at[4])
    mid[...] = jnp.sum(r1[...], axis=0)
    loop(16, lambda k: put(mid, *member2(k), r2.at[k2], 5, 7))
    wait_bytes(r2, recv.at[5])
    fin[...] = jnp.sum(r2[...], axis=0)
    loop(16, lambda k: put(fin, *member1(k), r3.at[k1], 6, 8))
    wait_bytes(r3, recv.at[6])
    sums_ref[...] = r3[...]

    pl.when(own == 1)(lambda: wait_bytes(rcol.at[0 : n_right - 1], send.at[0]))
    pl.when(own == 0)(lambda: wait_bytes(rcol.at[0:n_right], send.at[0]))
    wait_bytes(rrow.at[0 : nc - 1], send.at[1])
    pl.when((c > 0) & jnp.logical_not(low_self))(lambda: wait_bytes(colp.at[0], send.at[2]))
    pl.when((c < nc - 1) & jnp.logical_not(high_self))(lambda: wait_bytes(colp.at[0], send.at[3]))
    pl.when(r > 0)(lambda: wait_bytes(rowp.at[0], send.at[4]))
    pl.when(r < nr - 1)(lambda: wait_bytes(rowp.at[0], send.at[5]))
    for cls in (6, 7, 8):
        wait_bytes(r1.at[0:15], send.at[cls])


def finish_kernel(scale, sums, conv_ref, left_ref, right_ref):
    for k in range(9):
        q, at = divmod(k, 4)
        for part in range(4):
            piece = sums[4 * q + part, :, 256 + 32 * at : 288 + 32 * at]
            conv_ref[k, 8 * part : 8 * part + 8, :] = piece * scale
    for ref, first in ((left_ref, 0), (right_ref, 8)):
        for half in range(2):
            block = jnp.concatenate([sums[first + 2 * part + half, :, 0:256] for part in range(4)], axis=0)
            ref[256 * half : 256 * half + 256, :] = block.T * scale


def run_compute(lf, rf, cot, w):
    return pl.pallas_call(
        compute_kernel,
        out_shape=(
            jax.ShapeDtypeStruct((32, 64, 256), BF16),
            jax.ShapeDtypeStruct((96, 128), F32),
            jax.ShapeDtypeStruct((80, 128), F32),
            jax.ShapeDtypeStruct((272, 128), F32),
        ),
        in_specs=[VMEM] * 4,
        out_specs=(VMEM,) * 4,
        scratch_shapes=[
            pltpu.VMEM((256, 2560), BF16),
            pltpu.VMEM((3, 256, 2304), BF16),
            pltpu.VMEM((9, 768, 256), F32),
            pltpu.VMEM((256, 1536), BF16),
            pltpu.VMEM((768, 512), BF16),
            pltpu.VMEM((3, 256, 256), F32),
        ],
        compiler_params=pltpu.CompilerParams(vmem_limit_bytes=56 * 1024 * 1024),
        name="pair_compute",
    )(lf, rf, cot, w)


def shards(nr, nc, embed, left_proj, right_proj, conv_w, cotangent):
    lf, rf = pl.pallas_call(
        functools.partial(gather_kernel, nr, nc),
        out_shape=(jax.ShapeDtypeStruct((72, 128), F32), jax.ShapeDtypeStruct((32, 384), F32)),
        in_specs=[VMEM] * 3,
        out_specs=(VMEM,) * 2,
        scratch_shapes=[
            pltpu.VMEM((512, 128), BF16),
            pltpu.VMEM((8, 128), F32),
            pltpu.VMEM((8, 128), F32),
            pltpu.VMEM((nc + 2, 8, 128), F32),
            pltpu.VMEM((48, 8, 128), F32),
            pltpu.SemaphoreType.DMA,
            pltpu.SemaphoreType.DMA,
            pltpu.SemaphoreType.DMA((6,)),
        ],
        compiler_params=pltpu.CompilerParams(
            collective_id=0, has_side_effects=True, vmem_limit_bytes=32 * 1024 * 1024
        ),
        name="feature_gather",
    )(embed, left_proj, right_proj)
    pair_out, taps, rowp, colp = run_compute(lf, rf, cotangent, conv_w)
    sums, embed_grad = pl.pallas_call(
        functools.partial(reduce_kernel, nr, nc),
        out_shape=(jax.ShapeDtypeStruct((16, 8, 384), F32), jax.ShapeDtypeStruct((8, 512), F32)),
        in_specs=[VMEM] * 6,
        out_specs=(VMEM,) * 2,
        scratch_shapes=[
            pltpu.VMEM((512, 128), BF16),
            pltpu.VMEM((nc, 8, 128), F32),
            pltpu.VMEM((nc, 8, 128), F32),
            pltpu.VMEM((nr, 8, 128), F32),
            pltpu.VMEM((nr, 8, 128), F32),
            pltpu.VMEM((16, 8, 384), F32),
            pltpu.VMEM((16, 8, 384), F32),
            pltpu.VMEM((16, 8, 384), F32),
            pltpu.VMEM((16, 8, 384), F32),
            pltpu.VMEM((8, 384), F32),
            pltpu.VMEM((8, 384), F32),
            pltpu.SemaphoreType.DMA((7,)),
            pltpu.SemaphoreType.DMA((9,)),
        ],
        compiler_params=pltpu.CompilerParams(
            collective_id=1, has_side_effects=True, vmem_limit_bytes=32 * 1024 * 1024
        ),
        name="reduce_sums",
    )(embed, left_proj, right_proj, rowp.reshape(10, 8, 128), colp.reshape(34, 8, 128), taps)
    conv_grad, left_grad, right_grad = pl.pallas_call(
        functools.partial(finish_kernel, 32.0 / (8 * nr * nc)),
        out_shape=(
            jax.ShapeDtypeStruct((9, 32, 32), F32),
            jax.ShapeDtypeStruct((512, 32), F32),
            jax.ShapeDtypeStruct((512, 32), F32),
        ),
        in_specs=[VMEM],
        out_specs=(VMEM,) * 3,
        name="finish",
    )(sums)
    return pair_out, conv_grad, left_grad, right_grad, embed_grad


def solution(mesh):
    body = functools.partial(shards, mesh.shape["row"], mesh.shape["col"])
    in_specs = (P(("row", "col"), None), P(), P(), P(), P(None, "row", "col"))
    out_specs = (P(None, "row", "col"), P(), P(), P(), P(("row", "col"), None))
    return jax.shard_map(body, mesh=mesh, in_specs=in_specs, out_specs=out_specs, check_vma=False)
```

time: 1290 us -> 107 us (0.08)
  waiting for transfers between devices: 1030 us -> 0 us
  blocking collectives: 130 us -> 0 us
  Pallas kernels: 0 us -> 96.7 us
  matrix products: 62.3 us -> 0 us
  starting transfers between devices: 30.1 us -> 0 us
  between operations: 14.8 us -> 0.7 us
    all_gather x1 -> x0, waiting for transfers between devices: 657 us -> none  [shards(): whole = lax.all_gather(embed, ('row', 'col'), axis=0, tiled=True)]
    psum x1 -> x0, waiting for transfers between devices: 245 us -> none  [shards(): lax.psum((jnp.stack(tap_grads), left_part, right_part), ('row', 'col'))]
    unnamed x4 -> x0, waiting for transfers between devices: 122 us -> none
    pallas_call x0 -> x4, Pallas kernels: none -> 96.7 us  [the longest x1 39.7 us: run_compute(): pl.pallas_call(compute_kernel, out_shape=(jax.ShapeDtypeStruct((32, 64, 2...]
    psum x1 -> x0, blocking collectives: 83.3 us -> none  [shards(): lax.psum((jnp.stack(tap_grads), left_part, right_part), ('row', 'col'))]
    dot_general x33 -> x0, matrix products: 62.3 us -> none  [the longest x9 23.7 us: shards(): jnp.einsum('oc,oij->cij', conv_w[tap], shifted, preferred_element_type=jn...]
    unnamed x1 -> x0, blocking collectives: 46.9 us -> none
    ppermute x8 -> x0, starting transfers between devices: 30 us -> none  [the longest x4 23.4 us: with_halo(): before = lax.ppermute(last, axis, up)]
  transfers between devices with their start and end apart: 11 -> 0, of which waited for: 5 -> 0; matrix products, arithmetic and copies ran while one was open for 5% -> 0% of each run, Pallas kernels for 0% -> 0%
where the time goes in v1:
time: 107 us; the launch traced here: 106 us
  Pallas kernels  96.7 us (90%)
  local copies, waits for them, and re-layouts  9.03 us (8%)
    pallas_call x1, Pallas kernels, run_compute(): pl.pallas_call(compute_kernel, out_shape=(jax.ShapeDtypeStruct((32, 64, 2...  39.7 us
    pallas_call x1, Pallas kernels, shards(): pl.pallas_call(functools.partial(reduce_kernel, nr, nc), out_shape=(jax.S...  38.3 us
    pallas_call x1, Pallas kernels, shards(): pl.pallas_call(functools.partial(gather_kernel, nr, nc), out_shape=(jax.S...  16.7 us
    unnamed x23, local copies, waits for them, and re-layouts  9.03 us

profile of v1, /device:TPU:1, one launch (start us, length us, event | category | flops | bytes accessed | tf_op | source)
XLA Modules:
  0.0 106.4 jit_solution(3685808257608308050)
XLA Ops:
  0.6 0.0 copy-start.8
  0.6 0.9 copy.10.lp_ref
  1.5 0.0 copy-done.8
  1.5 0.0 copy-start.6
  1.5 0.1 copy.11.rp_ref
  1.7 0.6 copy-done.6
  2.2 16.7 %feature_gather.1 = (f32[72,128]{1,0:T(8,128)S(1)}, f32[32,384]{1,0:T(8,128)S(1)}) custom-call(bf16[8,512]{1,0:T(8,128)(2,1)S(1)} %copy-done.6, bf16[512,32]{1,0:T(8,128)(2,1)S(1)} %copy.10.lp_ref, bf16[512,32]{1,0:T(8,128)(2,1)S(1)} %copy.11.rp_ref), custom_call_target="tpu_custom_call" | custom-call | tf_op jit(solution)/shard_map/feature_gather/pallas_call | solution.py:430
  18.9 0.0 copy-start.2
  19.0 0.6 copy-done.2
  19.6 0.0 copy-start.5
  19.6 0.6 copy-done.5
  20.2 39.7 %pair_compute.1 = (bf16[32,64,256]{2,1,0:T(8,128)(2,1)}, f32[96,128]{1,0:T(8,128)}, f32[80,128]{1,0:T(8,128)}, f32[272,128]{1,0:T(8,128)}) custom-call(f32[72,128]{1,0:T(8,128)} %copy-done.5, f32[32,384]{1,0:T(8,128)} %copy-done.2, bf16[32,64,256]{2,1,0:T(8,128)(2,1)} %cot_ref.1, bf16[9,32,32]{2,1,0:T(8,128)(2,1)} %w_ref.1), custom_call_target="tpu_custom_call" | custom-call | tf_op jit(solution)/shard_map/pair_compute/pallas_call | solution.py:406
  59.9 0.0 copy-start.1
  59.9 0.9 copy-done.1
  60.8 0.0 copy-start.3
  60.8 0.8 copy-done.3
  61.6 0.0 copy-start.4
  61.6 0.8 copy-done.4
  62.3 38.3 %reduce_sums.1 = (f32[16,8,384]{2,1,0:T(8,128)S(1)}, f32[8,512]{1,0:T(8,128)S(1)}) custom-call(bf16[8,512]{1,0:T(8,128)(2,1)S(1)} %copy-done.6, bf16[512,32]{1,0:T(8,128)(2,1)S(1)} %copy.10.lp_ref, bf16[512,32]{1,0:T(8,128)(2,1)S(1)} %copy.11.rp_ref, f32[10,8,128]{2,1,0:T(8,128)S(1)} %bitcast.3, f32[34,8,128]{2,1,0:T(8,128)S(1)} %bitcast.2, ...), custom_call_target="tpu_custom_call" | custom-call | tf_op jit(solution)/shard_map/reduce_sums/pallas_call | solution.py:451
  100.7 0.0 copy-start
  100.7 0.7 copy-done
  101.4 2.0 %finish.1 = (f32[9,32,32]{2,1,0:T(8,128)}, f32[512,32]{1,0:T(8,128)}, f32[512,32]{1,0:T(8,128)}) custom-call(f32[16,8,384]{2,1,0:T(8,128)} %copy-done), custom_call_target="tpu_custom_call" | custom-call | tf_op jit(solution)/shard_map/finish/pallas_call | solution.py:476
  103.3 0.0 copy-start.7
  103.3 1.7 %copy.14 = f32[512,32]{0,1:T(8,128)} copy(f32[512,32]{1,0:T(8,128)} %get-tuple-element.29) | data formatting | bytes 131072
  105.1 0.0 copy-done.7
  105.1 0.7 copy.15
  105.8 0.6 copy.17
Async XLA Ops:
  0.6 0.9 copy-start.8
  1.5 0.7 copy-start.6
  18.9 0.6 copy-start.2
  19.6 0.6 copy-start.5
  59.9 0.9 copy-start.1
  60.8 0.8 copy-start.3
  61.6 0.8 copy-start.4
  100.7 0.7 copy-start
  103.3 1.7 %copy-start.7 = (f32[512,32]{1,0:T(8,128)S(1)}, f32[512,32]{1,0:T(8,128)}, u32[]{:S(2)}) copy-start(f32[512,32]{1,0:T(8,128)} %get-tuple-element.30) | copy-start | bytes 196612

commit v2 on v0

v2 whole, which is shorter than its diff:
```python
import functools

import jax
import jax.numpy as jnp
from jax import lax
from jax.experimental import pallas as pl
from jax.experimental.pallas import tpu as pltpu
from jax.sharding import PartitionSpec as P

MESH = pl.DeviceIdType.MESH
OUTSIDE = -1e30
LOG2E = 1.4426950408889634
LN2 = 0.6931471805599453
F32 = jnp.float32
BF16 = jnp.bfloat16
VMEM = pl.BlockSpec(memory_space=pltpu.VMEM)
HBM = pl.BlockSpec(memory_space=pltpu.HBM)


def iota(shape, dim):
    return lax.broadcasted_iota(jnp.int32, shape, dim)


def one_hot(cond):
    return jnp.where(cond, 1.0, 0.0).astype(BF16)


def dot(a, b):
    return jnp.dot(a, b, preferred_element_type=F32)


def dot_nt(a, b):
    return lax.dot_general(a, b, (((1,), (1,)), ((), ())), preferred_element_type=F32)


def dot_tn(a, b):
    return lax.dot_general(a, b, (((0,), (0,)), ((), ())), preferred_element_type=F32)


def halves(x):
    high = x.astype(BF16)
    return high, (x - high.astype(F32)).astype(BF16)


def loop(n, f):
    def body(k, _):
        f(k)
        return 0

    lax.fori_loop(0, n, body, 0)


def lanes(h):
    return pl.ds(pl.multiple_of(h * 256, 256), 256)


def wait_bytes(ref, sem):
    pltpu.make_async_copy(ref, ref, sem).wait()


def softplus_and_slope(s):
    t = jnp.exp2(-jnp.abs(s * LOG2E))
    u = 1.0 + t
    inv = pl.reciprocal(u, approx=True)
    inv = inv * (2.0 - u * inv)
    log = jnp.where(t < 1 / 256, t - 0.5 * t * t, LN2 * jnp.log2(u))
    return jnp.maximum(s, 0.0) + log, jnp.where(s >= 0, inv, t * inv)


def build_taps(w_ref, tf, tb):
    spread = one_hot((iota((256, 32), 0) >> 3) == iota((256, 32), 1))
    widen = one_hot((iota((32, 256), 1) >> 3) == iota((32, 256), 0))
    s0, s1 = (iota((256, 256), 0) & 7), (iota((256, 256), 1) & 7)
    same, above, below = s1 == s0, s1 == s0 + 4, s1 == s0 - 4

    def expand(x):
        return dot(spread, x.astype(BF16))

    for b in range(3):
        x = [expand(dot(w_ref[3 * a + b], widen)) for a in range(3)]
        tf[:, 256 * b : 256 * b + 256] = jnp.where(same, x[0], jnp.where(above, x[1], 0.0)).astype(BF16)
        tf[:, 768 + 256 * b : 1024 + 256 * b] = jnp.where(same, x[2], jnp.where(below, x[1], 0.0)).astype(BF16)
        y = [expand(dot_tn(w_ref[3 * a + b], widen)) for a in range(3)]
        tb[:, 512 * b : 512 * b + 256] = jnp.where(same, y[2], jnp.where(above, y[1], 0.0)).astype(BF16)
        tb[:, 512 * b + 256 : 512 * b + 512] = jnp.where(same, y[0], jnp.where(below, y[1], 0.0)).astype(BF16)


def build_shift(shift):
    k, n = iota((256, 512), 0), iota((256, 512), 1)
    shift[...] = one_hot(k == jnp.where(n < 256, n - 4, n - 252))


def mask_cotangent(r, c, cot_ref, shift, m3):
    for b in range(3):
        m3[b, :, 0:256] = jnp.zeros((256, 256), BF16)
        m3[b, :, 2304:2560] = jnp.zeros((256, 256), BF16)
    for k in range(4):
        x = cot_ref[:, 16 * k : 16 * k + 16, :].astype(F32)
        row = r * 64 + 16 * k + iota((16, 256), 0)
        x = jnp.where((c * 256 + iota((16, 256), 1) >= row)[None], x, 0.0)
        for half in range(2):
            m3[1, :, lanes(2 * k + half + 1)] = x[:, 8 * half : 8 * half + 8].reshape(256, 256).astype(BF16)

    def body(g):
        moved = dot(m3[1, :, lanes(g + 1)], shift[...]).astype(BF16)
        m3[2, :, lanes(g + 1)] = moved[:, 0:256]
        m3[0, :, lanes(g + 1)] = moved[:, 256:512]

    loop(8, body)


def input_gradient(m3, tb, z):
    def body(h):
        stack = [m3[b, :, lanes(h + u)] for b in range(3) for u in range(2)]
        z[h] = dot(tb[...], jnp.concatenate(stack, axis=0))

    loop(9, body)


def input_gradient_edge(m3, tb, z_edge):
    lane = iota((256, 128), 1)
    edges = jnp.zeros((256, 128), BF16)
    for g in range(8):
        at = 256 * (g + 1)
        ends = jnp.where(lane < 64, m3[1, :, at : at + 128], m3[1, :, at + 128 : at + 256])
        edges = jnp.where((lane >> 3) == g + 1, pltpu.roll(ends, (8 * g + 12) % 128, 1), edges)
    pair = jnp.concatenate([edges, pltpu.roll(edges, 120, 1)], axis=0)
    z_edge[...] = jnp.where((lane & 7) < 4, dot(tb[:, 1024:1536], pair), dot(tb[:, 0:512], pair))


def edge_part(lf, around, z_edge, act_edge, p_edge, left_m):
    spread = one_hot((iota((256, 128), 0) >> 3) == iota((256, 128), 1))
    spread_right = one_hot((iota((256, 128), 0) >> 3) + 32 == iota((256, 128), 1))
    row, lane = iota((256, 128), 0), iota((256, 128), 1)
    rows = jnp.concatenate([lf[...], jnp.zeros((56, 128), F32)], axis=0).astype(BF16)
    left = jnp.where((lane & 7) == (row & 7), dot_nt(spread, rows), 0.0).astype(BF16)
    left_m[...] = left
    block = one_hot((iota((128, 128), 0) >> 3) == (iota((128, 128), 1) >> 3))
    right = jnp.concatenate([around] * 16, axis=0).astype(BF16)
    act, slope = softplus_and_slope(dot(left, block) + dot_nt(spread_right, right))
    act_edge[...] = act.astype(BF16)
    p_edge[...] = slope * z_edge[...]


def elementwise(rf, z, act_edge, p_edge, left_m, shift, lb, a2, cacc, rhi, rlo):
    cacc[...] = jnp.zeros_like(cacc)

    def body(h):
        lb[...] = dot(left_m[...], one_hot((iota((128, 128), 0) >> 3) == h))
        here = (iota((8, 128), 1) >> 3) == h
        at = pl.ds(pl.multiple_of(h * 128, 128), 128)
        for pair in range(16):
            acts, totals = [], []
            for c in (2 * pair, 2 * pair + 1):
                rows = slice(8 * c, 8 * c + 8)
                total = jnp.where(here, p_edge[rows, :], 0.0)
                parts = []
                for tile in (slice(0, 128), slice(128, 256)):
                    act, slope = softplus_and_slope(lb[rows, :] + rf[c : c + 1, tile])
                    p = z[h, rows, tile] * slope
                    cacc[rows, tile] += p
                    total += p
                    parts.append(act)
                acts.append(jnp.concatenate(parts, axis=1))
                totals.append(total)
            rows = slice(16 * pair, 16 * pair + 16)
            a2[1, rows, lanes(h)] = jnp.concatenate(acts, axis=0).astype(BF16)
            high, low = halves(jnp.concatenate(totals, axis=0))
            rhi[rows, at] = high
            rlo[rows, at] = low
        k, n = iota((128, 512), 0), iota((128, 512), 1)
        source = jnp.where(n < 4, n + 4, jnp.where(n >= 508, n - 508, -1024)) + 8 * h
        pick = jnp.concatenate([shift[...], one_hot(k == source)], axis=0)
        moved = dot(jnp.concatenate([a2[1, :, lanes(h)], act_edge[...]], axis=1), pick).astype(BF16)
        a2[0, :, lanes(h)] = moved[:, 0:256]
        a2[2, :, lanes(h)] = moved[:, 256:512]

    loop(9, body)


def sums(cacc, p_edge, rhi, rlo, cols, col_ends, row_main, row_ends):
    by_channel = one_hot((iota((32, 256), 1) >> 3) == iota((32, 256), 0))
    lane = iota((16, 128), 1)

    def total(x):
        high, low = halves(x)
        return dot(by_channel, high) + dot(by_channel, low)

    def packed(first, second):
        return jnp.where(lane < 64, first, second)

    x = total(cacc[...])
    for q in range(4):
        tile = x[:, 128 * (q // 2) : 128 * (q // 2) + 128]
        turned = pltpu.roll(tile, 64, 1)
        cols[q] = packed(turned[0:16], tile[16:32]) if q % 2 else packed(tile[0:16], turned[16:32])
    high, low = halves(total(p_edge[...]))
    fold = one_hot((iota((128, 128), 0) & 7) == (iota((128, 128), 1) & 7))
    x = dot(high, fold) + dot(low, fold)
    x = packed(x[0:16], x[16:32])
    col_ends[0] = jnp.where((lane & 63) >= 60, x, 0.0)
    col_ends[1] = jnp.where((lane & 63) < 4, x, 0.0)
    by_group = one_hot((iota((1152, 128), 0) >> 7) == (iota((1152, 128), 1) >> 3))
    x = dot(rhi[...], by_group) + dot(rlo[...], by_group)
    x = total(jnp.where((iota((256, 128), 0) & 7) == (iota((256, 128), 1) & 7), x, 0.0))
    row_main[...] = packed(pltpu.roll(x[0:16], 124, 1), pltpu.roll(x[16:32], 60, 1))
    x = packed(pltpu.roll(x[0:16], 60, 1), pltpu.roll(x[16:32], 124, 1))
    row_ends[0] = jnp.where((lane & 63) >= 60, x, 0.0)
    row_ends[1] = jnp.where((lane & 63) < 4, x, 0.0)


def convolve(r, c, k, a2, tf, out_ref):
    parts = []
    for g in (2 * k, 2 * k + 1):
        stack = [a2[b, :, lanes(g + u)] for u in range(2) for b in range(3)]
        y = dot(tf[...], jnp.concatenate(stack, axis=0))
        parts.append(y.reshape(32, 8, 256))
    y = jnp.concatenate(parts, axis=1)
    row = r * 64 + 16 * k + iota((16, 256), 0)
    col = c * 256 + iota((16, 256), 1)
    y = jnp.where((col >= row)[None], y, 0.0).astype(BF16)
    out_ref[:, pl.ds(pl.multiple_of(16 * k, 16), 16), :] = y


def tap_gradient(m3, a2, taps):
    s0, s1 = iota((256, 256), 0) & 7, iota((256, 256), 1) & 7
    same, above, below = s1 == s0, s1 == s0 + 4, s1 == s0 - 4
    by_channel = one_hot(((iota((32, 512), 1) & 255) >> 3) == iota((32, 512), 0))
    rows = [None] * 9
    for b in range(3):
        g0 = dot_nt(m3[1, :, 256:2304], a2[b, :, 0:2048])
        g1 = dot_nt(m3[1, :, 256:2304], a2[b, :, 256:2304])
        ys = (
            jnp.where(same, g0, 0.0),
            jnp.where(above, g0, jnp.where(below, g1, 0.0)),
            jnp.where(same, g1, 0.0),
        )
        for a in range(3):
            rows[3 * a + b] = dot(by_channel, jnp.concatenate(halves(ys[a]), axis=0))
    for q in range(3):
        group = rows[4 * q : 4 * q + 4]
        pick = jnp.concatenate(
            [one_hot((iota((256, 128), 0) >> 3) + 32 * k == iota((256, 128), 1)) for k in range(len(group))], axis=0
        )
        high, low = halves(jnp.concatenate(group, axis=1))
        taps[32 * q : 32 * q + 32, :] = dot(high, pick) + dot(low, pick)


LOCAL_SCRATCH = [
    pltpu.VMEM((72, 128), F32),
    pltpu.VMEM((32, 256), F32),
    pltpu.VMEM((96, 128), F32),
    pltpu.VMEM((3, 256, 2560), BF16),
    pltpu.VMEM((3, 256, 2304), BF16),
    pltpu.VMEM((9, 256, 256), F32),
    pltpu.VMEM((256, 128), F32),
    pltpu.VMEM((256, 128), BF16),
    pltpu.VMEM((256, 128), F32),
    pltpu.VMEM((256, 1536), BF16),
    pltpu.VMEM((256, 1536), BF16),
    pltpu.VMEM((256, 256), F32),
    pltpu.VMEM((256, 512), BF16),
    pltpu.VMEM((256, 128), BF16),
    pltpu.VMEM((256, 128), F32),
    pltpu.VMEM((256, 1152), BF16),
    pltpu.VMEM((256, 1152), BF16),
    pltpu.VMEM((4, 16, 128), F32),
    pltpu.VMEM((2, 16, 128), F32),
    pltpu.VMEM((16, 128), F32),
    pltpu.VMEM((2, 16, 128), F32),
]


class Place:
    def __init__(self, nr, nc):
        r, c = lax.axis_index("row"), lax.axis_index("col")
        self.r, self.c, self.nr, self.nc = r, c, nr, nc
        self.per = nr // nc
        self.rb, self.rm = r // self.per, r % self.per
        self.k1 = r % 2 + 2 * (r // 2 % 2) + 4 * (r // 8 % 2) + 8 * (c // 2 % 2)
        self.k2 = r // 4 % 2 + 2 * (r // 16) + 4 * (c % 2) + 8 * (c // 4)
        self.has_up, self.has_down = r > 0, r < nr - 1
        self.has_left, self.has_right = c > 0, c < nc - 1
        self.ends_block = (self.rm == self.per - 1) & (self.rb < nc - 1)
        self.starts_block = (self.rm == 0) & (self.rb > 0)
        self.in_others = self.rb == c

    def member1(self, k):
        row = self.r // 16 * 16 + self.r // 4 % 2 * 4 + k % 2 + 2 * (k // 2 % 2) + 8 * (k // 4 % 2)
        return row, self.c // 4 * 4 + self.c % 2 + 2 * (k // 8)

    def member2(self, k):
        row = self.r // 8 % 2 * 8 + self.r % 4 + 4 * (k % 2) + 16 * (k // 2 % 2)
        return row, self.c // 2 % 2 * 2 + k // 4 % 2 + 4 * (k // 8)

    def other(self, k):
        return self.per * self.c + k, self.rb

    def greet(self):
        r, c, nc, per = self.r, self.c, self.nc, self.per
        barrier = pltpu.get_barrier_semaphore()

        def signal(a, b):
            pl.semaphore_signal(barrier, inc=1, device_id=(a, b), device_id_type=MESH)

        def signal_other(a, b):
            pl.when((a != r) | (b != c))(lambda: signal(a, b))

        def signal_all(col):
            for k in range(per):
                signal(per * c + k, col)

        for k in range(1, nc):
            signal(r, lax.rem(c + k, nc))
        for k in range(per):
            signal_other(*self.other(k))
        for k in range(1, 16):
            signal(*self.member1(lax.rem(self.k1 + k, 16)))
        for k in range(1, 16):
            signal(*self.member2(lax.rem(self.k2 + k, 16)))
        pl.when(self.has_up)(lambda: signal(r - 1, c))
        pl.when(self.has_down)(lambda: signal(r + 1, c))
        pl.when(self.has_left)(lambda: signal(per * c - 1, self.rb))
        pl.when(self.has_right)(lambda: signal(per * c + per, self.rb))
        pl.when(self.ends_block)(lambda: signal_all(self.rb + 1))
        pl.when(self.starts_block)(lambda: signal_all(self.rb - 1))
        n = nc - 1 + per + 30
        for cond, m in (
            (self.in_others, -1), (self.has_up, 1), (self.has_down, 1), (self.has_left, 1),
            (self.has_right, 1), (self.ends_block, per), (self.starts_block, per),
        ):
            n = n + jnp.where(cond, m, 0)
        return n

    def senders(self, send, recv):
        def put(src, dst_r, dst_c, dst, sem):
            pltpu.make_async_remote_copy(
                src, dst, send.at[sem], recv.at[sem], device_id=(dst_r, dst_c), device_id_type=MESH
            ).start()

        def put_other(src, k, dst, sem):
            a, b = self.other(k)
            mine = (a == self.r) & (b == self.c)
            pl.when(mine)(lambda: pltpu.make_async_copy(src, dst, recv.at[sem]).start())
            pl.when(jnp.logical_not(mine))(lambda: put(src, a, b, dst, sem))

        return put, put_other


def pair_kernel(
    nr, nc, e_hbm, lpt_hbm, rpt_hbm, w_hbm, cot_hbm,
    out_ref, sums_ref, eg_ref,
    lf, rf, taps, m3, a2, z, z_edge, act_edge, p_edge, tf, tb, cacc, shift, left_m, lb, rhi, rlo,
    cols, col_ends, row_main, row_ends,
    e_ref, w_ref, cot_ref, proj, es, eb, el, eh, fb, blocks, row_feats, col_feats,
    cparts, cends, rends, turned, gparts, buf, r1, r2, r3, mid, fin, recv, send, loads,
):
    ins = ((e_hbm, e_ref), (w_hbm, w_ref), (lpt_hbm, proj.at[0:32]), (rpt_hbm, proj.at[32:64]), (cot_hbm, cot_ref))
    ins = [pltpu.make_async_copy(src, dst, loads.at[k]) for k, (src, dst) in enumerate(ins)]
    for copy in ins:
        copy.start()
    p = Place(nr, nc)
    r, c, per, rb, rm, k1, k2 = p.r, p.c, p.per, p.rb, p.rm, p.k1, p.k2
    greeted = p.greet()
    put, put_other = p.senders(send, recv)

    proj[64:128, :] = jnp.zeros((64, 512), BF16)
    el[...] = jnp.zeros_like(el)
    eh[...] = jnp.zeros_like(eh)
    build_shift(shift)
    ins[0].wait()
    e = e_ref[...].astype(F32)
    es[...] = jnp.concatenate([e[:, 0:256], e[:, 256:512]], axis=0).astype(BF16)
    ins[1].wait()
    build_taps(w_ref, tf, tb)
    ins[4].wait()
    mask_cotangent(r, c, cot_ref, shift, m3)
    pl.semaphore_wait(pltpu.get_barrier_semaphore(), greeted)

    for k in range(1, nc):
        put(es, r, lax.rem(c + k, nc), eb.at[c], 0)
    pltpu.make_async_copy(es, eb.at[c], recv.at[0]).start()
    input_gradient(m3, tb, z)
    ins[2].wait()
    ins[3].wait()
    wait_bytes(eb, recv.at[0])
    e = eb[...].astype(F32)
    el[0:64, :] = e[:, 0:8].reshape(64, 256).astype(BF16)
    eh[0:64, :] = e[:, 8:16].reshape(64, 256).astype(BF16)
    feats = dot_nt(el[0:64, :], proj[:, 0:256]) + dot_nt(eh[0:64, :], proj[:, 256:512])
    fb[...] = feats.astype(BF16)

    for k in range(per):
        put_other(fb, k, blocks.at[rm], 1)
    bottom, top = fb.at[48:64], fb.at[0:16]

    def put_all(src, col, dst, sem):
        for k in range(per):
            put(src, per * c + k, col, dst, sem)

    pl.when(p.has_down)(lambda: put(bottom, r + 1, c, row_feats.at[0], 2))
    pl.when(p.has_up)(lambda: put(top, r - 1, c, row_feats.at[1], 3))
    pl.when(p.ends_block)(lambda: put_all(bottom, rb + 1, col_feats.at[0], 4))
    pl.when(p.starts_block)(lambda: put_all(top, rb - 1, col_feats.at[1], 5))
    input_gradient_edge(m3, tb, z_edge)

    def arrive(cond, ref, sem):
        pl.when(cond)(lambda: wait_bytes(ref, sem))
        pl.when(jnp.logical_not(cond))(lambda: ref.__setitem__(..., jnp.full(ref.shape, OUTSIDE, BF16)))

    arrive(p.has_up, row_feats.at[0], recv.at[2])
    arrive(p.has_down, row_feats.at[1], recv.at[3])
    arrive(p.has_left, col_feats.at[0], recv.at[4])
    arrive(p.has_right, col_feats.at[1], recv.at[5])
    wait_bytes(blocks, recv.at[1])
    lf[0:4, :] = row_feats[0].astype(F32)[12:16]
    lf[4:68, :] = fb[...].astype(F32)
    lf[68:72, :] = row_feats[1].astype(F32)[0:4]
    pick_right = one_hot(iota((32, 128), 0) + 32 == iota((32, 128), 1))
    rf[...] = dot_nt(pick_right, blocks[...].reshape(64 * per, 128))
    around = jnp.concatenate([col_feats[1].astype(F32)[0:4], col_feats[0].astype(F32)[12:16]], axis=0)
    edge_part(lf, around, z_edge, act_edge, p_edge, left_m)
    elementwise(rf, z, act_edge, p_edge, left_m, shift, lb, a2, cacc, rhi, rlo)
    sums(cacc, p_edge, rhi, rlo, cols, col_ends, row_main, row_ends)

    for k in range(per):
        put_other(cols.at[k], k, cparts.at[rm], 6)
    pl.when(p.has_up)(lambda: put(row_ends.at[0], r - 1, c, rends.at[0], 7))
    pl.when(p.has_down)(lambda: put(row_ends.at[1], r + 1, c, rends.at[1], 8))
    pl.when(p.has_left)(lambda: put(col_ends.at[0], per * c - 1, rb, cends.at[0, rm], 9))
    pl.when(p.has_right)(lambda: put(col_ends.at[1], per * c + per, rb, cends.at[1, rm], 10))

    tap_gradient(m3, a2, taps)
    for k in range(12):
        buf[k, :, 256:384] = taps[8 * k : 8 * k + 8, :]
    buf[12:16, :, 256:384] = jnp.zeros((4, 8, 128), F32)

    def gather_sum(cond, ref, sem):
        pl.when(cond)(lambda: wait_bytes(ref, sem))
        pl.when(jnp.logical_not(cond))(lambda: ref.__setitem__(..., jnp.zeros(ref.shape, F32)))

    gather_sum(p.has_down, rends.at[0], recv.at[7])
    gather_sum(p.has_up, rends.at[1], recv.at[8])
    gather_sum(p.ends_block, cends.at[0], recv.at[9])
    gather_sum(p.starts_block, cends.at[1], recv.at[10])
    wait_bytes(cparts, recv.at[6])
    grads = (
        row_main[...] + rends[0] + rends[1],
        jnp.sum(cparts[...], axis=0) + jnp.sum(cends[0], axis=0) + jnp.sum(cends[1], axis=0),
    )
    lower = iota((16, 128), 1) < 64
    grads = [jnp.where(lower, y, 0.0) for x in grads for y in (x, pltpu.roll(x, 64, 1))]
    grads = jnp.concatenate(grads, axis=0)

    high, low = halves(grads)
    for half, ref in enumerate((el, eh)):
        part = dot(high, ref[...]) + dot(low, ref[...])
        for k in range(8):
            buf[2 * k + half, :, 0:256] = part[8 * k : 8 * k + 8]

    for k in range(1, 16):
        at = lax.rem(k1 + k, 16)
        put(buf.at[at], *p.member1(at), r1.at[k1], 11)
    pltpu.make_async_copy(buf.at[k1], r1.at[k1], recv.at[11]).start()

    turned[...] = jnp.concatenate([grads, jnp.zeros((64, 128), F32)], axis=0).T
    for k in range(1, nc):
        at = lax.rem(c + k, nc)
        put(turned.at[pl.ds(pl.multiple_of(8 * at, 8), 8)], r, at, gparts.at[c], 14)
    pltpu.make_async_copy(turned.at[pl.ds(pl.multiple_of(8 * c, 8), 8)], gparts.at[c], recv.at[14]).start()

    convolve(r, c, 0, a2, tf, out_ref)
    convolve(r, c, 1, a2, tf, out_ref)
    wait_bytes(r1, recv.at[11])
    mid[...] = jnp.sum(r1[...], axis=0)
    for k in range(1, 16):
        put(mid, *p.member2(lax.rem(k2 + k, 16)), r2.at[k2], 12)
    pltpu.make_async_copy(mid, r2.at[k2], recv.at[12]).start()

    convolve(r, c, 2, a2, tf, out_ref)
    convolve(r, c, 3, a2, tf, out_ref)
    wait_bytes(r2, recv.at[12])
    fin[...] = jnp.sum(r2[...], axis=0)
    for k in range(1, 16):
        put(fin, *p.member1(lax.rem(k1 + k, 16)), r3.at[k1], 13)
    pltpu.make_async_copy(fin, r3.at[k1], recv.at[13]).start()

    wait_bytes(gparts, recv.at[14])
    high, low = halves(jnp.sum(gparts[...], axis=0))
    eg_ref[...] = dot(high, proj[...]) + dot(low, proj[...])

    wait_bytes(eb.at[0 : nc - 1], send.at[0])
    pl.when(p.in_others)(lambda: wait_bytes(blocks.at[0 : per - 1], send.at[1]))
    pl.when(jnp.logical_not(p.in_others))(lambda: wait_bytes(blocks, send.at[1]))
    pl.when(p.has_down)(lambda: wait_bytes(bottom, send.at[2]))
    pl.when(p.has_up)(lambda: wait_bytes(top, send.at[3]))
    pl.when(p.ends_block)(lambda: wait_bytes(fb, send.at[4]))
    pl.when(p.starts_block)(lambda: wait_bytes(fb, send.at[5]))
    pl.when(p.in_others)(lambda: wait_bytes(cparts.at[0 : per - 1], send.at[6]))
    pl.when(jnp.logical_not(p.in_others))(lambda: wait_bytes(cparts, send.at[6]))
    pl.when(p.has_up)(lambda: wait_bytes(row_ends.at[0], send.at[7]))
    pl.when(p.has_down)(lambda: wait_bytes(row_ends.at[1], send.at[8]))
    pl.when(p.has_left)(lambda: wait_bytes(col_ends.at[0], send.at[9]))
    pl.when(p.has_right)(lambda: wait_bytes(col_ends.at[1], send.at[10]))
    wait_bytes(r1.at[0:15], send.at[11])
    wait_bytes(r2.at[0:15], send.at[12])
    wait_bytes(gparts.at[0 : nc - 1], send.at[14])

    wait_bytes(r3, recv.at[13])
    sums_ref[...] = r3[...]
    wait_bytes(r3.at[0:15], send.at[13])


def finish_kernel(scale, sums_in, eg_in, conv_ref, left_ref, right_ref, eg_ref):
    for k in range(9):
        q, at = divmod(k, 4)
        for part in range(4):
            piece = sums_in[4 * q + part, :, 256 + 32 * at : 288 + 32 * at]
            conv_ref[k, 8 * part : 8 * part + 8, :] = piece * scale
    for ref, first in ((left_ref, 0), (right_ref, 8)):
        for half in range(2):
            for part in range(4):
                piece = sums_in[first + 2 * part + half, :, 0:256]
                ref[8 * part : 8 * part + 8, 256 * half : 256 * half + 256] = piece * scale
    eg_ref[...] = eg_in[...]


def shards(nr, nc, embed, left_proj, right_proj, conv_w, cotangent):
    per = nr // nc
    pair_out, totals, embed_grad = pl.pallas_call(
        functools.partial(pair_kernel, nr, nc),
        out_shape=(
            jax.ShapeDtypeStruct((32, 64, 256), BF16),
            jax.ShapeDtypeStruct((16, 8, 384), F32),
            jax.ShapeDtypeStruct((8, 512), F32),
        ),
        in_specs=[HBM] * 5,
        out_specs=(VMEM,) * 3,
        scratch_shapes=LOCAL_SCRATCH
        + [
            pltpu.VMEM((8, 512), BF16),
            pltpu.VMEM((9, 32, 32), BF16),
            pltpu.VMEM((32, 64, 256), BF16),
            pltpu.VMEM((128, 512), BF16),
            pltpu.VMEM((16, 256), BF16),
            pltpu.VMEM((nc, 16, 256), BF16),
            pltpu.VMEM((128, 256), BF16),
            pltpu.VMEM((128, 256), BF16),
            pltpu.VMEM((64, 128), BF16),
            pltpu.VMEM((per, 64, 128), BF16),
            pltpu.VMEM((2, 16, 128), BF16),
            pltpu.VMEM((2, 16, 128), BF16),
            pltpu.VMEM((per, 16, 128), F32),
            pltpu.VMEM((2, per, 16, 128), F32),
            pltpu.VMEM((2, 16, 128), F32),
            pltpu.VMEM((128, 128), F32),
            pltpu.VMEM((nc, 8, 128), F32),
            pltpu.VMEM((16, 8, 384), F32),
            pltpu.VMEM((16, 8, 384), F32),
            pltpu.VMEM((16, 8, 384), F32),
            pltpu.VMEM((16, 8, 384), F32),
            pltpu.VMEM((8, 384), F32),
            pltpu.VMEM((8, 384), F32),
            pltpu.SemaphoreType.DMA((15,)),
            pltpu.SemaphoreType.DMA((15,)),
            pltpu.SemaphoreType.DMA((5,)),
        ],
        compiler_params=pltpu.CompilerParams(
            collective_id=0, has_side_effects=True, vmem_limit_bytes=60 * 1024 * 1024
        ),
        name="pair_kernel",
    )(embed, left_proj.T, right_proj.T, conv_w, cotangent)
    conv_grad, left_t, right_t, embed_grad = pl.pallas_call(
        functools.partial(finish_kernel, 32.0 / (8 * nr * nc)),
        out_shape=(
            jax.ShapeDtypeStruct((9, 32, 32), F32),
            jax.ShapeDtypeStruct((32, 512), F32),
            jax.ShapeDtypeStruct((32, 512), F32),
            jax.ShapeDtypeStruct((8, 512), F32),
        ),
        in_specs=[VMEM] * 2,
        out_specs=(VMEM,) * 4,
        compiler_params=pltpu.CompilerParams(vmem_limit_bytes=60 * 1024 * 1024),
        name="finish",
    )(totals, embed_grad)
    return pair_out, conv_grad, left_t.T, right_t.T, embed_grad


def solution(mesh):
    body = functools.partial(shards, mesh.shape["row"], mesh.shape["col"])
    in_specs = (P(("row", "col"), None), P(), P(), P(), P(None, "row", "col"))
    out_specs = (P(None, "row", "col"), P(), P(), P(), P(("row", "col"), None))
    return jax.shard_map(body, mesh=mesh, in_specs=in_specs, out_specs=out_specs, check_vma=False)
```

time: 1290 us -> 63.7 us (0.05)
  waiting for transfers between devices: 1030 us -> 0 us
  blocking collectives: 130 us -> 0 us
  matrix products: 62.3 us -> 0 us
  Pallas kernels: 0 us -> 60.5 us
  starting transfers between devices: 30.1 us -> 0 us
  between operations: 14.8 us -> 0.64 us
    all_gather x1 -> x0, waiting for transfers between devices: 657 us -> none  [shards(): whole = lax.all_gather(embed, ('row', 'col'), axis=0, tiled=True)]
    psum x1 -> x0, waiting for transfers between devices: 245 us -> none  [shards(): lax.psum((jnp.stack(tap_grads), left_part, right_part), ('row', 'col'))]
    unnamed x4 -> x0, waiting for transfers between devices: 122 us -> none
    psum x1 -> x0, blocking collectives: 83.3 us -> none  [shards(): lax.psum((jnp.stack(tap_grads), left_part, right_part), ('row', 'col'))]
    dot_general x33 -> x0, matrix products: 62.3 us -> none  [the longest x9 23.7 us: shards(): jnp.einsum('oc,oij->cij', conv_w[tap], shifted, preferred_element_type=jn...]
    pallas_call x0 -> x2, Pallas kernels: none -> 60.5 us  [the longest x1 58.9 us: shards(): pl.pallas_call(functools.partial(pair_kernel, nr, nc), out_shape=(jax.Sha...]
    unnamed x1 -> x0, blocking collectives: 46.9 us -> none
    ppermute x8 -> x0, starting transfers between devices: 30 us -> none  [the longest x4 23.4 us: with_halo(): before = lax.ppermute(last, axis, up)]
  transfers between devices with their start and end apart: 11 -> 0, of which waited for: 5 -> 0; matrix products, arithmetic and copies ran while one was open for 5% -> 0% of each run, Pallas kernels for 0% -> 0%
where the time goes in v2:
time: 63.7 us; the launch traced here: 63.5 us
  Pallas kernels  60.5 us (95%)
  local copies, waits for them, and re-layouts  2.3 us (4%)
  between operations  0.64 us (1%)
    pallas_call x1, Pallas kernels, shards(): pl.pallas_call(functools.partial(pair_kernel, nr, nc), out_shape=(jax.Sha...  58.9 us
    unnamed x1, local copies, waits for them, and re-layouts  2.3 us
    pallas_call x1, Pallas kernels, shards(): pl.pallas_call(functools.partial(finish_kernel, 32.0 / (8 * nr * nc)), ou...  1.69 us

profile of v2, /device:TPU:1, one launch (start us, length us, event | category | flops | bytes accessed | tf_op | source)
XLA Modules:
  0.0 63.5 jit_solution(13778240976805267374)
XLA Ops:
  0.6 58.9 %pair_kernel.1 = (bf16[32,64,256]{2,1,0:T(8,128)(2,1)}, f32[16,8,384]{2,1,0:T(8,128)}, f32[8,512]{1,0:T(8,128)}) custom-call(bf16[8,512]{1,0:T(8,128)(2,1)} %e_hbm.1, bf16[32,512]{1,0:T(8,128)(2,1)} %bitcast.4, bf16[32,512]{1,0:T(8,128)(2,1)} %bitcast.5, bf16[9,32,32]{2,1,0:T(8,128)(2,1)} %w_hbm.1, bf16[32,64,256]{2,1,0:T(8,128)(2,1)} %cot_hbm.1), custom_call_target="tpu_custom_call" | custom-call | tf_op jit(solution)/shard_map/pair_kernel/pallas_call | solution.py:530
  59.5 1.7 %finish.1 = (f32[9,32,32]{2,1,0:T(8,128)}, f32[32,512]{1,0:T(8,128)}, f32[32,512]{1,0:T(8,128)}, f32[8,512]{1,0:T(8,128)}) custom-call(f32[16,8,384]{2,1,0:T(8,128)} %get-tuple-element.13.sums_in, f32[8,512]{1,0:T(8,128)} %get-tuple-element.14.eg_in), custom_call_target="tpu_custom_call" | custom-call | tf_op jit(solution)/shard_map/finish/pallas_call | solution.py:573
  61.2 2.3 %copy.11 = bf16[32,64,256]{2,1,0:T(8,128)(2,1)} copy(bf16[32,64,256]{2,1,0:T(8,128)(2,1)} %get-tuple-element.24) | data formatting | bytes 2097152

commit v3 on v2

v3 whole, which is shorter than its diff:
```python
import functools

import jax
import jax.numpy as jnp
from jax import lax
from jax.experimental import pallas as pl
from jax.experimental.pallas import tpu as pltpu
from jax.sharding import PartitionSpec as P

MESH = pl.DeviceIdType.MESH
OUTSIDE = -1e30
LOG2E = 1.4426950408889634
LN2 = 0.6931471805599453
F32 = jnp.float32
BF16 = jnp.bfloat16
VMEM = pl.BlockSpec(memory_space=pltpu.VMEM)
HBM = pl.BlockSpec(memory_space=pltpu.HBM)


def iota(shape, dim):
    return lax.broadcasted_iota(jnp.int32, shape, dim)


def one_hot(cond):
    return jnp.where(cond, 1.0, 0.0).astype(BF16)


def dot(a, b):
    return jnp.dot(a, b, preferred_element_type=F32)


def dot_nt(a, b):
    return lax.dot_general(a, b, (((1,), (1,)), ((), ())), preferred_element_type=F32)


def dot_tn(a, b):
    return lax.dot_general(a, b, (((0,), (0,)), ((), ())), preferred_element_type=F32)


def halves(x):
    high = x.astype(BF16)
    return high, (x - high.astype(F32)).astype(BF16)


def loop(n, f):
    def body(k, _):
        f(k)
        return 0

    lax.fori_loop(0, n, body, 0)


def lanes(h):
    return pl.ds(pl.multiple_of(h * 256, 256), 256)


def wait_bytes(ref, sem):
    pltpu.make_async_copy(ref, ref, sem).wait()


def softplus_and_slope(y):
    t = jnp.exp2(-jnp.abs(y))
    u = 1.0 + t
    inv = pltpu.reciprocal(u, approx=True, full_range=False)
    inv = inv * (2.0 - u * inv)
    log = jnp.where(t < 1 / 256, t * (LOG2E - (0.5 * LOG2E) * t), jnp.log2(u))
    return LN2 * (jnp.maximum(y, 0.0) + log), jnp.where(y >= 0, inv, t * inv)


def build_taps(w_ref, tf):
    spread = one_hot((iota((256, 32), 0) >> 3) == iota((256, 32), 1))
    widen = one_hot((iota((32, 256), 1) >> 3) == iota((32, 256), 0))
    s0, s1 = iota((256, 256), 0) & 7, iota((256, 256), 1) & 7
    same, above, below = s1 == s0, s1 == s0 + 4, s1 == s0 - 4
    for b in range(3):
        x = [dot(spread, dot(w_ref[3 * a + b], widen).astype(BF16)) for a in range(3)]
        tf[:, 256 * b : 256 * b + 256] = jnp.where(same, x[0], jnp.where(above, x[1], 0.0)).astype(BF16)
        tf[:, 768 + 256 * b : 1024 + 256 * b] = jnp.where(same, x[2], jnp.where(below, x[1], 0.0)).astype(BF16)


def mask_cotangent(r, c, cot_ref, mall, mt):
    for k in range(4):
        x = cot_ref[:, 16 * k : 16 * k + 16, :].astype(F32)
        row = r * 64 + 16 * k + iota((16, 256), 0)
        x = jnp.where((c * 256 + iota((16, 256), 1) >= row)[None], x, 0.0)
        for half in range(2):
            mall[:, lanes(2 * k + half)] = x[:, 8 * half : 8 * half + 8].reshape(256, 256).astype(BF16)
    for b in range(3):
        mt[0, :, 256 * b : 256 * b + 256] = jnp.zeros((272, 256), BF16)
        mt[9, :, 256 * b : 256 * b + 256] = jnp.zeros((272, 256), BF16)

    def body(g):
        for b in range(3):
            move = one_hot(iota((272, 256), 0) - 4 * b == iota((272, 256), 1))
            mt[g + 1, :, 256 * b : 256 * b + 256] = dot_nt(move, mall[:, lanes(g)]).astype(BF16)

    loop(8, body)


def input_gradient(mt, tf, z):
    def body(h):
        z[h] = dot_nt_blocks(mt, tf, h)

    loop(9, body)


def dot_nt_blocks(mt, tf, h):
    left = jnp.concatenate([mt[h], mt[h + 1]], axis=1)
    right = jnp.concatenate(
        [tf[:, 768 * (1 - u) + 256 * b : 768 * (1 - u) + 256 * b + 256] for u in range(2) for b in range(3)], axis=0
    )
    return dot(left, right)


def features(rows, cols, rowf, colf):
    k, n = iota((128, 256), 0), iota((128, 256), 1) >> 3
    colf[...] = dot(cols, one_hot(k == n + 32)) * LOG2E
    x = dot(rows, one_hot(k == n))
    x = jnp.where((iota((128, 256), 0) & 7) == (iota((128, 256), 1) & 7), x, 0.0).astype(BF16)
    rowf[...] = dot(one_hot((iota((16, 128), 1) >> 3) == iota((16, 128), 0)), x) * LOG2E


def elementwise(rowf, colf, z, act, cacc, rsum):
    rsum[...] = jnp.zeros_like(rsum)

    def body(step):
        for part in range(3):
            rows = pl.ds(pl.multiple_of(24 * step + 8 * part, 8), 8)
            right = colf[rows, :]
            total = jnp.zeros((8, 256), F32)
            for h in range(9):
                value, slope = softplus_and_slope(right + rowf[h : h + 1, :])
                act[h, rows, :] = value
                p = z[h, rows, :] * slope
                total += p
                rsum[8 * h : 8 * h + 8, :] += p
            cacc[rows, :] = total

    loop(11, body)


def sums(cacc, rsum, cols, col_ends, row_main, row_ends):
    k, n = iota((256, 128), 0) >> 3, iota((256, 128), 1)
    picks = [one_hot(k + 32 * g == n) for g in range(4)]
    pick = jnp.concatenate(picks, axis=0)
    x = [
        jnp.concatenate([cacc[4 + 64 * q + 16 * g : 20 + 64 * q + 16 * g, :] for g in range(4)], axis=1) for q in range(4)
    ]
    high, low = halves(jnp.concatenate(x, axis=0))
    x = dot(high, pick) + dot(low, pick)
    for q in range(4):
        cols[q] = x[16 * q : 16 * q + 16]
    sub, lane = iota((16, 128), 0), iota((16, 128), 1)
    ends = jnp.concatenate([cacc[0:8, :], cacc[256:264, :]], axis=0)
    high, low = halves(ends)
    first = dot(high, picks[3]) + dot(low, picks[3])
    second = dot(high, picks[0]) + dot(low, picks[0])
    col_ends[0] = jnp.where(sub >= 12, pltpu.roll(first, 12, 0), 0.0)
    col_ends[1] = jnp.where(sub < 4, pltpu.roll(second, 4, 0), 0.0)
    x = jnp.concatenate([rsum[...], jnp.zeros((56, 256), F32)], axis=0)
    by_group = one_hot((iota((80, 128), 0) >> 3) == (iota((80, 128), 1) >> 3))
    high, low = halves(x)
    x = dot(by_group, high) + dot(by_group, low)
    x = jnp.where((iota((80, 256), 0) & 7) == (iota((80, 256), 1) & 7), x, 0.0)
    high, low = halves(jnp.concatenate([x[4 + 16 * g : 20 + 16 * g] for g in range(4)], axis=1))
    row_main[...] = dot(high, pick) + dot(low, pick)
    ends = jnp.concatenate([x[0:8], x[64:72]], axis=0)
    high, low = halves(ends)
    first = dot(high, picks[3]) + dot(low, picks[3])
    second = dot(high, picks[0]) + dot(low, picks[0])
    row_ends[0] = jnp.where(sub >= 12, pltpu.roll(first, 12, 0), 0.0)
    row_ends[1] = jnp.where(sub < 4, pltpu.roll(second, 4, 0), 0.0)


def build_windows(act, a3):
    def body(h):
        at = pl.ds(pl.multiple_of(256 * h, 256), 256)
        for b in range(3):
            a3[at, 256 * b : 256 * b + 256] = act[h, 4 * b : 4 * b + 256, :].astype(BF16)

    loop(9, body)


def convolve(r, c, k, a3, tf, out_ref):
    parts = []
    for g in (2 * k, 2 * k + 1):
        both = jnp.concatenate([a3[256 * (g + u) : 256 * (g + u) + 256, :] for u in range(2)], axis=1)
        parts.append(dot_nt(tf[...], both).reshape(32, 8, 256))
    y = jnp.concatenate(parts, axis=1)
    row = r * 64 + 16 * k + iota((16, 256), 0)
    col = c * 256 + iota((16, 256), 1)
    out_ref[:, 16 * k : 16 * k + 16, :] = jnp.where((col >= row)[None], y, 0.0).astype(BF16)


def tap_gradient(mall, a3, taps):
    s0, s1 = iota((256, 256), 0) & 7, iota((256, 256), 1) & 7
    same, above, below = s1 == s0, s1 == s0 + 4, s1 == s0 - 4
    by_channel = one_hot(((iota((32, 512), 1) & 255) >> 3) == iota((32, 512), 0))
    rows = [None] * 9
    for b in range(3):
        g0 = dot(mall[...], a3[0:2048, 256 * b : 256 * b + 256])
        g1 = dot(mall[...], a3[256:2304, 256 * b : 256 * b + 256])
        ys = (
            jnp.where(same, g0, 0.0),
            jnp.where(above, g0, jnp.where(below, g1, 0.0)),
            jnp.where(same, g1, 0.0),
        )
        for a in range(3):
            rows[3 * a + b] = dot(by_channel, jnp.concatenate(halves(ys[a]), axis=0))
    for q in range(3):
        group = rows[4 * q : 4 * q + 4]
        pick = jnp.concatenate(
            [one_hot((iota((256, 128), 0) >> 3) + 32 * k == iota((256, 128), 1)) for k in range(len(group))], axis=0
        )
        high, low = halves(jnp.concatenate(group, axis=1))
        taps[32 * q : 32 * q + 32, :] = dot(high, pick) + dot(low, pick)


LOCAL_SCRATCH = [
    pltpu.VMEM((16, 256), F32),
    pltpu.VMEM((272, 256), F32),
    pltpu.VMEM((96, 128), F32),
    pltpu.VMEM((256, 2048), BF16),
    pltpu.VMEM((10, 272, 768), BF16),
    pltpu.VMEM((9, 272, 256), F32),
    pltpu.VMEM((2304, 768), BF16),
    pltpu.VMEM((9, 272, 256), F32),
    pltpu.VMEM((256, 1536), BF16),
    pltpu.VMEM((272, 256), F32),
    pltpu.VMEM((72, 256), F32),
    pltpu.VMEM((4, 16, 128), F32),
    pltpu.VMEM((2, 16, 128), F32),
    pltpu.VMEM((16, 128), F32),
    pltpu.VMEM((2, 16, 128), F32),
]


class Place:
    def __init__(self, nr, nc):
        r, c = lax.axis_index("row"), lax.axis_index("col")
        self.r, self.c, self.nr, self.nc = r, c, nr, nc
        self.per = nr // nc
        self.rb, self.rm = lax.div(r, self.per), lax.rem(r, self.per)
        bits1 = ((r, 1, 0), (r, 2, 0), (r, 8, 0), (c, 2, 1))
        bits2 = ((r, 4, 0), (r, 16, 0), (c, 1, 1), (c, 4, 1))
        self.k1, self.group1 = self.group(bits1)
        self.k2, self.group2 = self.group(bits2)
        _, self.group0 = self.group(((c, 1, 1), (c, 2, 1), (c, 4, 1)))
        self.has_up, self.has_down = r > 0, r < nr - 1
        self.has_left, self.has_right = c > 0, c < nc - 1
        self.ends_block = (self.rm == self.per - 1) & (self.rb < nc - 1)
        self.starts_block = (self.rm == 0) & (self.rb > 0)
        self.in_others = self.rb == c

    def group(self, bits):
        number, turns = 0, []
        for k, (x, weight, is_col) in enumerate(bits):
            bit = lax.rem(lax.div(x, weight), 2)
            number = number + bit * (1 << k)
            sign = 1 - 2 * bit
            turns.append((sign * weight, is_col, sign * (1 << k)))
        members = [(self.r, self.c, number)]
        for move, is_col, step in turns:
            members += [
                (a, b + move, n + step) if is_col else (a + move, b, n + step) for a, b, n in members
            ]
        return number, members[:0:-1]

    def other(self, k):
        return self.per * self.c + k, self.rb

    def greet(self):
        r, c, nc, per = self.r, self.c, self.nc, self.per
        barrier = pltpu.get_barrier_semaphore()

        def signal(a, b):
            pl.semaphore_signal(barrier, inc=1, device_id=(a, b), device_id_type=MESH)

        def signal_other(a, b):
            pl.when((a != r) | (b != c))(lambda: signal(a, b))

        def signal_all(col):
            for k in range(per):
                signal(per * c + k, col)

        for a, b, _ in self.group0 + self.group1 + self.group2:
            signal(a, b)
        for k in range(per):
            signal_other(*self.other(k))
        pl.when(self.has_up)(lambda: signal(r - 1, c))
        pl.when(self.has_down)(lambda: signal(r + 1, c))
        pl.when(self.has_left)(lambda: signal(per * c - 1, self.rb))
        pl.when(self.has_right)(lambda: signal(per * c + per, self.rb))
        pl.when(self.ends_block)(lambda: signal_all(self.rb + 1))
        pl.when(self.starts_block)(lambda: signal_all(self.rb - 1))
        n = nc - 1 + per + 30
        for cond, m in (
            (self.in_others, -1), (self.has_up, 1), (self.has_down, 1), (self.has_left, 1),
            (self.has_right, 1), (self.ends_block, per), (self.starts_block, per),
        ):
            n = n + jnp.where(cond, m, 0)
        return n

    def senders(self, send, recv):
        def put(src, dst_r, dst_c, dst, sem):
            pltpu.make_async_remote_copy(
                src, dst, send.at[sem], recv.at[sem], device_id=(dst_r, dst_c), device_id_type=MESH
            ).start()

        def put_other(src, k, dst, sem):
            a, b = self.other(k)
            mine = (a == self.r) & (b == self.c)
            pl.when(mine)(lambda: pltpu.make_async_copy(src, dst, recv.at[sem]).start())
            pl.when(jnp.logical_not(mine))(lambda: put(src, a, b, dst, sem))

        return put, put_other


def pair_kernel(
    nr, nc, e_hbm, lpt_hbm, rpt_hbm, w_hbm, cot_hbm,
    out_hbm, sums_ref, eg_ref,
    rowf, colf, taps, mall, mt, act, a3, z, tf, cacc, rsum, cols, col_ends, row_main, row_ends,
    out_ref, feats, e_ref, w_ref, cot_ref, proj, es, eb, el, eh, fb, blocks, row_feats, col_feats,
    cparts, cends, rends, turned, gparts, buf, r1, r2, r3, mid, fin, recv, send, loads, stores,
):
    ins = ((e_hbm, e_ref), (w_hbm, w_ref), (lpt_hbm, proj.at[0:32]), (rpt_hbm, proj.at[32:64]), (cot_hbm, cot_ref))
    ins = [pltpu.make_async_copy(src, dst, loads.at[k]) for k, (src, dst) in enumerate(ins)]
    for copy in ins:
        copy.start()
    p = Place(nr, nc)
    r, c, per, rb, rm, k1, k2 = p.r, p.c, p.per, p.rb, p.rm, p.k1, p.k2
    greeted = p.greet()
    put, put_other = p.senders(send, recv)

    ins[0].wait()
    e = e_ref[...].astype(F32)
    es[...] = jnp.concatenate([e[:, 0:256], e[:, 256:512]], axis=0).astype(BF16)
    pl.semaphore_wait(pltpu.get_barrier_semaphore(), greeted)

    for a, b, _ in p.group0:
        put(es, a, b, eb.at[c], 0)
    pltpu.make_async_copy(es, eb.at[c], recv.at[0]).start()
    proj[64:128, :] = jnp.zeros((64, 512), BF16)
    ins[1].wait()
    build_taps(w_ref, tf)
    ins[4].wait()
    mask_cotangent(r, c, cot_ref, mall, mt)
    ins[2].wait()
    ins[3].wait()
    wait_bytes(eb, recv.at[0])
    e = eb[...].astype(F32)
    el[...] = e[:, 0:8].reshape(64, 256).astype(BF16)
    eh[...] = e[:, 8:16].reshape(64, 256).astype(BF16)
    fb[...] = (dot_nt(el[...], proj[:, 0:256]) + dot_nt(eh[...], proj[:, 256:512])).astype(BF16)

    for k in range(per):
        put_other(fb, k, blocks.at[rm], 1)
    bottom, top = fb.at[48:64], fb.at[0:16]

    def put_all(src, col, dst, sem):
        for k in range(per):
            put(src, per * c + k, col, dst, sem)

    pl.when(p.has_down)(lambda: put(bottom, r + 1, c, row_feats.at[0], 2))
    pl.when(p.has_up)(lambda: put(top, r - 1, c, row_feats.at[1], 3))
    pl.when(p.ends_block)(lambda: put_all(bottom, rb + 1, col_feats.at[0], 4))
    pl.when(p.starts_block)(lambda: put_all(top, rb - 1, col_feats.at[1], 5))
    input_gradient(mt, tf, z)

    def arrive(cond, ref, sem):
        pl.when(cond)(lambda: wait_bytes(ref, sem))
        pl.when(jnp.logical_not(cond))(lambda: ref.__setitem__(..., jnp.full(ref.shape, OUTSIDE, BF16)))

    arrive(p.has_up, row_feats.at[0], recv.at[2])
    arrive(p.has_down, row_feats.at[1], recv.at[3])
    arrive(p.has_left, col_feats.at[0], recv.at[4])
    arrive(p.has_right, col_feats.at[1], recv.at[5])
    wait_bytes(blocks, recv.at[1])
    feats[0:4, :] = row_feats[0].astype(F32)[12:16]
    feats[4:68, :] = fb[...].astype(F32)
    feats[68:72, :] = row_feats[1].astype(F32)[0:4]
    feats[72:128, :] = jnp.zeros((56, 128), F32)
    rows = feats[0:128, :].astype(BF16)
    feats[128:132, :] = col_feats[0].astype(F32)[12:16]
    feats[132 : 132 + 64 * per, :] = blocks[...].reshape(64 * per, 128).astype(F32)
    feats[388:392, :] = col_feats[1].astype(F32)[0:4]
    feats[392:400, :] = jnp.zeros((8, 128), F32)
    features(rows, feats[128:400, :].astype(BF16), rowf, colf)
    elementwise(rowf, colf, z, act, cacc, rsum)
    sums(cacc, rsum, cols, col_ends, row_main, row_ends)

    for k in range(per):
        put_other(cols.at[k], k, cparts.at[rm], 6)
    pl.when(p.has_up)(lambda: put(row_ends.at[0], r - 1, c, rends.at[0], 7))
    pl.when(p.has_down)(lambda: put(row_ends.at[1], r + 1, c, rends.at[1], 8))
    pl.when(p.has_left)(lambda: put(col_ends.at[0], per * c - 1, rb, cends.at[0, rm], 9))
    pl.when(p.has_right)(lambda: put(col_ends.at[1], per * c + per, rb, cends.at[1, rm], 10))

    build_windows(act, a3)
    tap_gradient(mall, a3, taps)
    for k in range(12):
        buf[k, :, 256:384] = taps[8 * k : 8 * k + 8, :]
    buf[12:16, :, 256:384] = jnp.zeros((4, 8, 128), F32)

    def gather_sum(cond, ref, sem):
        pl.when(cond)(lambda: wait_bytes(ref, sem))
        pl.when(jnp.logical_not(cond))(lambda: ref.__setitem__(..., jnp.zeros(ref.shape, F32)))

    gather_sum(p.has_down, rends.at[0], recv.at[7])
    gather_sum(p.has_up, rends.at[1], recv.at[8])
    gather_sum(p.ends_block, cends.at[0], recv.at[9])
    gather_sum(p.starts_block, cends.at[1], recv.at[10])
    wait_bytes(cparts, recv.at[6])
    grads = (
        row_main[...] + rends[0] + rends[1],
        jnp.sum(cparts[...], axis=0) + jnp.sum(cends[0], axis=0) + jnp.sum(cends[1], axis=0),
    )
    lane = iota((16, 128), 1)
    spread = []
    for g in range(4):
        parts = [x if turn % 128 == 0 else pltpu.roll(x, turn % 128, 1) for x, turn in zip(grads, (-32 * g, 32 - 32 * g))]
        spread.append(jnp.where(lane < 32, parts[0], jnp.where(lane < 64, parts[1], 0.0)))
    turned[...] = jnp.concatenate(spread, axis=0)

    high, low = halves(turned[...])
    for half, ref in enumerate((el, eh)):
        part = dot_tn(high, ref[...]) + dot_tn(low, ref[...])
        for k in range(8):
            buf[2 * k + half, :, 0:256] = part[8 * k : 8 * k + 8]

    for a, b, at in p.group1:
        put(buf.at[at], a, b, r1.at[k1], 11)
    pltpu.make_async_copy(buf.at[k1], r1.at[k1], recv.at[11]).start()

    for a, b, _ in p.group0:
        put(turned.at[pl.ds(pl.multiple_of(8 * b, 8), 8)], a, b, gparts.at[c], 14)
    pltpu.make_async_copy(turned.at[pl.ds(pl.multiple_of(8 * c, 8), 8)], gparts.at[c], recv.at[14]).start()

    outs = [
        pltpu.make_async_copy(out_ref.at[:, 16 * q : 16 * q + 16, :], out_hbm.at[:, 16 * q : 16 * q + 16, :], stores.at[q])
        for q in range(4)
    ]
    convolve(r, c, 0, a3, tf, out_ref)
    outs[0].start()
    convolve(r, c, 1, a3, tf, out_ref)
    outs[1].start()
    wait_bytes(r1, recv.at[11])
    mid[...] = jnp.sum(r1[...], axis=0)
    for a, b, _ in p.group2:
        put(mid, a, b, r2.at[k2], 12)
    pltpu.make_async_copy(mid, r2.at[k2], recv.at[12]).start()

    convolve(r, c, 2, a3, tf, out_ref)
    outs[2].start()
    convolve(r, c, 3, a3, tf, out_ref)
    outs[3].start()
    wait_bytes(r2, recv.at[12])
    fin[...] = jnp.sum(r2[...], axis=0)
    for a, b, _ in p.group1:
        put(fin, a, b, r3.at[k1], 13)
    pltpu.make_async_copy(fin, r3.at[k1], recv.at[13]).start()

    wait_bytes(gparts, recv.at[14])
    high, low = halves(jnp.sum(gparts[...], axis=0))
    eg_ref[...] = dot(high, proj[...]) + dot(low, proj[...])

    for copy in outs:
        copy.wait()
    wait_bytes(eb.at[0 : nc - 1], send.at[0])
    pl.when(p.in_others)(lambda: wait_bytes(blocks.at[0 : per - 1], send.at[1]))
    pl.when(jnp.logical_not(p.in_others))(lambda: wait_bytes(blocks, send.at[1]))
    pl.when(p.has_down)(lambda: wait_bytes(bottom, send.at[2]))
    pl.when(p.has_up)(lambda: wait_bytes(top, send.at[3]))
    pl.when(p.ends_block)(lambda: wait_bytes(fb, send.at[4]))
    pl.when(p.starts_block)(lambda: wait_bytes(fb, send.at[5]))
    pl.when(p.in_others)(lambda: wait_bytes(cparts.at[0 : per - 1], send.at[6]))
    pl.when(jnp.logical_not(p.in_others))(lambda: wait_bytes(cparts, send.at[6]))
    pl.when(p.has_up)(lambda: wait_bytes(row_ends.at[0], send.at[7]))
    pl.when(p.has_down)(lambda: wait_bytes(row_ends.at[1], send.at[8]))
    pl.when(p.has_left)(lambda: wait_bytes(col_ends.at[0], send.at[9]))
    pl.when(p.has_right)(lambda: wait_bytes(col_ends.at[1], send.at[10]))
    wait_bytes(r1.at[0:15], send.at[11])
    wait_bytes(r2.at[0:15], send.at[12])
    wait_bytes(gparts.at[0 : nc - 1], send.at[14])

    wait_bytes(r3, recv.at[13])
    sums_ref[...] = r3[...]
    wait_bytes(r3.at[0:15], send.at[13])


def finish_kernel(
    scale, sums_in, eg_in, pair_in, conv_ref, left_ref, right_ref, eg_ref, pair_ref, held, loads, stores
):
    def piece(k):
        return slice(8 * k, 8 * k + 8)

    ins = [pltpu.make_async_copy(pair_in.at[piece(k)], held.at[piece(k)], loads.at[k]) for k in range(4)]
    outs = [pltpu.make_async_copy(held.at[piece(k)], pair_ref.at[piece(k)], stores.at[k]) for k in range(4)]
    for copy in ins:
        copy.start()
    for k in range(9):
        q, at = divmod(k, 4)
        for part in range(4):
            x = sums_in[4 * q + part, :, 256 + 32 * at : 288 + 32 * at]
            conv_ref[k, 8 * part : 8 * part + 8, :] = x * scale
    for ref, first in ((left_ref, 0), (right_ref, 8)):
        for half in range(2):
            for part in range(4):
                x = sums_in[first + 2 * part + half, :, 0:256]
                ref[8 * part : 8 * part + 8, 256 * half : 256 * half + 256] = x * scale
    eg_ref[...] = eg_in[...]
    for k in range(4):
        ins[k].wait()
        outs[k].start()
    for copy in outs:
        copy.wait()


def shards(nr, nc, embed, left_proj, right_proj, conv_w, cotangent):
    per = nr // nc
    pair_out, totals, embed_grad = pl.pallas_call(
        functools.partial(pair_kernel, nr, nc),
        out_shape=(
            jax.ShapeDtypeStruct((32, 64, 256), BF16),
            jax.ShapeDtypeStruct((16, 8, 384), F32),
            jax.ShapeDtypeStruct((8, 512), F32),
        ),
        in_specs=[HBM] * 5,
        out_specs=(HBM, VMEM, VMEM),
        scratch_shapes=LOCAL_SCRATCH
        + [
            pltpu.VMEM((32, 64, 256), BF16),
            pltpu.VMEM((400, 128), F32),
            pltpu.VMEM((8, 512), BF16),
            pltpu.VMEM((9, 32, 32), BF16),
            pltpu.VMEM((32, 64, 256), BF16),
            pltpu.VMEM((128, 512), BF16),
            pltpu.VMEM((16, 256), BF16),
            pltpu.VMEM((nc, 16, 256), BF16),
            pltpu.VMEM((64, 256), BF16),
            pltpu.VMEM((64, 256), BF16),
            pltpu.VMEM((64, 128), BF16),
            pltpu.VMEM((per, 64, 128), BF16),
            pltpu.VMEM((2, 16, 128), BF16),
            pltpu.VMEM((2, 16, 128), BF16),
            pltpu.VMEM((per, 16, 128), F32),
            pltpu.VMEM((2, per, 16, 128), F32),
            pltpu.VMEM((2, 16, 128), F32),
            pltpu.VMEM((64, 128), F32),
            pltpu.VMEM((nc, 8, 128), F32),
            pltpu.VMEM((16, 8, 384), F32),
            pltpu.VMEM((16, 8, 384), F32),
            pltpu.VMEM((16, 8, 384), F32),
            pltpu.VMEM((16, 8, 384), F32),
            pltpu.VMEM((8, 384), F32),
            pltpu.VMEM((8, 384), F32),
            pltpu.SemaphoreType.DMA((15,)),
            pltpu.SemaphoreType.DMA((15,)),
            pltpu.SemaphoreType.DMA((5,)),
            pltpu.SemaphoreType.DMA((4,)),
        ],
        compiler_params=pltpu.CompilerParams(
            collective_id=0, has_side_effects=True, vmem_limit_bytes=60 * 1024 * 1024
        ),
        name="pair_kernel",
    )(embed, left_proj.T, right_proj.T, conv_w, cotangent)
    conv_grad, left_t, right_t, embed_grad, pair_out = pl.pallas_call(
        functools.partial(finish_kernel, 32.0 / (8 * nr * nc)),
        out_shape=(
            jax.ShapeDtypeStruct((9, 32, 32), F32),
            jax.ShapeDtypeStruct((32, 512), F32),
            jax.ShapeDtypeStruct((32, 512), F32),
            jax.ShapeDtypeStruct((8, 512), F32),
            jax.ShapeDtypeStruct((32, 64, 256), BF16),
        ),
        in_specs=[VMEM, VMEM, HBM],
        out_specs=(VMEM,) * 4 + (HBM,),
        scratch_shapes=[
            pltpu.VMEM((32, 64, 256), BF16),
            pltpu.SemaphoreType.DMA((4,)),
            pltpu.SemaphoreType.DMA((4,)),
        ],
        compiler_params=pltpu.CompilerParams(vmem_limit_bytes=60 * 1024 * 1024),
        name="finish",
    )(totals, embed_grad, pair_out)
    return pair_out, conv_grad, left_t.T, right_t.T, embed_grad


def solution(mesh):
    body = functools.partial(shards, mesh.shape["row"], mesh.shape["col"])
    in_specs = (P(("row", "col"), None), P(), P(), P(), P(None, "row", "col"))
    out_specs = (P(None, "row", "col"), P(), P(), P(), P(("row", "col"), None))
    return jax.shard_map(body, mesh=mesh, in_specs=in_specs, out_specs=out_specs, check_vma=False)
```

time: 63.7 us -> 59 us (0.926)
  local copies, waits for them, and re-layouts: 2.3 us -> 0 us
  Pallas kernels: 60.5 us -> 58.2 us
    pallas_call x1, Pallas kernels: 58.9 us -> 54.6 us  [shards(): pl.pallas_call(functools.partial(pair_kernel, nr, nc), out_shape=(jax.Sha...]
    unnamed x1 -> x0, local copies, waits for them, and re-layouts: 2.3 us -> none
    pallas_call x1, Pallas kernels: 1.69 us -> 3.62 us  [shards(): pl.pallas_call(functools.partial(finish_kernel, 32.0 / (8 * nr * nc)), ou...]
where the time goes in v3:
time: 59 us; the launch traced here: 58.9 us
  Pallas kernels  58.2 us (99%)
  between operations  0.64 us (1%)
    pallas_call x1, Pallas kernels, shards(): pl.pallas_call(functools.partial(pair_kernel, nr, nc), out_shape=(jax.Sha...  54.6 us
    pallas_call x1, Pallas kernels, shards(): pl.pallas_call(functools.partial(finish_kernel, 32.0 / (8 * nr * nc)), ou...  3.62 us

profile of v3, /device:TPU:1, one launch (start us, length us, event | category | flops | bytes accessed | tf_op | source)
XLA Modules:
  0.0 58.9 jit_solution(952150380240798496)
XLA Ops:
  0.6 54.6 %pair_kernel.1 = (bf16[32,64,256]{2,1,0:T(8,128)(2,1)}, f32[16,8,384]{2,1,0:T(8,128)}, f32[8,512]{1,0:T(8,128)}) custom-call(bf16[8,512]{1,0:T(8,128)(2,1)} %e_hbm.1, bf16[32,512]{1,0:T(8,128)(2,1)} %bitcast.4, bf16[32,512]{1,0:T(8,128)(2,1)} %bitcast.5, bf16[9,32,32]{2,1,0:T(8,128)(2,1)} %w_hbm.1, bf16[32,64,256]{2,1,0:T(8,128)(2,1)} %cot_hbm.1), custom_call_target="tpu_custom_call" | custom-call | tf_op jit(solution)/shard_map/pair_kernel/pallas_call | solution.py:521
  55.3 3.6 %finish.1 = (f32[9,32,32]{2,1,0:T(8,128)}, f32[32,512]{1,0:T(8,128)}, f32[32,512]{1,0:T(8,128)}, f32[8,512]{1,0:T(8,128)}, bf16[32,64,256]{2,1,0:T(8,128)(2,1)}) custom-call(f32[16,8,384]{2,1,0:T(8,128)} %get-tuple-element.13.sums_in, f32[8,512]{1,0:T(8,128)} %get-tuple-element.14.eg_in, bf16[32,64,256]{2,1,0:T(8,128)(2,1)} %get-tuple-element.15.pair_in), custom_call_target="tpu_custom_call" | custom-call | tf_op jit(solution)/shard_map/finish/pallas_call | solution.py:567

commit v4 on v3

--- a/solution.py
+++ b/solution.py
@@ -241,8 +241,8 @@
         self.r, self.c, self.nr, self.nc = r, c, nr, nc
         self.per = nr // nc
         self.rb, self.rm = lax.div(r, self.per), lax.rem(r, self.per)
-        bits1 = ((r, 1, 0), (r, 2, 0), (r, 8, 0), (c, 2, 1))
-        bits2 = ((r, 4, 0), (r, 16, 0), (c, 1, 1), (c, 4, 1))
+        bits1 = ((r, 8, 0), (r, 16, 0), (c, 2, 1), (c, 4, 1))
+        bits2 = ((r, 1, 0), (r, 2, 0), (r, 4, 0), (c, 1, 1))
         self.k1, self.group1 = self.group(bits1)
         self.k2, self.group2 = self.group(bits2)
         _, self.group0 = self.group(((c, 1, 1), (c, 2, 1), (c, 4, 1)))
@@ -318,9 +318,9 @@
 
 def pair_kernel(
     nr, nc, e_hbm, lpt_hbm, rpt_hbm, w_hbm, cot_hbm,
-    out_hbm, sums_ref, eg_ref,
+    out_hbm, sums_hbm, eg_hbm,
     rowf, colf, taps, mall, mt, act, a3, z, tf, cacc, rsum, cols, col_ends, row_main, row_ends,
-    out_ref, feats, e_ref, w_ref, cot_ref, proj, es, eb, el, eh, fb, blocks, row_feats, col_feats,
+    out_ref, eg_ref, feats, e_ref, w_ref, cot_ref, proj, es, eb, el, eh, fb, blocks, row_feats, col_feats,
     cparts, cends, rends, turned, gparts, buf, r1, r2, r3, mid, fin, recv, send, loads, stores,
 ):
     ins = ((e_hbm, e_ref), (w_hbm, w_ref), (lpt_hbm, proj.at[0:32]), (rpt_hbm, proj.at[32:64]), (cot_hbm, cot_ref))
@@ -398,9 +398,9 @@
 
     build_windows(act, a3)
     tap_gradient(mall, a3, taps)
-    for k in range(12):
-        buf[k, :, 256:384] = taps[8 * k : 8 * k + 8, :]
-    buf[12:16, :, 256:384] = jnp.zeros((4, 8, 128), F32)
+    for k in range(16):
+        piece = taps[8 * k : 8 * k + 8, :] if k < 12 else jnp.zeros((8, 128), F32)
+        buf[k, 16:32, :] = jnp.concatenate([piece, jnp.zeros((8, 128), F32)], axis=0).astype(BF16)
 
     def gather_sum(cond, ref, sem):
         pl.when(cond)(lambda: wait_bytes(ref, sem))
@@ -426,7 +426,8 @@
     for half, ref in enumerate((el, eh)):
         part = dot_tn(high, ref[...]) + dot_tn(low, ref[...])
         for k in range(8):
-            buf[2 * k + half, :, 0:256] = part[8 * k : 8 * k + 8]
+            at = slice(16 * (k // 2), 16 * (k // 2) + 16), slice(128 * (k % 2), 128 * (k % 2) + 128)
+            buf[4 * (k // 2) + 2 * half + k % 2, 0:16, :] = part[at].astype(BF16)
 
     for a, b, at in p.group1:
         put(buf.at[at], a, b, r1.at[k1], 11)
@@ -445,7 +446,7 @@
     convolve(r, c, 1, a3, tf, out_ref)
     outs[1].start()
     wait_bytes(r1, recv.at[11])
-    mid[...] = jnp.sum(r1[...], axis=0)
+    mid[...] = jnp.sum(r1[...].astype(F32), axis=0).astype(BF16)
     for a, b, _ in p.group2:
         put(mid, a, b, r2.at[k2], 12)
     pltpu.make_async_copy(mid, r2.at[k2], recv.at[12]).start()
@@ -455,7 +456,7 @@
     convolve(r, c, 3, a3, tf, out_ref)
     outs[3].start()
     wait_bytes(r2, recv.at[12])
-    fin[...] = jnp.sum(r2[...], axis=0)
+    fin[...] = jnp.sum(r2[...].astype(F32), axis=0).astype(BF16)
     for a, b, _ in p.group1:
         put(fin, a, b, r3.at[k1], 13)
     pltpu.make_async_copy(fin, r3.at[k1], recv.at[13]).start()
@@ -463,6 +464,8 @@
     wait_bytes(gparts, recv.at[14])
     high, low = halves(jnp.sum(gparts[...], axis=0))
     eg_ref[...] = dot(high, proj[...]) + dot(low, proj[...])
+    outs.append(pltpu.make_async_copy(eg_ref, eg_hbm, stores.at[4]))
+    outs[4].start()
 
     for copy in outs:
         copy.wait()
@@ -484,34 +487,47 @@
     wait_bytes(gparts.at[0 : nc - 1], send.at[14])
 
     wait_bytes(r3, recv.at[13])
-    sums_ref[...] = r3[...]
+    last = pltpu.make_async_copy(r3, sums_hbm, stores.at[5])
+    last.start()
     wait_bytes(r3.at[0:15], send.at[13])
+    last.wait()
 
 
 def finish_kernel(
-    scale, sums_in, eg_in, pair_in, conv_ref, left_ref, right_ref, eg_ref, pair_ref, held, loads, stores
+    scale, sums_in, eg_in, pair_in, conv_out, left_out, right_out, eg_out, pair_out,
+    sums_ref, eg_ref, held, conv_ref, left_ref, right_ref, loads, stores,
 ):
     def piece(k):
         return slice(8 * k, 8 * k + 8)
 
-    ins = [pltpu.make_async_copy(pair_in.at[piece(k)], held.at[piece(k)], loads.at[k]) for k in range(4)]
-    outs = [pltpu.make_async_copy(held.at[piece(k)], pair_ref.at[piece(k)], stores.at[k]) for k in range(4)]
+    ins = [pltpu.make_async_copy(sums_in, sums_ref, loads.at[0]), pltpu.make_async_copy(eg_in, eg_ref, loads.at[1])]
+    ins += [pltpu.make_async_copy(pair_in.at[piece(k)], held.at[piece(k)], loads.at[2 + k]) for k in range(4)]
+    outs = [
+        pltpu.make_async_copy(conv_ref, conv_out, stores.at[0]),
+        pltpu.make_async_copy(left_ref, left_out, stores.at[1]),
+        pltpu.make_async_copy(right_ref, right_out, stores.at[2]),
+        pltpu.make_async_copy(eg_ref, eg_out, stores.at[3]),
+    ]
+    outs += [pltpu.make_async_copy(held.at[piece(k)], pair_out.at[piece(k)], stores.at[4 + k]) for k in range(4)]
     for copy in ins:
         copy.start()
+    ins[0].wait()
+    for ref, first, at in ((left_ref, 0, 1), (right_ref, 8, 2)):
+        for k in range(8):
+            x = sums_ref[first + k, 0:16, :].astype(F32)
+            ref[16 * (k // 4) : 16 * (k // 4) + 16, 128 * (k % 4) : 128 * (k % 4) + 128] = x * scale
+        outs[at].start()
+    ins[1].wait()
+    outs[3].start()
+    for k in range(4):
+        ins[2 + k].wait()
+        outs[4 + k].start()
     for k in range(9):
         q, at = divmod(k, 4)
         for part in range(4):
-            x = sums_in[4 * q + part, :, 256 + 32 * at : 288 + 32 * at]
-            conv_ref[k, 8 * part : 8 * part + 8, :] = x * scale
-    for ref, first in ((left_ref, 0), (right_ref, 8)):
-        for half in range(2):
-            for part in range(4):
-                x = sums_in[first + 2 * part + half, :, 0:256]
-                ref[8 * part : 8 * part + 8, 256 * half : 256 * half + 256] = x * scale
-    eg_ref[...] = eg_in[...]
-    for k in range(4):
-        ins[k].wait()
-        outs[k].start()
+            x = sums_ref[4 * q + part, 16:32, :].astype(F32)
+            conv_ref[k, 8 * part : 8 * part + 8, :] = x[0:8, 32 * at : 32 * at + 32] * scale
+    outs[0].start()
     for copy in outs:
         copy.wait()
 
@@ -522,14 +538,15 @@
         functools.partial(pair_kernel, nr, nc),
         out_shape=(
             jax.ShapeDtypeStruct((32, 64, 256), BF16),
-            jax.ShapeDtypeStruct((16, 8, 384), F32),
+            jax.ShapeDtypeStruct((16, 32, 128), BF16),
             jax.ShapeDtypeStruct((8, 512), F32),
         ),
         in_specs=[HBM] * 5,
-        out_specs=(HBM, VMEM, VMEM),
+        out_specs=(HBM,) * 3,
         scratch_shapes=LOCAL_SCRATCH
         + [
             pltpu.VMEM((32, 64, 256), BF16),
+            pltpu.VMEM((8, 512), F32),
             pltpu.VMEM((400, 128), F32),
             pltpu.VMEM((8, 512), BF16),
             pltpu.VMEM((9, 32, 32), BF16),
@@ -548,16 +565,16 @@
             pltpu.VMEM((2, 16, 128), F32),
             pltpu.VMEM((64, 128), F32),
             pltpu.VMEM((nc, 8, 128), F32),
-            pltpu.VMEM((16, 8, 384), F32),
-            pltpu.VMEM((16, 8, 384), F32),
-            pltpu.VMEM((16, 8, 384), F32),
-            pltpu.VMEM((16, 8, 384), F32),
-            pltpu.VMEM((8, 384), F32),
-            pltpu.VMEM((8, 384), F32),
+            pltpu.VMEM((16, 32, 128), BF16),
+            pltpu.VMEM((16, 32, 128), BF16),
+            pltpu.VMEM((16, 32, 128), BF16),
+            pltpu.VMEM((16, 32, 128), BF16),
+            pltpu.VMEM((32, 128), BF16),
+            pltpu.VMEM((32, 128), BF16),
             pltpu.SemaphoreType.DMA((15,)),
             pltpu.SemaphoreType.DMA((15,)),
             pltpu.SemaphoreType.DMA((5,)),
-            pltpu.SemaphoreType.DMA((4,)),
+            pltpu.SemaphoreType.DMA((6,)),
         ],
         compiler_params=pltpu.CompilerParams(
             collective_id=0, has_side_effects=True, vmem_limit_bytes=60 * 1024 * 1024
@@ -573,12 +590,17 @@
             jax.ShapeDtypeStruct((8, 512), F32),
             jax.ShapeDtypeStruct((32, 64, 256), BF16),
         ),
-        in_specs=[VMEM, VMEM, HBM],
-        out_specs=(VMEM,) * 4 + (HBM,),
+        in_specs=[HBM] * 3,
+        out_specs=(HBM,) * 5,
         scratch_shapes=[
+            pltpu.VMEM((16, 32, 128), BF16),
+            pltpu.VMEM((8, 512), F32),
             pltpu.VMEM((32, 64, 256), BF16),
-            pltpu.SemaphoreType.DMA((4,)),
-            pltpu.SemaphoreType.DMA((4,)),
+            pltpu.VMEM((9, 32, 32), F32),
+            pltpu.VMEM((32, 512), F32),
+            pltpu.VMEM((32, 512), F32),
+            pltpu.SemaphoreType.DMA((6,)),
+            pltpu.SemaphoreType.DMA((8,)),
         ],
         compiler_params=pltpu.CompilerParams(vmem_limit_bytes=60 * 1024 * 1024),
         name="finish",

time: 59 us -> 52.8 us (0.89)
  Pallas kernels: 58.2 us -> 52.1 us
    pallas_call x1, Pallas kernels: 54.6 us -> 49.9 us  [shards(): pl.pallas_call(functools.partial(pair_kernel, nr, nc), out_shape=(jax.Sha...]
    pallas_call x1, Pallas kernels: 3.62 us -> 2.18 us  [shards(): pl.pallas_call(functools.partial(finish_kernel, 32.0 / (8 * nr * nc)), ou...]
where the time goes in v4:
time: 52.8 us; the launch traced here: 52.7 us
  Pallas kernels  52.1 us (99%)
  between operations  0.64 us (1%)
    pallas_call x1, Pallas kernels, shards(): pl.pallas_call(functools.partial(pair_kernel, nr, nc), out_shape=(jax.Sha...  49.9 us
    pallas_call x1, Pallas kernels, shards(): pl.pallas_call(functools.partial(finish_kernel, 32.0 / (8 * nr * nc)), ou...  2.18 us

profile of v4, /device:TPU:1, one launch (start us, length us, event | category | flops | bytes accessed | tf_op | source)
XLA Modules:
  0.0 52.7 jit_solution(15692094308053773645)
XLA Ops:
  0.6 49.9 %pair_kernel.1 = (bf16[32,64,256]{2,1,0:T(8,128)(2,1)}, bf16[16,32,128]{2,1,0:T(8,128)(2,1)}, f32[8,512]{1,0:T(8,128)}) custom-call(bf16[8,512]{1,0:T(8,128)(2,1)} %e_hbm.1, bf16[32,512]{1,0:T(8,128)(2,1)} %bitcast.4, bf16[32,512]{1,0:T(8,128)(2,1)} %bitcast.5, bf16[9,32,32]{2,1,0:T(8,128)(2,1)} %w_hbm.1, bf16[32,64,256]{2,1,0:T(8,128)(2,1)} %cot_hbm.1), custom_call_target="tpu_custom_call" | custom-call | tf_op jit(solution)/shard_map/pair_kernel/pallas_call | solution.py:537
  50.5 2.2 %finish.1 = (f32[9,32,32]{2,1,0:T(8,128)}, f32[32,512]{1,0:T(8,128)}, f32[32,512]{1,0:T(8,128)}, f32[8,512]{1,0:T(8,128)}, bf16[32,64,256]{2,1,0:T(8,128)(2,1)}) custom-call(bf16[16,32,128]{2,1,0:T(8,128)(2,1)} %get-tuple-element.13.sums_in, f32[8,512]{1,0:T(8,128)} %get-tuple-element.14.eg_in, bf16[32,64,256]{2,1,0:T(8,128)(2,1)} %get-tuple-element.15.pair_in), custom_call_target="tpu_custom_call" | custom-call | tf_op jit(solution)/shard_map/finish/pallas_call | solution.py:584

commit v5 on v4

--- a/solution.py
+++ b/solution.py
@@ -61,9 +61,8 @@
 def softplus_and_slope(y):
     t = jnp.exp2(-jnp.abs(y))
     u = 1.0 + t
-    inv = pltpu.reciprocal(u, approx=True, full_range=False)
-    inv = inv * (2.0 - u * inv)
-    log = jnp.where(t < 1 / 256, t * (LOG2E - (0.5 * LOG2E) * t), jnp.log2(u))
+    inv = pltpu.reciprocal(u, full_range=False)
+    log = jnp.where(t < 2.0**-11, t * LOG2E, jnp.log2(u))
     return LN2 * (jnp.maximum(y, 0.0) + log), jnp.where(y >= 0, inv, t * inv)
 
 
@@ -78,7 +77,7 @@
         tf[:, 768 + 256 * b : 1024 + 256 * b] = jnp.where(same, x[2], jnp.where(below, x[1], 0.0)).astype(BF16)
 
 
-def mask_cotangent(r, c, cot_ref, mall, mt):
+def mask_cotangent(r, c, cot_ref, move, mall, mt):
     for k in range(4):
         x = cot_ref[:, 16 * k : 16 * k + 16, :].astype(F32)
         row = r * 64 + 16 * k + iota((16, 256), 0)
@@ -86,13 +85,14 @@
         for half in range(2):
             mall[:, lanes(2 * k + half)] = x[:, 8 * half : 8 * half + 8].reshape(256, 256).astype(BF16)
     for b in range(3):
+        move[272 * b : 272 * b + 272, :] = one_hot(iota((272, 256), 0) - 4 * b == iota((272, 256), 1))
         mt[0, :, 256 * b : 256 * b + 256] = jnp.zeros((272, 256), BF16)
         mt[9, :, 256 * b : 256 * b + 256] = jnp.zeros((272, 256), BF16)
 
     def body(g):
+        moved = dot_nt(move[...], mall[:, lanes(g)]).astype(BF16)
         for b in range(3):
-            move = one_hot(iota((272, 256), 0) - 4 * b == iota((272, 256), 1))
-            mt[g + 1, :, 256 * b : 256 * b + 256] = dot_nt(move, mall[:, lanes(g)]).astype(BF16)
+            mt[g + 1, :, 256 * b : 256 * b + 256] = moved[272 * b : 272 * b + 272]
 
     loop(8, body)
 
@@ -124,17 +124,20 @@
     rsum[...] = jnp.zeros_like(rsum)
 
     def body(step):
-        for part in range(3):
-            rows = pl.ds(pl.multiple_of(24 * step + 8 * part, 8), 8)
-            right = colf[rows, :]
-            total = jnp.zeros((8, 256), F32)
-            for h in range(9):
-                value, slope = softplus_and_slope(right + rowf[h : h + 1, :])
+        parts = [pl.ds(pl.multiple_of(24 * step + 8 * part, 8), 8) for part in range(3)]
+        totals = [jnp.zeros((8, 256), F32)] * 3
+        for h in range(9):
+            left = rowf[h : h + 1, :]
+            row = jnp.zeros((8, 256), F32)
+            for k, rows in enumerate(parts):
+                value, slope = softplus_and_slope(colf[rows, :] + left)
                 act[h, rows, :] = value
                 p = z[h, rows, :] * slope
-                total += p
-                rsum[8 * h : 8 * h + 8, :] += p
-            cacc[rows, :] = total
+                totals[k] += p
+                row += p
+            rsum[8 * h : 8 * h + 8, :] += row
+        for k, rows in enumerate(parts):
+            cacc[rows, :] = totals[k]
 
     loop(11, body)
 
@@ -192,28 +195,40 @@
     out_ref[:, 16 * k : 16 * k + 16, :] = jnp.where((col >= row)[None], y, 0.0).astype(BF16)
 
 
-def tap_gradient(mall, a3, taps):
-    s0, s1 = iota((256, 256), 0) & 7, iota((256, 256), 1) & 7
-    same, above, below = s1 == s0, s1 == s0 + 4, s1 == s0 - 4
-    by_channel = one_hot(((iota((32, 512), 1) & 255) >> 3) == iota((32, 512), 0))
-    rows = [None] * 9
-    for b in range(3):
-        g0 = dot(mall[...], a3[0:2048, 256 * b : 256 * b + 256])
-        g1 = dot(mall[...], a3[256:2304, 256 * b : 256 * b + 256])
-        ys = (
-            jnp.where(same, g0, 0.0),
-            jnp.where(above, g0, jnp.where(below, g1, 0.0)),
-            jnp.where(same, g1, 0.0),
-        )
-        for a in range(3):
-            rows[3 * a + b] = dot(by_channel, jnp.concatenate(halves(ys[a]), axis=0))
+def build_picks(picks):
+    for s in range(8):
+        k, n = iota((256, 128), 0), iota((256, 128), 1)
+        for which, wanted in enumerate((s, (s + 4) % 8)):
+            picks[which, 256 * s : 256 * s + 256, :] = one_hot(k == 8 * n + wanted)
+
+
+def tap_gradient(mall, a3, picks, gram, taps):
+    for u in range(2):
+        x = dot(mall[...], a3[256 * u : 256 * u + 2048, :])
+        for k in range(6):
+            gram[6 * u + k] = x[:, 128 * k : 128 * k + 128]
+
+    def part(s, u, b):
+        return jnp.concatenate([gram[6 * u + 2 * b + k, pl.ds(s, 32, stride=8), :] for k in range(2)], axis=1)
+
+    def folded(x, which):
+        high, low = halves(x)
+        y = dot(jnp.concatenate([high, low], axis=0), picks[which])
+        return y[0 : x.shape[0]] + y[x.shape[0] :]
+
+    outer = [jnp.concatenate([part(s, u, b) for s in range(8)], axis=1) for u in range(2) for b in range(3)]
+    outer = folded(jnp.concatenate(outer, axis=0), 0)
+    inner = [jnp.concatenate([part(s, s // 4, b) for s in range(8)], axis=1) for b in range(3)]
+    inner = folded(jnp.concatenate(inner, axis=0), 1)
+    rows = [outer[32 * b : 32 * b + 32] for b in range(3)]
+    rows += [inner[32 * b : 32 * b + 32] for b in range(3)]
+    rows += [outer[96 + 32 * b : 128 + 32 * b] for b in range(3)]
+    lane = iota((32, 128), 1)
     for q in range(3):
-        group = rows[4 * q : 4 * q + 4]
-        pick = jnp.concatenate(
-            [one_hot((iota((256, 128), 0) >> 3) + 32 * k == iota((256, 128), 1)) for k in range(len(group))], axis=0
-        )
-        high, low = halves(jnp.concatenate(group, axis=1))
-        taps[32 * q : 32 * q + 32, :] = dot(high, pick) + dot(low, pick)
+        total = jnp.zeros((32, 128), F32)
+        for k, x in enumerate(rows[4 * q : 4 * q + 4]):
+            total = jnp.where((lane >> 5) == k, pltpu.roll(x, 32 * k, 1) if k else x, total)
+        taps[32 * q : 32 * q + 32, :] = total
 
 
 LOCAL_SCRATCH = [
@@ -226,6 +241,9 @@
     pltpu.VMEM((2304, 768), BF16),
     pltpu.VMEM((9, 272, 256), F32),
     pltpu.VMEM((256, 1536), BF16),
+    pltpu.VMEM((816, 256), BF16),
+    pltpu.VMEM((2, 2048, 128), BF16),
+    pltpu.VMEM((12, 256, 128), F32),
     pltpu.VMEM((272, 256), F32),
     pltpu.VMEM((72, 256), F32),
     pltpu.VMEM((4, 16, 128), F32),
@@ -241,11 +259,10 @@
         self.r, self.c, self.nr, self.nc = r, c, nr, nc
         self.per = nr // nc
         self.rb, self.rm = lax.div(r, self.per), lax.rem(r, self.per)
-        bits1 = ((r, 8, 0), (r, 16, 0), (c, 2, 1), (c, 4, 1))
-        bits2 = ((r, 1, 0), (r, 2, 0), (r, 4, 0), (c, 1, 1))
-        self.k1, self.group1 = self.group(bits1)
-        self.k2, self.group2 = self.group(bits2)
-        _, self.group0 = self.group(((c, 1, 1), (c, 2, 1), (c, 4, 1)))
+        _, self.quad = self.group(((r, 1, 0), (r, 2, 0)))
+        _, self.line = self.group(((c, 1, 1), (c, 2, 1), (c, 4, 1)))
+        self.k1, self.group1 = self.group(((r, 1, 0), (r, 8, 0), (r, 16, 0), (c, 2, 1), (c, 4, 1)))
+        self.k2, self.group2 = self.group(((r, 2, 0), (r, 4, 0), (c, 1, 1)))
         self.has_up, self.has_down = r > 0, r < nr - 1
         self.has_left, self.has_right = c > 0, c < nc - 1
         self.ends_block = (self.rm == self.per - 1) & (self.rb < nc - 1)
@@ -269,34 +286,47 @@
     def other(self, k):
         return self.per * self.c + k, self.rb
 
+    def targets(self, col):
+        return [(lax.rem(self.r + self.per * k, self.nr), col) for k in range(self.nr // self.per)]
+
     def greet(self):
-        r, c, nc, per = self.r, self.c, self.nc, self.per
+        r, c, nc, per, rb, rm = self.r, self.c, self.nc, self.per, self.rb, self.rm
         barrier = pltpu.get_barrier_semaphore()
 
         def signal(a, b):
             pl.semaphore_signal(barrier, inc=1, device_id=(a, b), device_id_type=MESH)
-
-        def signal_other(a, b):
-            pl.when((a != r) | (b != c))(lambda: signal(a, b))
 
         def signal_all(col):
             for k in range(per):
                 signal(per * c + k, col)
 
-        for a, b, _ in self.group0 + self.group1 + self.group2:
+        is_first, is_last = c == 0, c == nc - 1
+        before_is_me = is_last & (rb == nc - 2)
+        after_is_me = is_first & (rb == 1)
+        for a, b, _ in self.quad + self.line:
             signal(a, b)
-        for k in range(per):
-            signal_other(*self.other(k))
+        pl.when(jnp.logical_not(self.in_others))(lambda: signal(per * c + rm, c))
+        for _, b, _ in self.line:
+            signal(per * c + rm, b)
+        pl.when(self.has_up)(lambda: signal(r - 1, nc - 1))
+        pl.when(self.has_down)(lambda: signal(r + 1, 0))
+        pl.when(self.has_left & jnp.logical_not(before_is_me))(lambda: signal(per * (c - 1) + rm, nc - 1))
+        pl.when(self.has_right & jnp.logical_not(after_is_me))(lambda: signal(per * (c + 1) + rm, 0))
+        pl.when(jnp.logical_not(self.in_others))(lambda: signal(per * c + rm, rb))
+        for a, _, _ in self.quad:
+            signal(per * (c - rb) + a, rb)
         pl.when(self.has_up)(lambda: signal(r - 1, c))
         pl.when(self.has_down)(lambda: signal(r + 1, c))
-        pl.when(self.has_left)(lambda: signal(per * c - 1, self.rb))
-        pl.when(self.has_right)(lambda: signal(per * c + per, self.rb))
-        pl.when(self.ends_block)(lambda: signal_all(self.rb + 1))
-        pl.when(self.starts_block)(lambda: signal_all(self.rb - 1))
-        n = nc - 1 + per + 30
+        pl.when(self.ends_block)(lambda: signal_all(rb + 1))
+        pl.when(self.starts_block)(lambda: signal_all(rb - 1))
+        for a, b, _ in self.group1 + self.group2:
+            signal(a, b)
+        n = len(self.quad + self.line + self.group1 + self.group2) + nc + per
+        up, down = self.has_up, self.has_down
         for cond, m in (
-            (self.in_others, -1), (self.has_up, 1), (self.has_down, 1), (self.has_left, 1),
-            (self.has_right, 1), (self.ends_block, per), (self.starts_block, per),
+            (self.in_others, -2), (is_last & down, nc), (is_first & up, nc),
+            (is_last & (rb < nc - 1), nc), (before_is_me, -1), (is_first & (rb > 0), nc), (after_is_me, -1),
+            (up, 1), (down, 1), (self.has_left, 1), (self.has_right, 1),
         ):
             n = n + jnp.where(cond, m, 0)
         return n
@@ -319,8 +349,8 @@
 def pair_kernel(
     nr, nc, e_hbm, lpt_hbm, rpt_hbm, w_hbm, cot_hbm,
     out_hbm, sums_hbm, eg_hbm,
-    rowf, colf, taps, mall, mt, act, a3, z, tf, cacc, rsum, cols, col_ends, row_main, row_ends,
-    out_ref, eg_ref, feats, e_ref, w_ref, cot_ref, proj, es, eb, el, eh, fb, blocks, row_feats, col_feats,
+    rowf, colf, taps, mall, mt, act, a3, z, tf, move, picks, gram, cacc, rsum, cols, col_ends, row_main, row_ends,
+    out_ref, eg_ref, feats, e_ref, w_ref, cot_ref, own, quad, proj, es, eb, el, eh, blocks, row_feats, col_feats,
     cparts, cends, rends, turned, gparts, buf, r1, r2, r3, mid, fin, recv, send, loads, stores,
 ):
     ins = ((e_hbm, e_ref), (w_hbm, w_ref), (lpt_hbm, proj.at[0:32]), (rpt_hbm, proj.at[32:64]), (cot_hbm, cot_ref))
@@ -331,61 +361,79 @@
     r, c, per, rb, rm, k1, k2 = p.r, p.c, p.per, p.rb, p.rm, p.k1, p.k2
     greeted = p.greet()
     put, put_other = p.senders(send, recv)
-
+    rows8, rows7 = gparts, gparts.at[0 : nc - 1]
+
+    proj[64:128, :] = jnp.zeros((64, 512), BF16)
     ins[0].wait()
     e = e_ref[...].astype(F32)
     es[...] = jnp.concatenate([e[:, 0:256], e[:, 256:512]], axis=0).astype(BF16)
-    pl.semaphore_wait(pltpu.get_barrier_semaphore(), greeted)
-
-    for a, b, _ in p.group0:
-        put(es, a, b, eb.at[c], 0)
-    pltpu.make_async_copy(es, eb.at[c], recv.at[0]).start()
-    proj[64:128, :] = jnp.zeros((64, 512), BF16)
+    ins[2].wait()
+    ins[3].wait()
+    own[...] = dot_nt(e_ref[...], proj[...]).astype(BF16).astype(F32)
     ins[1].wait()
     build_taps(w_ref, tf)
     ins[4].wait()
-    mask_cotangent(r, c, cot_ref, mall, mt)
-    ins[2].wait()
-    ins[3].wait()
+    mask_cotangent(r, c, cot_ref, move, mall, mt)
+    pl.semaphore_wait(pltpu.get_barrier_semaphore(), greeted)
+
+    for a, b, _ in p.quad:
+        put(own, a, b, quad.at[rm], 1)
+    pltpu.make_async_copy(own, quad.at[rm], recv.at[1]).start()
+
+    def put_line(row, dst, sem):
+        for k in range(nc):
+            put(own, row, k, dst, sem)
+
+    is_first, is_last = c == 0, c == nc - 1
+    row_after, row_before = is_last & p.has_down, is_first & p.has_up
+    pl.when(row_after)(lambda: put_line(r + 1, row_feats.at[0], 2))
+    pl.when(row_before)(lambda: put_line(r - 1, row_feats.at[1], 3))
+    for a, b, _ in p.line:
+        put(es, a, b, eb.at[c], 0)
+    pltpu.make_async_copy(es, eb.at[c], recv.at[0]).start()
+
+    def put_targets(src, col, dst, sem):
+        first, *rest = p.targets(col)
+        mine = c == col
+        pl.when(mine)(lambda: pltpu.make_async_copy(src, dst, recv.at[sem]).start())
+        pl.when(jnp.logical_not(mine))(lambda: put(src, *first, dst, sem))
+        for a, b in rest:
+            put(src, a, b, dst, sem)
+
+    col_after, col_before = is_last & (rb < nc - 1), is_first & (rb > 0)
+    wait_bytes(quad, recv.at[1])
+    put_targets(quad, rb, blocks.at[c], 15)
+    pl.when(col_after)(lambda: put_targets(quad.at[per - 1], rb + 1, col_feats.at[0], 4))
+    pl.when(col_before)(lambda: put_targets(quad.at[0], rb - 1, col_feats.at[1], 5))
+    input_gradient(mt, tf, z)
+    build_picks(picks)
+
     wait_bytes(eb, recv.at[0])
     e = eb[...].astype(F32)
     el[...] = e[:, 0:8].reshape(64, 256).astype(BF16)
     eh[...] = e[:, 8:16].reshape(64, 256).astype(BF16)
-    fb[...] = (dot_nt(el[...], proj[:, 0:256]) + dot_nt(eh[...], proj[:, 256:512])).astype(BF16)
-
-    for k in range(per):
-        put_other(fb, k, blocks.at[rm], 1)
-    bottom, top = fb.at[48:64], fb.at[0:16]
-
-    def put_all(src, col, dst, sem):
-        for k in range(per):
-            put(src, per * c + k, col, dst, sem)
-
-    pl.when(p.has_down)(lambda: put(bottom, r + 1, c, row_feats.at[0], 2))
-    pl.when(p.has_up)(lambda: put(top, r - 1, c, row_feats.at[1], 3))
-    pl.when(p.ends_block)(lambda: put_all(bottom, rb + 1, col_feats.at[0], 4))
-    pl.when(p.starts_block)(lambda: put_all(top, rb - 1, col_feats.at[1], 5))
-    input_gradient(mt, tf, z)
+    feats[8:72, :] = dot_nt(el[...], proj[:, 0:256]) + dot_nt(eh[...], proj[:, 256:512])
 
     def arrive(cond, ref, sem):
         pl.when(cond)(lambda: wait_bytes(ref, sem))
-        pl.when(jnp.logical_not(cond))(lambda: ref.__setitem__(..., jnp.full(ref.shape, OUTSIDE, BF16)))
+        pl.when(jnp.logical_not(cond))(lambda: ref.__setitem__(..., jnp.full(ref.shape, OUTSIDE, F32)))
 
     arrive(p.has_up, row_feats.at[0], recv.at[2])
     arrive(p.has_down, row_feats.at[1], recv.at[3])
     arrive(p.has_left, col_feats.at[0], recv.at[4])
     arrive(p.has_right, col_feats.at[1], recv.at[5])
-    wait_bytes(blocks, recv.at[1])
-    feats[0:4, :] = row_feats[0].astype(F32)[12:16]
-    feats[4:68, :] = fb[...].astype(F32)
-    feats[68:72, :] = row_feats[1].astype(F32)[0:4]
-    feats[72:128, :] = jnp.zeros((56, 128), F32)
-    rows = feats[0:128, :].astype(BF16)
-    feats[128:132, :] = col_feats[0].astype(F32)[12:16]
-    feats[132 : 132 + 64 * per, :] = blocks[...].reshape(64 * per, 128).astype(F32)
-    feats[388:392, :] = col_feats[1].astype(F32)[0:4]
-    feats[392:400, :] = jnp.zeros((8, 128), F32)
-    features(rows, feats[128:400, :].astype(BF16), rowf, colf)
+    wait_bytes(blocks, recv.at[15])
+    feats[0:8, :] = row_feats[0]
+    feats[72:80, :] = row_feats[1]
+    feats[80:136, :] = jnp.zeros((56, 128), F32)
+    feats[136:144, :] = col_feats[0]
+    for k in range(per):
+        for q in range(nc):
+            at = 144 + 8 * (nc * k + q)
+            feats[at : at + 8, :] = blocks[q, k]
+    feats[400:408, :] = col_feats[1]
+    feats[408:416, :] = jnp.zeros((8, 128), F32)
+    features(feats[4:132, :].astype(BF16), feats[140:412, :].astype(BF16), rowf, colf)
     elementwise(rowf, colf, z, act, cacc, rsum)
     sums(cacc, rsum, cols, col_ends, row_main, row_ends)
 
@@ -397,11 +445,7 @@
     pl.when(p.has_right)(lambda: put(col_ends.at[1], per * c + per, rb, cends.at[1, rm], 10))
 
     build_windows(act, a3)
-    tap_gradient(mall, a3, taps)
-    for k in range(16):
-        piece = taps[8 * k : 8 * k + 8, :] if k < 12 else jnp.zeros((8, 128), F32)
-        buf[k, 16:32, :] = jnp.concatenate([piece, jnp.zeros((8, 128), F32)], axis=0).astype(BF16)
-
+    tap_gradient(mall, a3, picks, gram, taps)
     def gather_sum(cond, ref, sem):
         pl.when(cond)(lambda: wait_bytes(ref, sem))
         pl.when(jnp.logical_not(cond))(lambda: ref.__setitem__(..., jnp.zeros(ref.shape, F32)))
@@ -425,15 +469,17 @@
     high, low = halves(turned[...])
     for half, ref in enumerate((el, eh)):
         part = dot_tn(high, ref[...]) + dot_tn(low, ref[...])
-        for k in range(8):
-            at = slice(16 * (k // 2), 16 * (k // 2) + 16), slice(128 * (k % 2), 128 * (k % 2) + 128)
-            buf[4 * (k // 2) + 2 * half + k % 2, 0:16, :] = part[at].astype(BF16)
+        for k in range(16):
+            at = 4 * (k // 2) + 2 * half + k % 2
+            x = part[8 * (k // 2) : 8 * (k // 2) + 8, 128 * (k % 2) : 128 * (k % 2) + 128]
+            y = taps[8 * at : 8 * at + 8, :] if at < 12 else jnp.zeros((8, 128), F32)
+            buf[at] = jnp.concatenate([x, y], axis=0).astype(BF16)
 
     for a, b, at in p.group1:
         put(buf.at[at], a, b, r1.at[k1], 11)
     pltpu.make_async_copy(buf.at[k1], r1.at[k1], recv.at[11]).start()
 
-    for a, b, _ in p.group0:
+    for a, b, _ in p.line:
         put(turned.at[pl.ds(pl.multiple_of(8 * b, 8), 8)], a, b, gparts.at[c], 14)
     pltpu.make_async_copy(turned.at[pl.ds(pl.multiple_of(8 * c, 8), 8)], gparts.at[c], recv.at[14]).start()
 
@@ -470,26 +516,31 @@
     for copy in outs:
         copy.wait()
     wait_bytes(eb.at[0 : nc - 1], send.at[0])
-    pl.when(p.in_others)(lambda: wait_bytes(blocks.at[0 : per - 1], send.at[1]))
-    pl.when(jnp.logical_not(p.in_others))(lambda: wait_bytes(blocks, send.at[1]))
-    pl.when(p.has_down)(lambda: wait_bytes(bottom, send.at[2]))
-    pl.when(p.has_up)(lambda: wait_bytes(top, send.at[3]))
-    pl.when(p.ends_block)(lambda: wait_bytes(fb, send.at[4]))
-    pl.when(p.starts_block)(lambda: wait_bytes(fb, send.at[5]))
+    wait_bytes(quad.at[0 : per - 1], send.at[1])
+    pl.when(row_after)(lambda: wait_bytes(rows8, send.at[2]))
+    pl.when(row_before)(lambda: wait_bytes(rows8, send.at[3]))
+
+    def sent_targets(cond, mine, eight, seven, sem):
+        pl.when(cond & mine)(lambda: wait_bytes(seven, send.at[sem]))
+        pl.when(cond & jnp.logical_not(mine))(lambda: wait_bytes(eight, send.at[sem]))
+
+    sent_targets(col_after, rb + 1 == c, rows8, rows7, 4)
+    sent_targets(col_before, rb - 1 == c, rows8, rows7, 5)
+    sent_targets(rb >= 0, p.in_others, blocks, blocks.at[0 : nc - 1], 15)
     pl.when(p.in_others)(lambda: wait_bytes(cparts.at[0 : per - 1], send.at[6]))
     pl.when(jnp.logical_not(p.in_others))(lambda: wait_bytes(cparts, send.at[6]))
     pl.when(p.has_up)(lambda: wait_bytes(row_ends.at[0], send.at[7]))
     pl.when(p.has_down)(lambda: wait_bytes(row_ends.at[1], send.at[8]))
     pl.when(p.has_left)(lambda: wait_bytes(col_ends.at[0], send.at[9]))
     pl.when(p.has_right)(lambda: wait_bytes(col_ends.at[1], send.at[10]))
-    wait_bytes(r1.at[0:15], send.at[11])
-    wait_bytes(r2.at[0:15], send.at[12])
+    wait_bytes(r1.at[0 : r1.shape[0] - 1], send.at[11])
+    wait_bytes(r2.at[0 : r2.shape[0] - 1], send.at[12])
     wait_bytes(gparts.at[0 : nc - 1], send.at[14])
 
     wait_bytes(r3, recv.at[13])
     last = pltpu.make_async_copy(r3, sums_hbm, stores.at[5])
     last.start()
-    wait_bytes(r3.at[0:15], send.at[13])
+    wait_bytes(r3.at[0 : r3.shape[0] - 1], send.at[13])
     last.wait()
 
 
@@ -512,10 +563,10 @@
     for copy in ins:
         copy.start()
     ins[0].wait()
-    for ref, first, at in ((left_ref, 0, 1), (right_ref, 8, 2)):
-        for k in range(8):
-            x = sums_ref[first + k, 0:16, :].astype(F32)
-            ref[16 * (k // 4) : 16 * (k // 4) + 16, 128 * (k % 4) : 128 * (k % 4) + 128] = x * scale
+    for ref, first, at in ((left_ref, 0, 1), (right_ref, 16, 2)):
+        for k in range(16):
+            x = sums_ref[first + k].astype(F32)[0:8]
+            ref[8 * (k // 4) : 8 * (k // 4) + 8, 128 * (k % 4) : 128 * (k % 4) + 128] = x * scale
         outs[at].start()
     ins[1].wait()
     outs[3].start()
@@ -525,8 +576,8 @@
     for k in range(9):
         q, at = divmod(k, 4)
         for part in range(4):
-            x = sums_ref[4 * q + part, 16:32, :].astype(F32)
-            conv_ref[k, 8 * part : 8 * part + 8, :] = x[0:8, 32 * at : 32 * at + 32] * scale
+            x = sums_ref[4 * q + part].astype(F32)
+            conv_ref[k, 8 * part : 8 * part + 8, :] = x[8:16, 32 * at : 32 * at + 32] * scale
     outs[0].start()
     for copy in outs:
         copy.wait()
@@ -538,7 +589,7 @@
         functools.partial(pair_kernel, nr, nc),
         out_shape=(
             jax.ShapeDtypeStruct((32, 64, 256), BF16),
-            jax.ShapeDtypeStruct((16, 32, 128), BF16),
+            jax.ShapeDtypeStruct((32, 16, 128), BF16),
             jax.ShapeDtypeStruct((8, 512), F32),
         ),
         in_specs=[HBM] * 5,
@@ -547,32 +598,33 @@
         + [
             pltpu.VMEM((32, 64, 256), BF16),
             pltpu.VMEM((8, 512), F32),
-            pltpu.VMEM((400, 128), F32),
+            pltpu.VMEM((416, 128), F32),
             pltpu.VMEM((8, 512), BF16),
             pltpu.VMEM((9, 32, 32), BF16),
             pltpu.VMEM((32, 64, 256), BF16),
+            pltpu.VMEM((8, 128), F32),
+            pltpu.VMEM((per, 8, 128), F32),
             pltpu.VMEM((128, 512), BF16),
             pltpu.VMEM((16, 256), BF16),
             pltpu.VMEM((nc, 16, 256), BF16),
             pltpu.VMEM((64, 256), BF16),
             pltpu.VMEM((64, 256), BF16),
-            pltpu.VMEM((64, 128), BF16),
-            pltpu.VMEM((per, 64, 128), BF16),
-            pltpu.VMEM((2, 16, 128), BF16),
-            pltpu.VMEM((2, 16, 128), BF16),
+            pltpu.VMEM((nc, per, 8, 128), F32),
+            pltpu.VMEM((2, 8, 128), F32),
+            pltpu.VMEM((2, 8, 128), F32),
             pltpu.VMEM((per, 16, 128), F32),
             pltpu.VMEM((2, per, 16, 128), F32),
             pltpu.VMEM((2, 16, 128), F32),
             pltpu.VMEM((64, 128), F32),
             pltpu.VMEM((nc, 8, 128), F32),
-            pltpu.VMEM((16, 32, 128), BF16),
-            pltpu.VMEM((16, 32, 128), BF16),
-            pltpu.VMEM((16, 32, 128), BF16),
-            pltpu.VMEM((16, 32, 128), BF16),
-            pltpu.VMEM((32, 128), BF16),
-            pltpu.VMEM((32, 128), BF16),
-            pltpu.SemaphoreType.DMA((15,)),
-            pltpu.SemaphoreType.DMA((15,)),
+            pltpu.VMEM((32, 16, 128), BF16),
+            pltpu.VMEM((32, 16, 128), BF16),
+            pltpu.VMEM((8, 16, 128), BF16),
+            pltpu.VMEM((32, 16, 128), BF16),
+            pltpu.VMEM((16, 128), BF16),
+            pltpu.VMEM((16, 128), BF16),
+            pltpu.SemaphoreType.DMA((16,)),
+            pltpu.SemaphoreType.DMA((16,)),
             pltpu.SemaphoreType.DMA((5,)),
             pltpu.SemaphoreType.DMA((6,)),
         ],
@@ -593,7 +645,7 @@
         in_specs=[HBM] * 3,
         out_specs=(HBM,) * 5,
         scratch_shapes=[
-            pltpu.VMEM((16, 32, 128), BF16),
+            pltpu.VMEM((32, 16, 128), BF16),
             pltpu.VMEM((8, 512), F32),
             pltpu.VMEM((32, 64, 256), BF16),
             pltpu.VMEM((9, 32, 32), F32),

time: 52.8 us -> 51.9 us (0.983)
  Pallas kernels: 52.1 us -> 51.1 us
    pallas_call x1, Pallas kernels: 49.9 us -> 49 us  [shards(): pl.pallas_call(functools.partial(pair_kernel, nr, nc), out_shape=(jax.Sha...]
where the time goes in v5:
time: 51.9 us; the launch traced here: 51.8 us
  Pallas kernels  51.1 us (98%)
  between operations  0.64 us (1%)
    pallas_call x1, Pallas kernels, shards(): pl.pallas_call(functools.partial(pair_kernel, nr, nc), out_shape=(jax.Sha...  49 us
    pallas_call x1, Pallas kernels, shards(): pl.pallas_call(functools.partial(finish_kernel, 32.0 / (8 * nr * nc)), ou...  2.18 us

profile of v5, /device:TPU:1, one launch (start us, length us, event | category | flops | bytes accessed | tf_op | source)
XLA Modules:
  0.0 51.8 jit_solution(4060377435841644713)
XLA Ops:
  0.6 49.0 %pair_kernel.1 = (bf16[32,64,256]{2,1,0:T(8,128)(2,1)}, bf16[32,16,128]{2,1,0:T(8,128)(2,1)}, f32[8,512]{1,0:T(8,128)}) custom-call(bf16[8,512]{1,0:T(8,128)(2,1)} %e_hbm.1, bf16[32,512]{1,0:T(8,128)(2,1)} %bitcast.4, bf16[32,512]{1,0:T(8,128)(2,1)} %bitcast.5, bf16[9,32,32]{2,1,0:T(8,128)(2,1)} %w_hbm.1, bf16[32,64,256]{2,1,0:T(8,128)(2,1)} %cot_hbm.1), custom_call_target="tpu_custom_call" | custom-call | tf_op jit(solution)/shard_map/pair_kernel/pallas_call | solution.py:588
  49.6 2.2 %finish.1 = (f32[9,32,32]{2,1,0:T(8,128)}, f32[32,512]{1,0:T(8,128)}, f32[32,512]{1,0:T(8,128)}, f32[8,512]{1,0:T(8,128)}, bf16[32,64,256]{2,1,0:T(8,128)(2,1)}) custom-call(bf16[32,16,128]{2,1,0:T(8,128)(2,1)} %get-tuple-element.13.sums_in, f32[8,512]{1,0:T(8,128)} %get-tuple-element.14.eg_in, bf16[32,64,256]{2,1,0:T(8,128)(2,1)} %get-tuple-element.15.pair_in), custom_call_target="tpu_custom_call" | custom-call | tf_op jit(solution)/shard_map/finish/pallas_call | solution.py:636

commit v6 on v5

--- a/solution.py
+++ b/solution.py
@@ -97,14 +97,15 @@
     loop(8, body)
 
 
-def input_gradient(mt, tf, z):
-    def body(h):
-        z[h] = dot_nt_blocks(mt, tf, h)
-
-    loop(9, body)
-
-
-def dot_nt_blocks(mt, tf, h):
+def input_gradient(mt, tf, z, groups):
+    def body(h, _):
+        z[h] = group_gradient(mt, tf, h)
+        return 0
+
+    lax.fori_loop(*groups, body, 0)
+
+
+def group_gradient(mt, tf, h):
     left = jnp.concatenate([mt[h], mt[h + 1]], axis=1)
     right = jnp.concatenate(
         [tf[:, 768 * (1 - u) + 256 * b : 768 * (1 - u) + 256 * b + 256] for u in range(2) for b in range(3)], axis=0
@@ -195,39 +196,32 @@
     out_ref[:, 16 * k : 16 * k + 16, :] = jnp.where((col >= row)[None], y, 0.0).astype(BF16)
 
 
-def build_picks(picks):
-    for s in range(8):
-        k, n = iota((256, 128), 0), iota((256, 128), 1)
-        for which, wanted in enumerate((s, (s + 4) % 8)):
-            picks[which, 256 * s : 256 * s + 256, :] = one_hot(k == 8 * n + wanted)
-
-
-def tap_gradient(mall, a3, picks, gram, taps):
+def tap_gradient(mall, a3, gram, taps):
     for u in range(2):
         x = dot(mall[...], a3[256 * u : 256 * u + 2048, :])
         for k in range(6):
             gram[6 * u + k] = x[:, 128 * k : 128 * k + 128]
-
-    def part(s, u, b):
-        return jnp.concatenate([gram[6 * u + 2 * b + k, pl.ds(s, 32, stride=8), :] for k in range(2)], axis=1)
-
-    def folded(x, which):
-        high, low = halves(x)
-        y = dot(jnp.concatenate([high, low], axis=0), picks[which])
-        return y[0 : x.shape[0]] + y[x.shape[0] :]
-
-    outer = [jnp.concatenate([part(s, u, b) for s in range(8)], axis=1) for u in range(2) for b in range(3)]
-    outer = folded(jnp.concatenate(outer, axis=0), 0)
-    inner = [jnp.concatenate([part(s, s // 4, b) for s in range(8)], axis=1) for b in range(3)]
-    inner = folded(jnp.concatenate(inner, axis=0), 1)
-    rows = [outer[32 * b : 32 * b + 32] for b in range(3)]
-    rows += [inner[32 * b : 32 * b + 32] for b in range(3)]
-    rows += [outer[96 + 32 * b : 128 + 32 * b] for b in range(3)]
     lane = iota((32, 128), 1)
+
+    def along(b, k, sources):
+        total = jnp.zeros((32, 128), F32)
+        for at, (s, u) in enumerate(sources):
+            total = jnp.where((lane & 7) == at, gram[6 * u + 2 * b + k, pl.ds(s, 32, stride=8), :], total)
+        return total
+
+    sources = (
+        [(s, 0) for s in range(8)],
+        [((s + 4) % 8, 1 - s // 4) for s in range(8)],
+        [(s, 1) for s in range(8)],
+    )
+    x = [jnp.concatenate([along(b, k, sources[a]) for k in range(2)], axis=1) for a in range(3) for b in range(3)]
+    y = dot(jnp.concatenate(halves(jnp.concatenate(x, axis=0)), axis=0), one_hot((iota((256, 128), 0) >> 3) == iota((256, 128), 1)))
+    y = y[0:288] + y[288:576]
     for q in range(3):
         total = jnp.zeros((32, 128), F32)
-        for k, x in enumerate(rows[4 * q : 4 * q + 4]):
-            total = jnp.where((lane >> 5) == k, pltpu.roll(x, 32 * k, 1) if k else x, total)
+        for k in range(min(4, 9 - 4 * q)):
+            tap = y[32 * (4 * q + k) : 32 * (4 * q + k) + 32]
+            total = jnp.where((lane >> 5) == k, pltpu.roll(tap, 32 * k, 1) if k else tap, total)
         taps[32 * q : 32 * q + 32, :] = total
 
 
@@ -242,7 +236,6 @@
     pltpu.VMEM((9, 272, 256), F32),
     pltpu.VMEM((256, 1536), BF16),
     pltpu.VMEM((816, 256), BF16),
-    pltpu.VMEM((2, 2048, 128), BF16),
     pltpu.VMEM((12, 256, 128), F32),
     pltpu.VMEM((272, 256), F32),
     pltpu.VMEM((72, 256), F32),
@@ -349,9 +342,9 @@
 def pair_kernel(
     nr, nc, e_hbm, lpt_hbm, rpt_hbm, w_hbm, cot_hbm,
     out_hbm, sums_hbm, eg_hbm,
-    rowf, colf, taps, mall, mt, act, a3, z, tf, move, picks, gram, cacc, rsum, cols, col_ends, row_main, row_ends,
+    rowf, colf, taps, mall, mt, act, a3, z, tf, move, gram, cacc, rsum, cols, col_ends, row_main, row_ends,
     out_ref, eg_ref, feats, e_ref, w_ref, cot_ref, own, quad, proj, es, eb, el, eh, blocks, row_feats, col_feats,
-    cparts, cends, rends, turned, gparts, buf, r1, r2, r3, mid, fin, recv, send, loads, stores,
+    cparts, cends, rends, turned, gparts, buf, r1, r2, mid, fin, recv, send, loads, stores,
 ):
     ins = ((e_hbm, e_ref), (w_hbm, w_ref), (lpt_hbm, proj.at[0:32]), (rpt_hbm, proj.at[32:64]), (cot_hbm, cot_ref))
     ins = [pltpu.make_async_copy(src, dst, loads.at[k]) for k, (src, dst) in enumerate(ins)]
@@ -401,12 +394,12 @@
             put(src, a, b, dst, sem)
 
     col_after, col_before = is_last & (rb < nc - 1), is_first & (rb > 0)
+    input_gradient(mt, tf, z, (0, 5))
     wait_bytes(quad, recv.at[1])
     put_targets(quad, rb, blocks.at[c], 15)
     pl.when(col_after)(lambda: put_targets(quad.at[per - 1], rb + 1, col_feats.at[0], 4))
     pl.when(col_before)(lambda: put_targets(quad.at[0], rb - 1, col_feats.at[1], 5))
-    input_gradient(mt, tf, z)
-    build_picks(picks)
+    input_gradient(mt, tf, z, (5, 9))
 
     wait_bytes(eb, recv.at[0])
     e = eb[...].astype(F32)
@@ -445,7 +438,7 @@
     pl.when(p.has_right)(lambda: put(col_ends.at[1], per * c + per, rb, cends.at[1, rm], 10))
 
     build_windows(act, a3)
-    tap_gradient(mall, a3, picks, gram, taps)
+    tap_gradient(mall, a3, gram, taps)
     def gather_sum(cond, ref, sem):
         pl.when(cond)(lambda: wait_bytes(ref, sem))
         pl.when(jnp.logical_not(cond))(lambda: ref.__setitem__(..., jnp.zeros(ref.shape, F32)))
@@ -504,8 +497,8 @@
     wait_bytes(r2, recv.at[12])
     fin[...] = jnp.sum(r2[...].astype(F32), axis=0).astype(BF16)
     for a, b, _ in p.group1:
-        put(fin, a, b, r3.at[k1], 13)
-    pltpu.make_async_copy(fin, r3.at[k1], recv.at[13]).start()
+        put(fin, a, b, sums_hbm.at[k1], 13)
+    pltpu.make_async_copy(fin, sums_hbm.at[k1], recv.at[13]).start()
 
     wait_bytes(gparts, recv.at[14])
     high, low = halves(jnp.sum(gparts[...], axis=0))
@@ -537,11 +530,8 @@
     wait_bytes(r2.at[0 : r2.shape[0] - 1], send.at[12])
     wait_bytes(gparts.at[0 : nc - 1], send.at[14])
 
-    wait_bytes(r3, recv.at[13])
-    last = pltpu.make_async_copy(r3, sums_hbm, stores.at[5])
-    last.start()
-    wait_bytes(r3.at[0 : r3.shape[0] - 1], send.at[13])
-    last.wait()
+    wait_bytes(r1.at[0 : r1.shape[0] - 1], send.at[13])
+    wait_bytes(sums_hbm, recv.at[13])
 
 
 def finish_kernel(
@@ -620,7 +610,6 @@
             pltpu.VMEM((32, 16, 128), BF16),
             pltpu.VMEM((32, 16, 128), BF16),
             pltpu.VMEM((8, 16, 128), BF16),
-            pltpu.VMEM((32, 16, 128), BF16),
             pltpu.VMEM((16, 128), BF16),
             pltpu.VMEM((16, 128), BF16),
             pltpu.SemaphoreType.DMA((16,)),

time: 51.9 us -> 51.4 us (level)
    pallas_call x1, Pallas kernels: 49 us -> 48.4 us  [shards(): pl.pallas_call(functools.partial(pair_kernel, nr, nc), out_shape=(jax.Sha...]
where the time goes in v6:
time: 51.4 us; the launch traced here: 51.2 us
  Pallas kernels  50.6 us (98%)
  between operations  0.64 us (1%)
    pallas_call x1, Pallas kernels, shards(): pl.pallas_call(functools.partial(pair_kernel, nr, nc), out_shape=(jax.Sha...  48.4 us
    pallas_call x1, Pallas kernels, shards(): pl.pallas_call(functools.partial(finish_kernel, 32.0 / (8 * nr * nc)), ou...  2.18 us

profile of v6, /device:TPU:1, one launch (start us, length us, event | category | flops | bytes accessed | tf_op | source)
XLA Modules:
  0.0 51.2 jit_solution(15904952333873654238)
XLA Ops:
  0.6 48.4 %pair_kernel.1 = (bf16[32,64,256]{2,1,0:T(8,128)(2,1)}, bf16[32,16,128]{2,1,0:T(8,128)(2,1)}, f32[8,512]{1,0:T(8,128)}) custom-call(bf16[8,512]{1,0:T(8,128)(2,1)} %e_hbm.1, bf16[32,512]{1,0:T(8,128)(2,1)} %bitcast.4, bf16[32,512]{1,0:T(8,128)(2,1)} %bitcast.5, bf16[9,32,32]{2,1,0:T(8,128)(2,1)} %w_hbm.1, bf16[32,64,256]{2,1,0:T(8,128)(2,1)} %cot_hbm.1), custom_call_target="tpu_custom_call" | custom-call | tf_op jit(solution)/shard_map/pair_kernel/pallas_call | solution.py:578
  49.0 2.2 %finish.1 = (f32[9,32,32]{2,1,0:T(8,128)}, f32[32,512]{1,0:T(8,128)}, f32[32,512]{1,0:T(8,128)}, f32[8,512]{1,0:T(8,128)}, bf16[32,64,256]{2,1,0:T(8,128)(2,1)}) custom-call(bf16[32,16,128]{2,1,0:T(8,128)(2,1)} %get-tuple-element.13.sums_in, f32[8,512]{1,0:T(8,128)} %get-tuple-element.14.eg_in, bf16[32,64,256]{2,1,0:T(8,128)(2,1)} %get-tuple-element.15.pair_in), custom_call_target="tpu_custom_call" | custom-call | tf_op jit(solution)/shard_map/finish/pallas_call | solution.py:625

commit v7 on v6

--- a/solution.py
+++ b/solution.py
@@ -113,10 +113,14 @@
     return dot(left, right)
 
 
-def features(rows, cols, rowf, colf):
+def features(rows, blocks, before, after, rowf, colf):
     k, n = iota((128, 256), 0), iota((128, 256), 1) >> 3
-    colf[...] = dot(cols, one_hot(k == n + 32)) * LOG2E
-    x = dot(rows, one_hot(k == n))
+    picks = [one_hot(k == n + 32 * at) for at in range(4)]
+    first = dot(before, picks[3])
+    last = dot(after, picks[0])
+    x = [first[4:8]] + [dot(blocks, pick) for pick in picks] + [last[0:4], jnp.zeros((8, 256), F32)]
+    colf[...] = jnp.concatenate(x, axis=0) * LOG2E
+    x = dot(rows, picks[0])
     x = jnp.where((iota((128, 256), 0) & 7) == (iota((128, 256), 1) & 7), x, 0.0).astype(BF16)
     rowf[...] = dot(one_hot((iota((16, 128), 1) >> 3) == iota((16, 128), 0)), x) * LOG2E
 
@@ -343,7 +347,7 @@
     nr, nc, e_hbm, lpt_hbm, rpt_hbm, w_hbm, cot_hbm,
     out_hbm, sums_hbm, eg_hbm,
     rowf, colf, taps, mall, mt, act, a3, z, tf, move, gram, cacc, rsum, cols, col_ends, row_main, row_ends,
-    out_ref, eg_ref, feats, e_ref, w_ref, cot_ref, own, quad, proj, es, eb, el, eh, blocks, row_feats, col_feats,
+    out_ref, eg_ref, feats, e_ref, w_ref, cot_ref, own, right, packed, quad, proj, es, eb, el, eh, blocks, row_feats, col_feats,
     cparts, cends, rends, turned, gparts, buf, r1, r2, mid, fin, recv, send, loads, stores,
 ):
     ins = ((e_hbm, e_ref), (w_hbm, w_ref), (lpt_hbm, proj.at[0:32]), (rpt_hbm, proj.at[32:64]), (cot_hbm, cot_ref))
@@ -363,6 +367,8 @@
     ins[2].wait()
     ins[3].wait()
     own[...] = dot_nt(e_ref[...], proj[...]).astype(BF16).astype(F32)
+    group = iota((8, 128), 1) >> 5
+    right[...] = jnp.where(group == rm, pltpu.roll(own[...], lax.rem(32 * rm + 96, 128), 1), 0.0)
     ins[1].wait()
     build_taps(w_ref, tf)
     ins[4].wait()
@@ -370,8 +376,8 @@
     pl.semaphore_wait(pltpu.get_barrier_semaphore(), greeted)
 
     for a, b, _ in p.quad:
-        put(own, a, b, quad.at[rm], 1)
-    pltpu.make_async_copy(own, quad.at[rm], recv.at[1]).start()
+        put(right, a, b, quad.at[rm], 1)
+    pltpu.make_async_copy(right, quad.at[rm], recv.at[1]).start()
 
     def put_line(row, dst, sem):
         for k in range(nc):
@@ -396,9 +402,10 @@
     col_after, col_before = is_last & (rb < nc - 1), is_first & (rb > 0)
     input_gradient(mt, tf, z, (0, 5))
     wait_bytes(quad, recv.at[1])
-    put_targets(quad, rb, blocks.at[c], 15)
-    pl.when(col_after)(lambda: put_targets(quad.at[per - 1], rb + 1, col_feats.at[0], 4))
-    pl.when(col_before)(lambda: put_targets(quad.at[0], rb - 1, col_feats.at[1], 5))
+    packed[...] = jnp.sum(quad[...], axis=0)
+    put_targets(packed, rb, blocks.at[c], 15)
+    pl.when(col_after)(lambda: put_targets(packed, rb + 1, col_feats.at[0], 4))
+    pl.when(col_before)(lambda: put_targets(packed, rb - 1, col_feats.at[1], 5))
     input_gradient(mt, tf, z, (5, 9))
 
     wait_bytes(eb, recv.at[0])
@@ -419,14 +426,8 @@
     feats[0:8, :] = row_feats[0]
     feats[72:80, :] = row_feats[1]
     feats[80:136, :] = jnp.zeros((56, 128), F32)
-    feats[136:144, :] = col_feats[0]
-    for k in range(per):
-        for q in range(nc):
-            at = 144 + 8 * (nc * k + q)
-            feats[at : at + 8, :] = blocks[q, k]
-    feats[400:408, :] = col_feats[1]
-    feats[408:416, :] = jnp.zeros((8, 128), F32)
-    features(feats[4:132, :].astype(BF16), feats[140:412, :].astype(BF16), rowf, colf)
+    ends = [jnp.concatenate([col_feats[k], jnp.zeros((8, 128), F32)], axis=0).astype(BF16) for k in range(2)]
+    features(feats[4:132, :].astype(BF16), blocks[...].reshape(8 * nc, 128).astype(BF16), *ends, rowf, colf)
     elementwise(rowf, colf, z, act, cacc, rsum)
     sums(cacc, rsum, cols, col_ends, row_main, row_ends)
 
@@ -588,10 +589,12 @@
         + [
             pltpu.VMEM((32, 64, 256), BF16),
             pltpu.VMEM((8, 512), F32),
-            pltpu.VMEM((416, 128), F32),
+            pltpu.VMEM((136, 128), F32),
             pltpu.VMEM((8, 512), BF16),
             pltpu.VMEM((9, 32, 32), BF16),
             pltpu.VMEM((32, 64, 256), BF16),
+            pltpu.VMEM((8, 128), F32),
+            pltpu.VMEM((8, 128), F32),
             pltpu.VMEM((8, 128), F32),
             pltpu.VMEM((per, 8, 128), F32),
             pltpu.VMEM((128, 512), BF16),
@@ -599,7 +602,7 @@
             pltpu.VMEM((nc, 16, 256), BF16),
             pltpu.VMEM((64, 256), BF16),
             pltpu.VMEM((64, 256), BF16),
-            pltpu.VMEM((nc, per, 8, 128), F32),
+            pltpu.VMEM((nc, 8, 128), F32),
             pltpu.VMEM((2, 8, 128), F32),
             pltpu.VMEM((2, 8, 128), F32),
             pltpu.VMEM((per, 16, 128), F32),

time: 51.4 us -> 49.2 us (0.957)
  Pallas kernels: 50.6 us -> 48.5 us
    pallas_call x1, Pallas kernels: 48.4 us -> 46.3 us  [shards(): pl.pallas_call(functools.partial(pair_kernel, nr, nc), out_shape=(jax.Sha...]
where the time goes in v7:
time: 49.2 us; the launch traced here: 49.1 us
  Pallas kernels  48.5 us (99%)
  between operations  0.64 us (1%)
    pallas_call x1, Pallas kernels, shards(): pl.pallas_call(functools.partial(pair_kernel, nr, nc), out_shape=(jax.Sha...  46.3 us
    pallas_call x1, Pallas kernels, shards(): pl.pallas_call(functools.partial(finish_kernel, 32.0 / (8 * nr * nc)), ou...  2.18 us

profile of v7, /device:TPU:1, one launch (start us, length us, event | category | flops | bytes accessed | tf_op | source)
XLA Modules:
  0.0 49.1 jit_solution(17316129531781339614)
XLA Ops:
  0.6 46.3 %pair_kernel.1 = (bf16[32,64,256]{2,1,0:T(8,128)(2,1)}, bf16[32,16,128]{2,1,0:T(8,128)(2,1)}, f32[8,512]{1,0:T(8,128)}) custom-call(bf16[8,512]{1,0:T(8,128)(2,1)} %e_hbm.1, bf16[32,512]{1,0:T(8,128)(2,1)} %bitcast.4, bf16[32,512]{1,0:T(8,128)(2,1)} %bitcast.5, bf16[9,32,32]{2,1,0:T(8,128)(2,1)} %w_hbm.1, bf16[32,64,256]{2,1,0:T(8,128)(2,1)} %cot_hbm.1), custom_call_target="tpu_custom_call" | custom-call | tf_op jit(solution)/shard_map/pair_kernel/pallas_call | solution.py:579
  46.9 2.2 %finish.1 = (f32[9,32,32]{2,1,0:T(8,128)}, f32[32,512]{1,0:T(8,128)}, f32[32,512]{1,0:T(8,128)}, f32[8,512]{1,0:T(8,128)}, bf16[32,64,256]{2,1,0:T(8,128)(2,1)}) custom-call(bf16[32,16,128]{2,1,0:T(8,128)(2,1)} %get-tuple-element.13.sums_in, f32[8,512]{1,0:T(8,128)} %get-tuple-element.14.eg_in, bf16[32,64,256]{2,1,0:T(8,128)(2,1)} %get-tuple-element.15.pair_in), custom_call_target="tpu_custom_call" | custom-call | tf_op jit(solution)/shard_map/finish/pallas_call | solution.py:628

commit v8 on v7

--- a/solution.py
+++ b/solution.py
@@ -11,6 +11,7 @@
 OUTSIDE = -1e30
 LOG2E = 1.4426950408889634
 LN2 = 0.6931471805599453
+PIECES = 22
 F32 = jnp.float32
 BF16 = jnp.bfloat16
 VMEM = pl.BlockSpec(memory_space=pltpu.VMEM)
@@ -258,7 +259,8 @@
         self.rb, self.rm = lax.div(r, self.per), lax.rem(r, self.per)
         _, self.quad = self.group(((r, 1, 0), (r, 2, 0)))
         _, self.line = self.group(((c, 1, 1), (c, 2, 1), (c, 4, 1)))
-        self.k1, self.group1 = self.group(((r, 1, 0), (r, 8, 0), (r, 16, 0), (c, 2, 1), (c, 4, 1)))
+        self.plane = ((r, 8, 0), (r, 16, 0), (c, 2, 1), (c, 4, 1), (r, 1, 0))
+        self.k1, self.group1 = self.group(self.plane)
         self.k2, self.group2 = self.group(((r, 2, 0), (r, 4, 0), (c, 1, 1)))
         self.has_up, self.has_down = r > 0, r < nr - 1
         self.has_left, self.has_right = c > 0, c < nc - 1
@@ -279,6 +281,13 @@
                 (a, b + move, n + step) if is_col else (a + move, b, n + step) for a, b, n in members
             ]
         return number, members[:0:-1]
+
+    def plane_member(self, k):
+        a, b = self.r, self.c
+        for at, (x, weight, is_col) in enumerate(self.plane):
+            move = weight * (k >> at & 1) - weight * lax.rem(lax.div(x, weight), 2)
+            a, b = (a, b + move) if is_col else (a + move, b)
+        return a, b
 
     def other(self, k):
         return self.per * self.c + k, self.rb
@@ -347,7 +356,7 @@
     nr, nc, e_hbm, lpt_hbm, rpt_hbm, w_hbm, cot_hbm,
     out_hbm, sums_hbm, eg_hbm,
     rowf, colf, taps, mall, mt, act, a3, z, tf, move, gram, cacc, rsum, cols, col_ends, row_main, row_ends,
-    out_ref, eg_ref, feats, e_ref, w_ref, cot_ref, own, right, packed, quad, proj, es, eb, el, eh, blocks, row_feats, col_feats,
+    out_ref, eg_ref, feats, e_ref, w_ref, cot_ref, own, right, packed, quad, line, proj, es, eb, el, eh, blocks, row_feats, col_feats,
     cparts, cends, rends, turned, gparts, buf, r1, r2, mid, fin, recv, send, loads, stores,
 ):
     ins = ((e_hbm, e_ref), (w_hbm, w_ref), (lpt_hbm, proj.at[0:32]), (rpt_hbm, proj.at[32:64]), (cot_hbm, cot_ref))
@@ -388,8 +397,8 @@
     pl.when(row_after)(lambda: put_line(r + 1, row_feats.at[0], 2))
     pl.when(row_before)(lambda: put_line(r - 1, row_feats.at[1], 3))
     for a, b, _ in p.line:
-        put(es, a, b, eb.at[c], 0)
-    pltpu.make_async_copy(es, eb.at[c], recv.at[0]).start()
+        put(own, a, b, line.at[c], 16)
+    pltpu.make_async_copy(own, line.at[c], recv.at[16]).start()
 
     def put_targets(src, col, dst, sem):
         first, *rest = p.targets(col)
@@ -408,12 +417,6 @@
     pl.when(col_before)(lambda: put_targets(packed, rb - 1, col_feats.at[1], 5))
     input_gradient(mt, tf, z, (5, 9))
 
-    wait_bytes(eb, recv.at[0])
-    e = eb[...].astype(F32)
-    el[...] = e[:, 0:8].reshape(64, 256).astype(BF16)
-    eh[...] = e[:, 8:16].reshape(64, 256).astype(BF16)
-    feats[8:72, :] = dot_nt(el[...], proj[:, 0:256]) + dot_nt(eh[...], proj[:, 256:512])
-
     def arrive(cond, ref, sem):
         pl.when(cond)(lambda: wait_bytes(ref, sem))
         pl.when(jnp.logical_not(cond))(lambda: ref.__setitem__(..., jnp.full(ref.shape, OUTSIDE, F32)))
@@ -422,12 +425,17 @@
     arrive(p.has_down, row_feats.at[1], recv.at[3])
     arrive(p.has_left, col_feats.at[0], recv.at[4])
     arrive(p.has_right, col_feats.at[1], recv.at[5])
+    wait_bytes(line, recv.at[16])
     wait_bytes(blocks, recv.at[15])
+    feats[8:72, :] = line[...].reshape(8 * nc, 128)
     feats[0:8, :] = row_feats[0]
     feats[72:80, :] = row_feats[1]
     feats[80:136, :] = jnp.zeros((56, 128), F32)
     ends = [jnp.concatenate([col_feats[k], jnp.zeros((8, 128), F32)], axis=0).astype(BF16) for k in range(2)]
     features(feats[4:132, :].astype(BF16), blocks[...].reshape(8 * nc, 128).astype(BF16), *ends, rowf, colf)
+    for a, b, _ in p.line:
+        put(es, a, b, eb.at[c], 0)
+    pltpu.make_async_copy(es, eb.at[c], recv.at[0]).start()
     elementwise(rowf, colf, z, act, cacc, rsum)
     sums(cacc, rsum, cols, col_ends, row_main, row_ends)
 
@@ -460,18 +468,24 @@
         spread.append(jnp.where(lane < 32, parts[0], jnp.where(lane < 64, parts[1], 0.0)))
     turned[...] = jnp.concatenate(spread, axis=0)
 
+    wait_bytes(eb, recv.at[0])
+    e = eb[...].astype(F32)
+    el[...] = e[:, 0:8].reshape(64, 256).astype(BF16)
+    eh[...] = e[:, 8:16].reshape(64, 256).astype(BF16)
+
     high, low = halves(turned[...])
     for half, ref in enumerate((el, eh)):
         part = dot_tn(high, ref[...]) + dot_tn(low, ref[...])
-        for k in range(16):
-            at = 4 * (k // 2) + 2 * half + k % 2
-            x = part[8 * (k // 2) : 8 * (k // 2) + 8, 128 * (k % 2) : 128 * (k % 2) + 128]
-            y = taps[8 * at : 8 * at + 8, :] if at < 12 else jnp.zeros((8, 128), F32)
-            buf[at] = jnp.concatenate([x, y], axis=0).astype(BF16)
-
-    for a, b, at in p.group1:
-        put(buf.at[at], a, b, r1.at[k1], 11)
-    pltpu.make_async_copy(buf.at[k1], r1.at[k1], recv.at[11]).start()
+        for k in range(8):
+            at = slice(16 * (k // 2), 16 * (k // 2) + 16), slice(128 * (k % 2), 128 * (k % 2) + 128)
+            buf[4 * (k // 2) + 2 * half + k % 2] = part[at].astype(BF16)
+    for k in range(PIECES - 16):
+        buf[16 + k] = taps[16 * k : 16 * k + 16, :].astype(BF16)
+
+    owner = k1 < PIECES
+    for k in range(PIECES):
+        pl.when(k1 != k)(lambda k=k: put(buf.at[k], *p.plane_member(k), r1.at[k1], 11))
+    pl.when(owner)(lambda: pltpu.make_async_copy(buf.at[k1], r1.at[k1], recv.at[11]).start())
 
     for a, b, _ in p.line:
         put(turned.at[pl.ds(pl.multiple_of(8 * b, 8), 8)], a, b, gparts.at[c], 14)
@@ -485,21 +499,27 @@
     outs[0].start()
     convolve(r, c, 1, a3, tf, out_ref)
     outs[1].start()
-    wait_bytes(r1, recv.at[11])
-    mid[...] = jnp.sum(r1[...].astype(F32), axis=0).astype(BF16)
-    for a, b, _ in p.group2:
-        put(mid, a, b, r2.at[k2], 12)
-    pltpu.make_async_copy(mid, r2.at[k2], recv.at[12]).start()
+
+    @pl.when(owner)
+    def _():
+        wait_bytes(r1, recv.at[11])
+        mid[...] = jnp.sum(r1[...].astype(F32), axis=0).astype(BF16)
+        for a, b, _ in p.group2:
+            put(mid, a, b, r2.at[k2], 12)
+        pltpu.make_async_copy(mid, r2.at[k2], recv.at[12]).start()
 
     convolve(r, c, 2, a3, tf, out_ref)
     outs[2].start()
     convolve(r, c, 3, a3, tf, out_ref)
     outs[3].start()
-    wait_bytes(r2, recv.at[12])
-    fin[...] = jnp.sum(r2[...].astype(F32), axis=0).astype(BF16)
-    for a, b, _ in p.group1:
-        put(fin, a, b, sums_hbm.at[k1], 13)
-    pltpu.make_async_copy(fin, sums_hbm.at[k1], recv.at[13]).start()
+
+    @pl.when(owner)
+    def _():
+        wait_bytes(r2, recv.at[12])
+        fin[...] = jnp.sum(r2[...].astype(F32), axis=0).astype(BF16)
+        for a, b, _ in p.group1:
+            put(fin, a, b, sums_hbm.at[k1], 13)
+        pltpu.make_async_copy(fin, sums_hbm.at[k1], recv.at[13]).start()
 
     wait_bytes(gparts, recv.at[14])
     high, low = halves(jnp.sum(gparts[...], axis=0))
@@ -527,11 +547,13 @@
     pl.when(p.has_down)(lambda: wait_bytes(row_ends.at[1], send.at[8]))
     pl.when(p.has_left)(lambda: wait_bytes(col_ends.at[0], send.at[9]))
     pl.when(p.has_right)(lambda: wait_bytes(col_ends.at[1], send.at[10]))
-    wait_bytes(r1.at[0 : r1.shape[0] - 1], send.at[11])
-    wait_bytes(r2.at[0 : r2.shape[0] - 1], send.at[12])
+    wait_bytes(line.at[0 : nc - 1], send.at[16])
+    pl.when(owner)(lambda: wait_bytes(r1.at[0 : PIECES - 1], send.at[11]))
+    pl.when(jnp.logical_not(owner))(lambda: wait_bytes(r1.at[0:PIECES], send.at[11]))
+    pl.when(owner)(lambda: wait_bytes(r2.at[0 : r2.shape[0] - 1], send.at[12]))
     wait_bytes(gparts.at[0 : nc - 1], send.at[14])
 
-    wait_bytes(r1.at[0 : r1.shape[0] - 1], send.at[13])
+    pl.when(owner)(lambda: wait_bytes(r1.at[0 : r1.shape[0] - 1], send.at[13]))
     wait_bytes(sums_hbm, recv.at[13])
 
 
@@ -554,10 +576,10 @@
     for copy in ins:
         copy.start()
     ins[0].wait()
-    for ref, first, at in ((left_ref, 0, 1), (right_ref, 16, 2)):
-        for k in range(16):
-            x = sums_ref[first + k].astype(F32)[0:8]
-            ref[8 * (k // 4) : 8 * (k // 4) + 8, 128 * (k % 4) : 128 * (k % 4) + 128] = x * scale
+    for ref, first, at in ((left_ref, 0, 1), (right_ref, 8, 2)):
+        for k in range(8):
+            x = sums_ref[first + k].astype(F32)
+            ref[16 * (k // 4) : 16 * (k // 4) + 16, 128 * (k % 4) : 128 * (k % 4) + 128] = x * scale
         outs[at].start()
     ins[1].wait()
     outs[3].start()
@@ -566,9 +588,9 @@
         outs[4 + k].start()
     for k in range(9):
         q, at = divmod(k, 4)
-        for part in range(4):
-            x = sums_ref[4 * q + part].astype(F32)
-            conv_ref[k, 8 * part : 8 * part + 8, :] = x[8:16, 32 * at : 32 * at + 32] * scale
+        for part in range(2):
+            x = sums_ref[16 + 2 * q + part].astype(F32)
+            conv_ref[k, 16 * part : 16 * part + 16, :] = x[:, 32 * at : 32 * at + 32] * scale
     outs[0].start()
     for copy in outs:
         copy.wait()
@@ -580,7 +602,7 @@
         functools.partial(pair_kernel, nr, nc),
         out_shape=(
             jax.ShapeDtypeStruct((32, 64, 256), BF16),
-            jax.ShapeDtypeStruct((32, 16, 128), BF16),
+            jax.ShapeDtypeStruct((PIECES, 16, 128), BF16),
             jax.ShapeDtypeStruct((8, 512), F32),
         ),
         in_specs=[HBM] * 5,
@@ -597,6 +619,7 @@
             pltpu.VMEM((8, 128), F32),
             pltpu.VMEM((8, 128), F32),
             pltpu.VMEM((per, 8, 128), F32),
+            pltpu.VMEM((nc, 8, 128), F32),
             pltpu.VMEM((128, 512), BF16),
             pltpu.VMEM((16, 256), BF16),
             pltpu.VMEM((nc, 16, 256), BF16),
@@ -610,13 +633,13 @@
             pltpu.VMEM((2, 16, 128), F32),
             pltpu.VMEM((64, 128), F32),
             pltpu.VMEM((nc, 8, 128), F32),
-            pltpu.VMEM((32, 16, 128), BF16),
+            pltpu.VMEM((PIECES, 16, 128), BF16),
             pltpu.VMEM((32, 16, 128), BF16),
             pltpu.VMEM((8, 16, 128), BF16),
             pltpu.VMEM((16, 128), BF16),
             pltpu.VMEM((16, 128), BF16),
-            pltpu.SemaphoreType.DMA((16,)),
-            pltpu.SemaphoreType.DMA((16,)),
+            pltpu.SemaphoreType.DMA((17,)),
+            pltpu.SemaphoreType.DMA((17,)),
             pltpu.SemaphoreType.DMA((5,)),
             pltpu.SemaphoreType.DMA((6,)),
         ],
@@ -637,7 +660,7 @@
         in_specs=[HBM] * 3,
         out_specs=(HBM,) * 5,
         scratch_shapes=[
-            pltpu.VMEM((32, 16, 128), BF16),
+            pltpu.VMEM((PIECES, 16, 128), BF16),
             pltpu.VMEM((8, 512), F32),
             pltpu.VMEM((32, 64, 256), BF16),
             pltpu.VMEM((9, 32, 32), F32),

time: 49.2 us -> 49.1 us (level)
  no operation moved by 1% of the time
where the time goes in v8:
time: 49.1 us; the launch traced here: 48.9 us
  Pallas kernels  48.3 us (98%)
  between operations  0.64 us (1%)
    pallas_call x1, Pallas kernels, shards(): pl.pallas_call(functools.partial(pair_kernel, nr, nc), out_shape=(jax.Sha...  46.1 us
    pallas_call x1, Pallas kernels, shards(): pl.pallas_call(functools.partial(finish_kernel, 32.0 / (8 * nr * nc)), ou...  2.16 us

profile of v8, /device:TPU:1, one launch (start us, length us, event | category | flops | bytes accessed | tf_op | source)
XLA Modules:
  0.0 48.9 jit_solution(9746507629969407011)
XLA Ops:
  0.6 46.1 %pair_kernel.1 = (bf16[32,64,256]{2,1,0:T(8,128)(2,1)}, bf16[22,16,128]{2,1,0:T(8,128)(2,1)}, f32[8,512]{1,0:T(8,128)}) custom-call(bf16[8,512]{1,0:T(8,128)(2,1)} %e_hbm.1, bf16[32,512]{1,0:T(8,128)(2,1)} %bitcast.4, bf16[32,512]{1,0:T(8,128)(2,1)} %bitcast.5, bf16[9,32,32]{2,1,0:T(8,128)(2,1)} %w_hbm.1, bf16[32,64,256]{2,1,0:T(8,128)(2,1)} %cot_hbm.1), custom_call_target="tpu_custom_call" | custom-call | tf_op jit(solution)/shard_map/pair_kernel/pallas_call | solution.py:601
  46.8 2.2 %finish.1 = (f32[9,32,32]{2,1,0:T(8,128)}, f32[32,512]{1,0:T(8,128)}, f32[32,512]{1,0:T(8,128)}, f32[8,512]{1,0:T(8,128)}, bf16[32,64,256]{2,1,0:T(8,128)(2,1)}) custom-call(bf16[22,16,128]{2,1,0:T(8,128)(2,1)} %get-tuple-element.13.sums_in, f32[8,512]{1,0:T(8,128)} %get-tuple-element.14.eg_in, bf16[32,64,256]{2,1,0:T(8,128)(2,1)} %get-tuple-element.15.pair_in), custom_call_target="tpu_custom_call" | custom-call | tf_op jit(solution)/shard_map/finish/pallas_call | solution.py:651

commit v9 on v8

--- a/solution.py
+++ b/solution.py
@@ -72,46 +72,51 @@
     widen = one_hot((iota((32, 256), 1) >> 3) == iota((32, 256), 0))
     s0, s1 = iota((256, 256), 0) & 7, iota((256, 256), 1) & 7
     same, above, below = s1 == s0, s1 == s0 + 4, s1 == s0 - 4
+    x = dot(w_ref[...].reshape(288, 32), widen).astype(BF16)
     for b in range(3):
-        x = [dot(spread, dot(w_ref[3 * a + b], widen).astype(BF16)) for a in range(3)]
-        tf[:, 256 * b : 256 * b + 256] = jnp.where(same, x[0], jnp.where(above, x[1], 0.0)).astype(BF16)
-        tf[:, 768 + 256 * b : 1024 + 256 * b] = jnp.where(same, x[2], jnp.where(below, x[1], 0.0)).astype(BF16)
+        x0, x1, x2 = (dot(spread, x[96 * a + 32 * b : 96 * a + 32 * b + 32]) for a in range(3))
+        tf[:, 256 * b : 256 * b + 256] = jnp.where(same, x0, jnp.where(above, x1, 0.0)).astype(BF16)
+        tf[:, 768 + 256 * b : 1024 + 256 * b] = jnp.where(same, x2, jnp.where(below, x1, 0.0)).astype(BF16)
 
 
 def mask_cotangent(r, c, cot_ref, move, mall, mt):
+    mall[0:256, 2048:2304] = jnp.zeros((256, 256), BF16)
+    mall[256:512, 0:256] = jnp.zeros((256, 256), BF16)
     for k in range(4):
         x = cot_ref[:, 16 * k : 16 * k + 16, :].astype(F32)
         row = r * 64 + 16 * k + iota((16, 256), 0)
         x = jnp.where((c * 256 + iota((16, 256), 1) >= row)[None], x, 0.0)
         for half in range(2):
-            mall[:, lanes(2 * k + half)] = x[:, 8 * half : 8 * half + 8].reshape(256, 256).astype(BF16)
-    for b in range(3):
+            m = x[:, 8 * half : 8 * half + 8].reshape(256, 256).astype(BF16)
+            mall[0:256, lanes(2 * k + half)] = m
+            mall[256:512, lanes(2 * k + half + 1)] = m
+    for b in range(2):
         move[272 * b : 272 * b + 272, :] = one_hot(iota((272, 256), 0) - 4 * b == iota((272, 256), 1))
-        mt[0, :, 256 * b : 256 * b + 256] = jnp.zeros((272, 256), BF16)
-        mt[9, :, 256 * b : 256 * b + 256] = jnp.zeros((272, 256), BF16)
+    mt[0] = jnp.zeros((272, 768), BF16)
+    mt[9] = jnp.zeros((272, 768), BF16)
+    none = jnp.zeros((8, 256), F32)
 
     def body(g):
-        moved = dot_nt(move[...], mall[:, lanes(g)]).astype(BF16)
-        for b in range(3):
-            mt[g + 1, :, 256 * b : 256 * b + 256] = moved[272 * b : 272 * b + 272]
+        moved = dot_nt(move[...], mall[0:256, lanes(g)])
+        mt[g + 1, :, 0:256] = moved[0:272].astype(BF16)
+        mt[g + 1, :, 256:512] = moved[272:544].astype(BF16)
+        mt[g + 1, :, 512:768] = jnp.concatenate([none, moved[0:264]], axis=0).astype(BF16)
 
     loop(8, body)
 
 
-def input_gradient(mt, tf, z, groups):
-    def body(h, _):
-        z[h] = group_gradient(mt, tf, h)
+def input_gradient(mt, tf, z, steps):
+    def body(step, _):
+        left = [jnp.concatenate([mt[3 * step + k], mt[3 * step + k + 1]], axis=1) for k in range(3)]
+        right = jnp.concatenate(
+            [tf[:, 768 * (1 - u) + 256 * b : 768 * (1 - u) + 256 * b + 256] for u in range(2) for b in range(3)], axis=0
+        )
+        x = dot(jnp.concatenate(left, axis=0), right)
+        for k in range(3):
+            z[3 * step + k] = x[272 * k : 272 * k + 272]
         return 0
 
-    lax.fori_loop(*groups, body, 0)
-
-
-def group_gradient(mt, tf, h):
-    left = jnp.concatenate([mt[h], mt[h + 1]], axis=1)
-    right = jnp.concatenate(
-        [tf[:, 768 * (1 - u) + 256 * b : 768 * (1 - u) + 256 * b + 256] for u in range(2) for b in range(3)], axis=0
-    )
-    return dot(left, right)
+    lax.fori_loop(*steps, body, 0)
 
 
 def features(rows, blocks, before, after, rowf, colf):
@@ -202,10 +207,10 @@
 
 
 def tap_gradient(mall, a3, gram, taps):
+    x = dot(mall[...], a3[...])
     for u in range(2):
-        x = dot(mall[...], a3[256 * u : 256 * u + 2048, :])
         for k in range(6):
-            gram[6 * u + k] = x[:, 128 * k : 128 * k + 128]
+            gram[6 * u + k] = x[256 * u : 256 * u + 256, 128 * k : 128 * k + 128]
     lane = iota((32, 128), 1)
 
     def along(b, k, sources):
@@ -234,13 +239,13 @@
     pltpu.VMEM((16, 256), F32),
     pltpu.VMEM((272, 256), F32),
     pltpu.VMEM((96, 128), F32),
-    pltpu.VMEM((256, 2048), BF16),
+    pltpu.VMEM((512, 2304), BF16),
     pltpu.VMEM((10, 272, 768), BF16),
     pltpu.VMEM((9, 272, 256), F32),
     pltpu.VMEM((2304, 768), BF16),
     pltpu.VMEM((9, 272, 256), F32),
     pltpu.VMEM((256, 1536), BF16),
-    pltpu.VMEM((816, 256), BF16),
+    pltpu.VMEM((544, 256), BF16),
     pltpu.VMEM((12, 256, 128), F32),
     pltpu.VMEM((272, 256), F32),
     pltpu.VMEM((72, 256), F32),
@@ -259,7 +264,7 @@
         self.rb, self.rm = lax.div(r, self.per), lax.rem(r, self.per)
         _, self.quad = self.group(((r, 1, 0), (r, 2, 0)))
         _, self.line = self.group(((c, 1, 1), (c, 2, 1), (c, 4, 1)))
-        self.plane = ((r, 8, 0), (r, 16, 0), (c, 2, 1), (c, 4, 1), (r, 1, 0))
+        self.plane = ((r, 1, 0), (r, 8, 0), (c, 2, 1), (r, 16, 0), (c, 4, 1))
         self.k1, self.group1 = self.group(self.plane)
         self.k2, self.group2 = self.group(((r, 2, 0), (r, 4, 0), (c, 1, 1)))
         self.has_up, self.has_down = r > 0, r < nr - 1
@@ -325,9 +330,20 @@
         pl.when(self.has_down)(lambda: signal(r + 1, c))
         pl.when(self.ends_block)(lambda: signal_all(rb + 1))
         pl.when(self.starts_block)(lambda: signal_all(rb - 1))
-        for a, b, _ in self.group1 + self.group2:
-            signal(a, b)
-        n = len(self.quad + self.line + self.group1 + self.group2) + nc + per
+        owner = self.k1 < PIECES
+
+        @pl.when(owner)
+        def _():
+            for a, b, _ in self.group1 + self.group2:
+                signal(a, b)
+
+        @pl.when(jnp.logical_not(owner))
+        def _():
+            for k in range(PIECES):
+                signal(*self.plane_member(k))
+
+        n = len(self.quad + self.line) + nc + per
+        n = n + jnp.where(owner, len(self.group1 + self.group2), PIECES)
         up, down = self.has_up, self.has_down
         for cond, m in (
             (self.in_others, -2), (is_last & down, nc), (is_first & up, nc),
@@ -409,13 +425,13 @@
             put(src, a, b, dst, sem)
 
     col_after, col_before = is_last & (rb < nc - 1), is_first & (rb > 0)
-    input_gradient(mt, tf, z, (0, 5))
+    input_gradient(mt, tf, z, (0, 1))
     wait_bytes(quad, recv.at[1])
     packed[...] = jnp.sum(quad[...], axis=0)
     put_targets(packed, rb, blocks.at[c], 15)
     pl.when(col_after)(lambda: put_targets(packed, rb + 1, col_feats.at[0], 4))
     pl.when(col_before)(lambda: put_targets(packed, rb - 1, col_feats.at[1], 5))
-    input_gradient(mt, tf, z, (5, 9))
+    input_gradient(mt, tf, z, (1, 3))
 
     def arrive(cond, ref, sem):
         pl.when(cond)(lambda: wait_bytes(ref, sem))

time: 49.1 us -> 48.5 us (0.988)
  Pallas kernels: 48.3 us -> 47.7 us
    pallas_call x1, Pallas kernels: 46.1 us -> 45.6 us  [shards(): pl.pallas_call(functools.partial(pair_kernel, nr, nc), out_shape=(jax.Sha...]
where the time goes in v9:
time: 48.5 us; the launch traced here: 48.4 us
  Pallas kernels  47.7 us (98%)
  between operations  0.64 us (1%)
    pallas_call x1, Pallas kernels, shards(): pl.pallas_call(functools.partial(pair_kernel, nr, nc), out_shape=(jax.Sha...  45.6 us
    pallas_call x1, Pallas kernels, shards(): pl.pallas_call(functools.partial(finish_kernel, 32.0 / (8 * nr * nc)), ou...  2.16 us

profile of v9, /device:TPU:1, one launch (start us, length us, event | category | flops | bytes accessed | tf_op | source)
XLA Modules:
  0.0 48.4 jit_solution(2152936111842888204)
XLA Ops:
  0.6 45.6 %pair_kernel.1 = (bf16[32,64,256]{2,1,0:T(8,128)(2,1)}, bf16[22,16,128]{2,1,0:T(8,128)(2,1)}, f32[8,512]{1,0:T(8,128)}) custom-call(bf16[8,512]{1,0:T(8,128)(2,1)} %e_hbm.1, bf16[32,512]{1,0:T(8,128)(2,1)} %bitcast.4, bf16[32,512]{1,0:T(8,128)(2,1)} %bitcast.5, bf16[9,32,32]{2,1,0:T(8,128)(2,1)} %w_hbm.1, bf16[32,64,256]{2,1,0:T(8,128)(2,1)} %cot_hbm.1), custom_call_target="tpu_custom_call" | custom-call | tf_op jit(solution)/shard_map/pair_kernel/pallas_call | solution.py:617
  46.2 2.2 %finish.1 = (f32[9,32,32]{2,1,0:T(8,128)}, f32[32,512]{1,0:T(8,128)}, f32[32,512]{1,0:T(8,128)}, f32[8,512]{1,0:T(8,128)}, bf16[32,64,256]{2,1,0:T(8,128)(2,1)}) custom-call(bf16[22,16,128]{2,1,0:T(8,128)(2,1)} %get-tuple-element.13.sums_in, f32[8,512]{1,0:T(8,128)} %get-tuple-element.14.eg_in, bf16[32,64,256]{2,1,0:T(8,128)(2,1)} %get-tuple-element.15.pair_in), custom_call_target="tpu_custom_call" | custom-call | tf_op jit(solution)/shard_map/finish/pallas_call | solution.py:667

commit v10 on v9

--- a/solution.py
+++ b/solution.py
@@ -119,9 +119,8 @@
     lax.fori_loop(*steps, body, 0)
 
 
-def features(rows, blocks, before, after, rowf, colf):
-    k, n = iota((128, 256), 0), iota((128, 256), 1) >> 3
-    picks = [one_hot(k == n + 32 * at) for at in range(4)]
+def features(rows, blocks, before, after, onto, rowf, colf):
+    picks = [onto[:, 256 * at : 256 * at + 256] for at in range(4)]
     first = dot(before, picks[3])
     last = dot(after, picks[0])
     x = [first[4:8]] + [dot(blocks, pick) for pick in picks] + [last[0:4], jnp.zeros((8, 256), F32)]
@@ -153,37 +152,47 @@
     loop(11, body)
 
 
-def sums(cacc, rsum, cols, col_ends, row_main, row_ends):
+def build_constants(onto, pick, by_group):
+    k, n = iota((128, 256), 0), iota((128, 256), 1) >> 3
+    for at in range(4):
+        onto[:, 256 * at : 256 * at + 256] = one_hot(k == n + 32 * at)
     k, n = iota((256, 128), 0) >> 3, iota((256, 128), 1)
-    picks = [one_hot(k + 32 * g == n) for g in range(4)]
-    pick = jnp.concatenate(picks, axis=0)
+    for g in range(4):
+        pick[256 * g : 256 * g + 256, :] = one_hot(k + 32 * g == n)
+    by_group[...] = one_hot((iota((80, 128), 0) >> 3) == (iota((80, 128), 1) >> 3))
+
+
+def ends_of(x, pick, ends):
+    sub = iota((16, 128), 0)
+    high, low = halves(x)
+    first = dot(high, pick[768:1024]) + dot(low, pick[768:1024])
+    second = dot(high, pick[0:256]) + dot(low, pick[0:256])
+    ends[0] = jnp.where(sub >= 12, pltpu.roll(first, 12, 0), 0.0)
+    ends[1] = jnp.where(sub < 4, pltpu.roll(second, 4, 0), 0.0)
+
+
+def column_sums(cacc, pick, cols):
     x = [
         jnp.concatenate([cacc[4 + 64 * q + 16 * g : 20 + 64 * q + 16 * g, :] for g in range(4)], axis=1) for q in range(4)
     ]
     high, low = halves(jnp.concatenate(x, axis=0))
-    x = dot(high, pick) + dot(low, pick)
+    x = dot(high, pick[...]) + dot(low, pick[...])
     for q in range(4):
         cols[q] = x[16 * q : 16 * q + 16]
-    sub, lane = iota((16, 128), 0), iota((16, 128), 1)
-    ends = jnp.concatenate([cacc[0:8, :], cacc[256:264, :]], axis=0)
-    high, low = halves(ends)
-    first = dot(high, picks[3]) + dot(low, picks[3])
-    second = dot(high, picks[0]) + dot(low, picks[0])
-    col_ends[0] = jnp.where(sub >= 12, pltpu.roll(first, 12, 0), 0.0)
-    col_ends[1] = jnp.where(sub < 4, pltpu.roll(second, 4, 0), 0.0)
+
+
+def column_end_sums(cacc, pick, col_ends):
+    ends_of(jnp.concatenate([cacc[0:8, :], cacc[256:264, :]], axis=0), pick, col_ends)
+
+
+def row_sums(rsum, pick, by_group, row_main, row_ends):
     x = jnp.concatenate([rsum[...], jnp.zeros((56, 256), F32)], axis=0)
-    by_group = one_hot((iota((80, 128), 0) >> 3) == (iota((80, 128), 1) >> 3))
     high, low = halves(x)
-    x = dot(by_group, high) + dot(by_group, low)
+    x = dot(by_group[...], high) + dot(by_group[...], low)
     x = jnp.where((iota((80, 256), 0) & 7) == (iota((80, 256), 1) & 7), x, 0.0)
+    ends_of(jnp.concatenate([x[0:8], x[64:72]], axis=0), pick, row_ends)
     high, low = halves(jnp.concatenate([x[4 + 16 * g : 20 + 16 * g] for g in range(4)], axis=1))
-    row_main[...] = dot(high, pick) + dot(low, pick)
-    ends = jnp.concatenate([x[0:8], x[64:72]], axis=0)
-    high, low = halves(ends)
-    first = dot(high, picks[3]) + dot(low, picks[3])
-    second = dot(high, picks[0]) + dot(low, picks[0])
-    row_ends[0] = jnp.where(sub >= 12, pltpu.roll(first, 12, 0), 0.0)
-    row_ends[1] = jnp.where(sub < 4, pltpu.roll(second, 4, 0), 0.0)
+    row_main[...] = dot(high, pick[...]) + dot(low, pick[...])
 
 
 def build_windows(act, a3):
@@ -206,7 +215,7 @@
     out_ref[:, 16 * k : 16 * k + 16, :] = jnp.where((col >= row)[None], y, 0.0).astype(BF16)
 
 
-def tap_gradient(mall, a3, gram, taps):
+def tap_gradient(mall, a3, pick, gram, taps):
     x = dot(mall[...], a3[...])
     for u in range(2):
         for k in range(6):
@@ -225,7 +234,7 @@
         [(s, 1) for s in range(8)],
     )
     x = [jnp.concatenate([along(b, k, sources[a]) for k in range(2)], axis=1) for a in range(3) for b in range(3)]
-    y = dot(jnp.concatenate(halves(jnp.concatenate(x, axis=0)), axis=0), one_hot((iota((256, 128), 0) >> 3) == iota((256, 128), 1)))
+    y = dot(jnp.concatenate(halves(jnp.concatenate(x, axis=0)), axis=0), pick[0:256])
     y = y[0:288] + y[288:576]
     for q in range(3):
         total = jnp.zeros((32, 128), F32)
@@ -246,6 +255,9 @@
     pltpu.VMEM((9, 272, 256), F32),
     pltpu.VMEM((256, 1536), BF16),
     pltpu.VMEM((544, 256), BF16),
+    pltpu.VMEM((128, 1024), BF16),
+    pltpu.VMEM((1024, 128), BF16),
+    pltpu.VMEM((80, 128), BF16),
     pltpu.VMEM((12, 256, 128), F32),
     pltpu.VMEM((272, 256), F32),
     pltpu.VMEM((72, 256), F32),
@@ -371,7 +383,7 @@
 def pair_kernel(
     nr, nc, e_hbm, lpt_hbm, rpt_hbm, w_hbm, cot_hbm,
     out_hbm, sums_hbm, eg_hbm,
-    rowf, colf, taps, mall, mt, act, a3, z, tf, move, gram, cacc, rsum, cols, col_ends, row_main, row_ends,
+    rowf, colf, taps, mall, mt, act, a3, z, tf, move, onto, pick, by_group, gram, cacc, rsum, cols, col_ends, row_main, row_ends,
     out_ref, eg_ref, feats, e_ref, w_ref, cot_ref, own, right, packed, quad, line, proj, es, eb, el, eh, blocks, row_feats, col_feats,
     cparts, cends, rends, turned, gparts, buf, r1, r2, mid, fin, recv, send, loads, stores,
 ):
@@ -432,6 +444,7 @@
     pl.when(col_after)(lambda: put_targets(packed, rb + 1, col_feats.at[0], 4))
     pl.when(col_before)(lambda: put_targets(packed, rb - 1, col_feats.at[1], 5))
     input_gradient(mt, tf, z, (1, 3))
+    build_constants(onto, pick, by_group)
 
     def arrive(cond, ref, sem):
         pl.when(cond)(lambda: wait_bytes(ref, sem))
@@ -448,22 +461,36 @@
     feats[72:80, :] = row_feats[1]
     feats[80:136, :] = jnp.zeros((56, 128), F32)
     ends = [jnp.concatenate([col_feats[k], jnp.zeros((8, 128), F32)], axis=0).astype(BF16) for k in range(2)]
-    features(feats[4:132, :].astype(BF16), blocks[...].reshape(8 * nc, 128).astype(BF16), *ends, rowf, colf)
+    features(feats[4:132, :].astype(BF16), blocks[...].reshape(8 * nc, 128).astype(BF16), *ends, onto, rowf, colf)
     for a, b, _ in p.line:
         put(es, a, b, eb.at[c], 0)
     pltpu.make_async_copy(es, eb.at[c], recv.at[0]).start()
     elementwise(rowf, colf, z, act, cacc, rsum)
-    sums(cacc, rsum, cols, col_ends, row_main, row_ends)
-
+
+    column_sums(cacc, pick, cols)
     for k in range(per):
         put_other(cols.at[k], k, cparts.at[rm], 6)
+    column_end_sums(cacc, pick, col_ends)
+    pl.when(p.has_left)(lambda: put(col_ends.at[0], per * c - 1, rb, cends.at[0, rm], 9))
+    pl.when(p.has_right)(lambda: put(col_ends.at[1], per * c + per, rb, cends.at[1, rm], 10))
+    row_sums(rsum, pick, by_group, row_main, row_ends)
     pl.when(p.has_up)(lambda: put(row_ends.at[0], r - 1, c, rends.at[0], 7))
     pl.when(p.has_down)(lambda: put(row_ends.at[1], r + 1, c, rends.at[1], 8))
-    pl.when(p.has_left)(lambda: put(col_ends.at[0], per * c - 1, rb, cends.at[0, rm], 9))
-    pl.when(p.has_right)(lambda: put(col_ends.at[1], per * c + per, rb, cends.at[1, rm], 10))
 
     build_windows(act, a3)
-    tap_gradient(mall, a3, gram, taps)
+    tap_gradient(mall, a3, pick, gram, taps)
+    for k in range(PIECES - 16):
+        buf[16 + k] = taps[16 * k : 16 * k + 16, :].astype(BF16)
+
+    def put_piece(k):
+        pl.when(k1 != k)(lambda: put(buf.at[k], *p.plane_member(k), r1.at[k1], 11))
+
+    for k in range(16, PIECES):
+        put_piece(k)
+    wait_bytes(eb, recv.at[0])
+    e = eb[...].astype(F32)
+    el[...] = e[:, 0:8].reshape(64, 256).astype(BF16)
+    eh[...] = e[:, 8:16].reshape(64, 256).astype(BF16)
     def gather_sum(cond, ref, sem):
         pl.when(cond)(lambda: wait_bytes(ref, sem))
         pl.when(jnp.logical_not(cond))(lambda: ref.__setitem__(..., jnp.zeros(ref.shape, F32)))
@@ -484,23 +511,16 @@
         spread.append(jnp.where(lane < 32, parts[0], jnp.where(lane < 64, parts[1], 0.0)))
     turned[...] = jnp.concatenate(spread, axis=0)
 
-    wait_bytes(eb, recv.at[0])
-    e = eb[...].astype(F32)
-    el[...] = e[:, 0:8].reshape(64, 256).astype(BF16)
-    eh[...] = e[:, 8:16].reshape(64, 256).astype(BF16)
-
     high, low = halves(turned[...])
     for half, ref in enumerate((el, eh)):
         part = dot_tn(high, ref[...]) + dot_tn(low, ref[...])
         for k in range(8):
             at = slice(16 * (k // 2), 16 * (k // 2) + 16), slice(128 * (k % 2), 128 * (k % 2) + 128)
             buf[4 * (k // 2) + 2 * half + k % 2] = part[at].astype(BF16)
-    for k in range(PIECES - 16):
-        buf[16 + k] = taps[16 * k : 16 * k + 16, :].astype(BF16)
 
     owner = k1 < PIECES
-    for k in range(PIECES):
-        pl.when(k1 != k)(lambda k=k: put(buf.at[k], *p.plane_member(k), r1.at[k1], 11))
+    for k in range(16):
+        put_piece(k)
     pl.when(owner)(lambda: pltpu.make_async_copy(buf.at[k1], r1.at[k1], recv.at[11]).start())
 
     for a, b, _ in p.line:

time: 48.5 us -> 47.6 us (0.981)
  Pallas kernels: 47.7 us -> 46.8 us
    pallas_call x1, Pallas kernels: 45.6 us -> 44.7 us  [shards(): pl.pallas_call(functools.partial(pair_kernel, nr, nc), out_shape=(jax.Sha...]
where the time goes in v10:
time: 47.6 us; the launch traced here: 47.5 us
  Pallas kernels  46.8 us (98%)
  between operations  0.64 us (1%)
    pallas_call x1, Pallas kernels, shards(): pl.pallas_call(functools.partial(pair_kernel, nr, nc), out_shape=(jax.Sha...  44.7 us
    pallas_call x1, Pallas kernels, shards(): pl.pallas_call(functools.partial(finish_kernel, 32.0 / (8 * nr * nc)), ou...  2.16 us

profile of v10, /device:TPU:1, one launch (start us, length us, event | category | flops | bytes accessed | tf_op | source)
XLA Modules:
  0.0 47.5 jit_solution(10153235293198721083)
XLA Ops:
  0.6 44.7 %pair_kernel.1 = (bf16[32,64,256]{2,1,0:T(8,128)(2,1)}, bf16[22,16,128]{2,1,0:T(8,128)(2,1)}, f32[8,512]{1,0:T(8,128)}) custom-call(bf16[8,512]{1,0:T(8,128)(2,1)} %e_hbm.1, bf16[32,512]{1,0:T(8,128)(2,1)} %bitcast.4, bf16[32,512]{1,0:T(8,128)(2,1)} %bitcast.5, bf16[9,32,32]{2,1,0:T(8,128)(2,1)} %w_hbm.1, bf16[32,64,256]{2,1,0:T(8,128)(2,1)} %cot_hbm.1), custom_call_target="tpu_custom_call" | custom-call | tf_op jit(solution)/shard_map/pair_kernel/pallas_call | solution.py:637
  45.3 2.2 %finish.1 = (f32[9,32,32]{2,1,0:T(8,128)}, f32[32,512]{1,0:T(8,128)}, f32[32,512]{1,0:T(8,128)}, f32[8,512]{1,0:T(8,128)}, bf16[32,64,256]{2,1,0:T(8,128)(2,1)}) custom-call(bf16[22,16,128]{2,1,0:T(8,128)(2,1)} %get-tuple-element.13.sums_in, f32[8,512]{1,0:T(8,128)} %get-tuple-element.14.eg_in, bf16[32,64,256]{2,1,0:T(8,128)(2,1)} %get-tuple-element.15.pair_in), custom_call_target="tpu_custom_call" | custom-call | tf_op jit(solution)/shard_map/finish/pallas_call | solution.py:687

commit v11 on v10

--- a/solution.py
+++ b/solution.py
@@ -64,7 +64,7 @@
     u = 1.0 + t
     inv = pltpu.reciprocal(u, full_range=False)
     log = jnp.where(t < 2.0**-11, t * LOG2E, jnp.log2(u))
-    return LN2 * (jnp.maximum(y, 0.0) + log), jnp.where(y >= 0, inv, t * inv)
+    return jnp.maximum(y, 0.0) + log, jnp.where(y >= 0, inv, t * inv)
 
 
 def build_taps(w_ref, tf):
@@ -199,7 +199,7 @@
     def body(h):
         at = pl.ds(pl.multiple_of(256 * h, 256), 256)
         for b in range(3):
-            a3[at, 256 * b : 256 * b + 256] = act[h, 4 * b : 4 * b + 256, :].astype(BF16)
+            a3[at, 256 * b : 256 * b + 256] = (act[h, 4 * b : 4 * b + 256, :] * LN2).astype(BF16)
 
     loop(9, body)
 
@@ -278,7 +278,8 @@
         _, self.line = self.group(((c, 1, 1), (c, 2, 1), (c, 4, 1)))
         self.plane = ((r, 1, 0), (r, 8, 0), (c, 2, 1), (r, 16, 0), (c, 4, 1))
         self.k1, self.group1 = self.group(self.plane)
-        self.k2, self.group2 = self.group(((r, 2, 0), (r, 4, 0), (c, 1, 1)))
+        self.z_line = ((r, 2, 0), (r, 4, 0), (c, 1, 1))
+        self.k2, self.group2 = self.group(self.z_line)
         self.has_up, self.has_down = r > 0, r < nr - 1
         self.has_left, self.has_right = c > 0, c < nc - 1
         self.ends_block = (self.rm == self.per - 1) & (self.rb < nc - 1)
@@ -299,9 +300,9 @@
             ]
         return number, members[:0:-1]
 
-    def plane_member(self, k):
+    def member(self, bits, k):
         a, b = self.r, self.c
-        for at, (x, weight, is_col) in enumerate(self.plane):
+        for at, (x, weight, is_col) in enumerate(bits):
             move = weight * (k >> at & 1) - weight * lax.rem(lax.div(x, weight), 2)
             a, b = (a, b + move) if is_col else (a + move, b)
         return a, b
@@ -352,7 +353,7 @@
         @pl.when(jnp.logical_not(owner))
         def _():
             for k in range(PIECES):
-                signal(*self.plane_member(k))
+                signal(*self.member(self.plane, k))
 
         n = len(self.quad + self.line) + nc + per
         n = n + jnp.where(owner, len(self.group1 + self.group2), PIECES)
@@ -483,7 +484,7 @@
         buf[16 + k] = taps[16 * k : 16 * k + 16, :].astype(BF16)
 
     def put_piece(k):
-        pl.when(k1 != k)(lambda: put(buf.at[k], *p.plane_member(k), r1.at[k1], 11))
+        pl.when(k1 != k)(lambda: put(buf.at[k], *p.member(p.plane, k), r1.at[k1], 11))
 
     for k in range(16, PIECES):
         put_piece(k)
@@ -540,8 +541,8 @@
     def _():
         wait_bytes(r1, recv.at[11])
         mid[...] = jnp.sum(r1[...].astype(F32), axis=0).astype(BF16)
-        for a, b, _ in p.group2:
-            put(mid, a, b, r2.at[k2], 12)
+        for k in range(8):
+            pl.when(k2 != k)(lambda k=k: put(mid, *p.member(p.z_line, k), r2.at[k2], 12))
         pltpu.make_async_copy(mid, r2.at[k2], recv.at[12]).start()
 
     convolve(r, c, 2, a3, tf, out_ref)
@@ -553,8 +554,8 @@
     def _():
         wait_bytes(r2, recv.at[12])
         fin[...] = jnp.sum(r2[...].astype(F32), axis=0).astype(BF16)
-        for a, b, _ in p.group1:
-            put(fin, a, b, sums_hbm.at[k1], 13)
+        for k in (1, 0, *range(2, 32)):
+            pl.when(k1 != k)(lambda k=k: put(fin, *p.member(p.plane, k), sums_hbm.at[k1], 13))
         pltpu.make_async_copy(fin, sums_hbm.at[k1], recv.at[13]).start()
 
     wait_bytes(gparts, recv.at[14])

time: 47.6 us -> 47 us (0.987)
  Pallas kernels: 46.8 us -> 46.3 us
    pallas_call x1, Pallas kernels: 44.7 us -> 44.1 us  [shards(): pl.pallas_call(functools.partial(pair_kernel, nr, nc), out_shape=(jax.Sha...]
where the time goes in v11:
time: 47 us; the launch traced here: 46.9 us
  Pallas kernels  46.3 us (99%)
  between operations  0.64 us (1%)
    pallas_call x1, Pallas kernels, shards(): pl.pallas_call(functools.partial(pair_kernel, nr, nc), out_shape=(jax.Sha...  44.1 us
    pallas_call x1, Pallas kernels, shards(): pl.pallas_call(functools.partial(finish_kernel, 32.0 / (8 * nr * nc)), ou...  2.16 us

profile of v11, /device:TPU:1, one launch (start us, length us, event | category | flops | bytes accessed | tf_op | source)
XLA Modules:
  0.0 46.9 jit_solution(6763836195711696526)
XLA Ops:
  0.6 44.1 %pair_kernel.1 = (bf16[32,64,256]{2,1,0:T(8,128)(2,1)}, bf16[22,16,128]{2,1,0:T(8,128)(2,1)}, f32[8,512]{1,0:T(8,128)}) custom-call(bf16[8,512]{1,0:T(8,128)(2,1)} %e_hbm.1, bf16[32,512]{1,0:T(8,128)(2,1)} %bitcast.4, bf16[32,512]{1,0:T(8,128)(2,1)} %bitcast.5, bf16[9,32,32]{2,1,0:T(8,128)(2,1)} %w_hbm.1, bf16[32,64,256]{2,1,0:T(8,128)(2,1)} %cot_hbm.1), custom_call_target="tpu_custom_call" | custom-call | tf_op jit(solution)/shard_map/pair_kernel/pallas_call | solution.py:638
  44.8 2.2 %finish.1 = (f32[9,32,32]{2,1,0:T(8,128)}, f32[32,512]{1,0:T(8,128)}, f32[32,512]{1,0:T(8,128)}, f32[8,512]{1,0:T(8,128)}, bf16[32,64,256]{2,1,0:T(8,128)(2,1)}) custom-call(bf16[22,16,128]{2,1,0:T(8,128)(2,1)} %get-tuple-element.13.sums_in, f32[8,512]{1,0:T(8,128)} %get-tuple-element.14.eg_in, bf16[32,64,256]{2,1,0:T(8,128)(2,1)} %get-tuple-element.15.pair_in), custom_call_target="tpu_custom_call" | custom-call | tf_op jit(solution)/shard_map/finish/pallas_call | solution.py:688

commit v12 on v11

--- a/solution.py
+++ b/solution.py
@@ -167,8 +167,8 @@
     high, low = halves(x)
     first = dot(high, pick[768:1024]) + dot(low, pick[768:1024])
     second = dot(high, pick[0:256]) + dot(low, pick[0:256])
-    ends[0] = jnp.where(sub >= 12, pltpu.roll(first, 12, 0), 0.0)
-    ends[1] = jnp.where(sub < 4, pltpu.roll(second, 4, 0), 0.0)
+    ends[0] = jnp.where(sub >= 12, pltpu.roll(first, 12, 0), 0.0)[8:16]
+    ends[1] = jnp.where(sub < 4, pltpu.roll(second, 4, 0), 0.0)[0:8]
 
 
 def column_sums(cacc, pick, cols):
@@ -262,9 +262,9 @@
     pltpu.VMEM((272, 256), F32),
     pltpu.VMEM((72, 256), F32),
     pltpu.VMEM((4, 16, 128), F32),
-    pltpu.VMEM((2, 16, 128), F32),
+    pltpu.VMEM((2, 8, 128), F32),
     pltpu.VMEM((16, 128), F32),
-    pltpu.VMEM((2, 16, 128), F32),
+    pltpu.VMEM((2, 8, 128), F32),
 ]
 
 
@@ -385,7 +385,7 @@
     nr, nc, e_hbm, lpt_hbm, rpt_hbm, w_hbm, cot_hbm,
     out_hbm, sums_hbm, eg_hbm,
     rowf, colf, taps, mall, mt, act, a3, z, tf, move, onto, pick, by_group, gram, cacc, rsum, cols, col_ends, row_main, row_ends,
-    out_ref, eg_ref, feats, e_ref, w_ref, cot_ref, own, right, packed, quad, line, proj, es, eb, el, eh, blocks, row_feats, col_feats,
+    out_ref, eg_ref, feats, e_ref, w_ref, cot_ref, own, right, packed, quad, line, proj, es, eb, twice, blocks, row_feats, col_feats,
     cparts, cends, rends, turned, gparts, buf, r1, r2, mid, fin, recv, send, loads, stores,
 ):
     ins = ((e_hbm, e_ref), (w_hbm, w_ref), (lpt_hbm, proj.at[0:32]), (rpt_hbm, proj.at[32:64]), (cot_hbm, cot_ref))
@@ -490,8 +490,9 @@
         put_piece(k)
     wait_bytes(eb, recv.at[0])
     e = eb[...].astype(F32)
-    el[...] = e[:, 0:8].reshape(64, 256).astype(BF16)
-    eh[...] = e[:, 8:16].reshape(64, 256).astype(BF16)
+    e = jnp.concatenate([e[:, 0:8].reshape(64, 256), e[:, 8:16].reshape(64, 256)], axis=1).astype(BF16)
+    twice[...] = jnp.concatenate([e, e], axis=0)
+
     def gather_sum(cond, ref, sem):
         pl.when(cond)(lambda: wait_bytes(ref, sem))
         pl.when(jnp.logical_not(cond))(lambda: ref.__setitem__(..., jnp.zeros(ref.shape, F32)))
@@ -502,8 +503,9 @@
     gather_sum(p.starts_block, cends.at[1], recv.at[10])
     wait_bytes(cparts, recv.at[6])
     grads = (
-        row_main[...] + rends[0] + rends[1],
-        jnp.sum(cparts[...], axis=0) + jnp.sum(cends[0], axis=0) + jnp.sum(cends[1], axis=0),
+        row_main[...] + jnp.concatenate([rends[1], rends[0]], axis=0),
+        jnp.sum(cparts[...], axis=0)
+        + jnp.concatenate([jnp.sum(cends[1], axis=0), jnp.sum(cends[0], axis=0)], axis=0),
     )
     lane = iota((16, 128), 1)
     spread = []
@@ -512,21 +514,15 @@
         spread.append(jnp.where(lane < 32, parts[0], jnp.where(lane < 64, parts[1], 0.0)))
     turned[...] = jnp.concatenate(spread, axis=0)
 
-    high, low = halves(turned[...])
-    for half, ref in enumerate((el, eh)):
-        part = dot_tn(high, ref[...]) + dot_tn(low, ref[...])
-        for k in range(8):
-            at = slice(16 * (k // 2), 16 * (k // 2) + 16), slice(128 * (k % 2), 128 * (k % 2) + 128)
-            buf[4 * (k // 2) + 2 * half + k % 2] = part[at].astype(BF16)
+    part = dot_tn(jnp.concatenate(halves(turned[...]), axis=0), twice[...])
+    for k in range(16):
+        at = slice(16 * (k // 4), 16 * (k // 4) + 16), slice(128 * (k % 4), 128 * (k % 4) + 128)
+        buf[k] = part[at].astype(BF16)
 
     owner = k1 < PIECES
     for k in range(16):
         put_piece(k)
     pl.when(owner)(lambda: pltpu.make_async_copy(buf.at[k1], r1.at[k1], recv.at[11]).start())
-
-    for a, b, _ in p.line:
-        put(turned.at[pl.ds(pl.multiple_of(8 * b, 8), 8)], a, b, gparts.at[c], 14)
-    pltpu.make_async_copy(turned.at[pl.ds(pl.multiple_of(8 * c, 8), 8)], gparts.at[c], recv.at[14]).start()
 
     outs = [
         pltpu.make_async_copy(out_ref.at[:, 16 * q : 16 * q + 16, :], out_hbm.at[:, 16 * q : 16 * q + 16, :], stores.at[q])
@@ -534,6 +530,9 @@
     ]
     convolve(r, c, 0, a3, tf, out_ref)
     outs[0].start()
+    for a, b, _ in p.line:
+        put(turned.at[pl.ds(pl.multiple_of(8 * b, 8), 8)], a, b, gparts.at[c], 14)
+    pltpu.make_async_copy(turned.at[pl.ds(pl.multiple_of(8 * c, 8), 8)], gparts.at[c], recv.at[14]).start()
     convolve(r, c, 1, a3, tf, out_ref)
     outs[1].start()
 
@@ -660,14 +659,13 @@
             pltpu.VMEM((128, 512), BF16),
             pltpu.VMEM((16, 256), BF16),
             pltpu.VMEM((nc, 16, 256), BF16),
-            pltpu.VMEM((64, 256), BF16),
-            pltpu.VMEM((64, 256), BF16),
+            pltpu.VMEM((128, 512), BF16),
             pltpu.VMEM((nc, 8, 128), F32),
             pltpu.VMEM((2, 8, 128), F32),
             pltpu.VMEM((2, 8, 128), F32),
             pltpu.VMEM((per, 16, 128), F32),
-            pltpu.VMEM((2, per, 16, 128), F32),
-            pltpu.VMEM((2, 16, 128), F32),
+            pltpu.VMEM((2, per, 8, 128), F32),
+            pltpu.VMEM((2, 8, 128), F32),
             pltpu.VMEM((64, 128), F32),
             pltpu.VMEM((nc, 8, 128), F32),
             pltpu.VMEM((PIECES, 16, 128), BF16),

time: 47 us -> 47 us (level)
  no operation moved by 1% of the time
where the time goes in v12:
time: 47 us; the launch traced here: 46.8 us
  Pallas kernels  46.2 us (98%)
  between operations  0.64 us (1%)
    pallas_call x1, Pallas kernels, shards(): pl.pallas_call(functools.partial(pair_kernel, nr, nc), out_shape=(jax.Sha...  44 us
    pallas_call x1, Pallas kernels, shards(): pl.pallas_call(functools.partial(finish_kernel, 32.0 / (8 * nr * nc)), ou...  2.16 us

profile of v12, /device:TPU:1, one launch (start us, length us, event | category | flops | bytes accessed | tf_op | source)
XLA Modules:
  0.0 46.8 jit_solution(13983216560228215063)
XLA Ops:
  0.6 44.0 %pair_kernel.1 = (bf16[32,64,256]{2,1,0:T(8,128)(2,1)}, bf16[22,16,128]{2,1,0:T(8,128)(2,1)}, f32[8,512]{1,0:T(8,128)}) custom-call(bf16[8,512]{1,0:T(8,128)(2,1)} %e_hbm.1, bf16[32,512]{1,0:T(8,128)(2,1)} %bitcast.4, bf16[32,512]{1,0:T(8,128)(2,1)} %bitcast.5, bf16[9,32,32]{2,1,0:T(8,128)(2,1)} %w_hbm.1, bf16[32,64,256]{2,1,0:T(8,128)(2,1)} %cot_hbm.1), custom_call_target="tpu_custom_call" | custom-call | tf_op jit(solution)/shard_map/pair_kernel/pallas_call | solution.py:637
  44.7 2.2 %finish.1 = (f32[9,32,32]{2,1,0:T(8,128)}, f32[32,512]{1,0:T(8,128)}, f32[32,512]{1,0:T(8,128)}, f32[8,512]{1,0:T(8,128)}, bf16[32,64,256]{2,1,0:T(8,128)(2,1)}) custom-call(bf16[22,16,128]{2,1,0:T(8,128)(2,1)} %get-tuple-element.13.sums_in, f32[8,512]{1,0:T(8,128)} %get-tuple-element.14.eg_in, bf16[32,64,256]{2,1,0:T(8,128)(2,1)} %get-tuple-element.15.pair_in), custom_call_target="tpu_custom_call" | custom-call | tf_op jit(solution)/shard_map/finish/pallas_call | solution.py:686

commit v13 on v12

--- a/solution.py
+++ b/solution.py
@@ -483,11 +483,23 @@
     for k in range(PIECES - 16):
         buf[16 + k] = taps[16 * k : 16 * k + 16, :].astype(BF16)
 
-    def put_piece(k):
-        pl.when(k1 != k)(lambda: put(buf.at[k], *p.member(p.plane, k), r1.at[k1], 11))
-
-    for k in range(16, PIECES):
-        put_piece(k)
+    owner = k1 < PIECES
+
+    def put_pieces(ks):
+        def piece(k):
+            put(buf.at[k], *p.member(p.plane, k), r1.at[k1], 11)
+
+        @pl.when(owner)
+        def _():
+            for k in ks:
+                pl.when(k1 != k)(lambda k=k: piece(k))
+
+        @pl.when(jnp.logical_not(owner))
+        def _():
+            for k in ks:
+                piece(k)
+
+    put_pieces(range(16, PIECES))
     wait_bytes(eb, recv.at[0])
     e = eb[...].astype(F32)
     e = jnp.concatenate([e[:, 0:8].reshape(64, 256), e[:, 8:16].reshape(64, 256)], axis=1).astype(BF16)
@@ -519,9 +531,7 @@
         at = slice(16 * (k // 4), 16 * (k // 4) + 16), slice(128 * (k % 4), 128 * (k % 4) + 128)
         buf[k] = part[at].astype(BF16)
 
-    owner = k1 < PIECES
-    for k in range(16):
-        put_piece(k)
+    put_pieces(range(16))
     pl.when(owner)(lambda: pltpu.make_async_copy(buf.at[k1], r1.at[k1], recv.at[11]).start())
 
     outs = [

time: 47 us -> 47 us (level)
  no operation moved by 1% of the time
where the time goes in v13:
time: 47 us; the launch traced here: 46.9 us
  Pallas kernels  46.2 us (98%)
  between operations  0.64 us (1%)
    pallas_call x1, Pallas kernels, shards(): pl.pallas_call(functools.partial(pair_kernel, nr, nc), out_shape=(jax.Sha...  44.1 us
    pallas_call x1, Pallas kernels, shards(): pl.pallas_call(functools.partial(finish_kernel, 32.0 / (8 * nr * nc)), ou...  2.16 us

profile of v13, /device:TPU:1, one launch (start us, length us, event | category | flops | bytes accessed | tf_op | source)
XLA Modules:
  0.0 46.9 jit_solution(14934078013122517309)
XLA Ops:
  0.6 44.1 %pair_kernel.1 = (bf16[32,64,256]{2,1,0:T(8,128)(2,1)}, bf16[22,16,128]{2,1,0:T(8,128)(2,1)}, f32[8,512]{1,0:T(8,128)}) custom-call(bf16[8,512]{1,0:T(8,128)(2,1)} %e_hbm.1, bf16[32,512]{1,0:T(8,128)(2,1)} %bitcast.4, bf16[32,512]{1,0:T(8,128)(2,1)} %bitcast.5, bf16[9,32,32]{2,1,0:T(8,128)(2,1)} %w_hbm.1, bf16[32,64,256]{2,1,0:T(8,128)(2,1)} %cot_hbm.1), custom_call_target="tpu_custom_call" | custom-call | tf_op jit(solution)/shard_map/pair_kernel/pallas_call | solution.py:647
  44.7 2.2 %finish.1 = (f32[9,32,32]{2,1,0:T(8,128)}, f32[32,512]{1,0:T(8,128)}, f32[32,512]{1,0:T(8,128)}, f32[8,512]{1,0:T(8,128)}, bf16[32,64,256]{2,1,0:T(8,128)(2,1)}) custom-call(bf16[22,16,128]{2,1,0:T(8,128)(2,1)} %get-tuple-element.13.sums_in, f32[8,512]{1,0:T(8,128)} %get-tuple-element.14.eg_in, bf16[32,64,256]{2,1,0:T(8,128)(2,1)} %get-tuple-element.15.pair_in), custom_call_target="tpu_custom_call" | custom-call | tf_op jit(solution)/shard_map/finish/pallas_call | solution.py:696

commit v14 on v13

--- a/solution.py
+++ b/solution.py
@@ -449,8 +449,21 @@
 
     def arrive(cond, ref, sem):
         pl.when(cond)(lambda: wait_bytes(ref, sem))
-        pl.when(jnp.logical_not(cond))(lambda: ref.__setitem__(..., jnp.full(ref.shape, OUTSIDE, F32)))
-
+
+    def fill(cond, ref, value):
+        pl.when(jnp.logical_not(cond))(lambda: ref.__setitem__(..., jnp.full(ref.shape, value, F32)))
+
+    for cond, feats_in, sums_in in (
+        (p.has_up, row_feats.at[0], rends.at[1]),
+        (p.has_down, row_feats.at[1], rends.at[0]),
+        (p.has_left, col_feats.at[0], None),
+        (p.has_right, col_feats.at[1], None),
+    ):
+        fill(cond, feats_in, OUTSIDE)
+        if sums_in is not None:
+            fill(cond, sums_in, 0.0)
+    fill(p.ends_block, cends.at[0], 0.0)
+    fill(p.starts_block, cends.at[1], 0.0)
     arrive(p.has_up, row_feats.at[0], recv.at[2])
     arrive(p.has_down, row_feats.at[1], recv.at[3])
     arrive(p.has_left, col_feats.at[0], recv.at[4])
@@ -469,8 +482,17 @@
     elementwise(rowf, colf, z, act, cacc, rsum)
 
     column_sums(cacc, pick, cols)
-    for k in range(per):
-        put_other(cols.at[k], k, cparts.at[rm], 6)
+
+    @pl.when(p.in_others)
+    def _():
+        for k in range(per):
+            put_other(cols.at[k], k, cparts.at[rm], 6)
+
+    @pl.when(jnp.logical_not(p.in_others))
+    def _():
+        for k in range(per):
+            put(cols.at[k], *p.other(k), cparts.at[rm], 6)
+
     column_end_sums(cacc, pick, col_ends)
     pl.when(p.has_left)(lambda: put(col_ends.at[0], per * c - 1, rb, cends.at[0, rm], 9))
     pl.when(p.has_right)(lambda: put(col_ends.at[1], per * c + per, rb, cends.at[1, rm], 10))
@@ -505,14 +527,10 @@
     e = jnp.concatenate([e[:, 0:8].reshape(64, 256), e[:, 8:16].reshape(64, 256)], axis=1).astype(BF16)
     twice[...] = jnp.concatenate([e, e], axis=0)
 
-    def gather_sum(cond, ref, sem):
-        pl.when(cond)(lambda: wait_bytes(ref, sem))
-        pl.when(jnp.logical_not(cond))(lambda: ref.__setitem__(..., jnp.zeros(ref.shape, F32)))
-
-    gather_sum(p.has_down, rends.at[0], recv.at[7])
-    gather_sum(p.has_up, rends.at[1], recv.at[8])
-    gather_sum(p.ends_block, cends.at[0], recv.at[9])
-    gather_sum(p.starts_block, cends.at[1], recv.at[10])
+    arrive(p.has_down, rends.at[0], recv.at[7])
+    arrive(p.has_up, rends.at[1], recv.at[8])
+    arrive(p.ends_block, cends.at[0], recv.at[9])
+    arrive(p.starts_block, cends.at[1], recv.at[10])
     wait_bytes(cparts, recv.at[6])
     grads = (
         row_main[...] + jnp.concatenate([rends[1], rends[0]], axis=0),
@@ -550,8 +568,8 @@
     def _():
         wait_bytes(r1, recv.at[11])
         mid[...] = jnp.sum(r1[...].astype(F32), axis=0).astype(BF16)
-        for k in range(8):
-            pl.when(k2 != k)(lambda k=k: put(mid, *p.member(p.z_line, k), r2.at[k2], 12))
+        for a, b, _ in p.group2:
+            put(mid, a, b, r2.at[k2], 12)
         pltpu.make_async_copy(mid, r2.at[k2], recv.at[12]).start()
 
     convolve(r, c, 2, a3, tf, out_ref)

time: 47 us -> 47 us (level)
  no operation moved by 1% of the time
where the time goes in v14:
time: 47 us; the launch traced here: 46.9 us
  Pallas kernels  46.2 us (98%)
  between operations  0.64 us (1%)
    pallas_call x1, Pallas kernels, shards(): pl.pallas_call(functools.partial(pair_kernel, nr, nc), out_shape=(jax.Sha...  44.1 us
    pallas_call x1, Pallas kernels, shards(): pl.pallas_call(functools.partial(finish_kernel, 32.0 / (8 * nr * nc)), ou...  2.16 us

profile of v14, /device:TPU:1, one launch (start us, length us, event | category | flops | bytes accessed | tf_op | source)
XLA Modules:
  0.0 46.9 jit_solution(2366913981115002313)
XLA Ops:
  0.6 44.1 %pair_kernel.1 = (bf16[32,64,256]{2,1,0:T(8,128)(2,1)}, bf16[22,16,128]{2,1,0:T(8,128)(2,1)}, f32[8,512]{1,0:T(8,128)}) custom-call(bf16[8,512]{1,0:T(8,128)(2,1)} %e_hbm.1, bf16[32,512]{1,0:T(8,128)(2,1)} %bitcast.4, bf16[32,512]{1,0:T(8,128)(2,1)} %bitcast.5, bf16[9,32,32]{2,1,0:T(8,128)(2,1)} %w_hbm.1, bf16[32,64,256]{2,1,0:T(8,128)(2,1)} %cot_hbm.1), custom_call_target="tpu_custom_call" | custom-call | tf_op jit(solution)/shard_map/pair_kernel/pallas_call | solution.py:665
  44.7 2.2 %finish.1 = (f32[9,32,32]{2,1,0:T(8,128)}, f32[32,512]{1,0:T(8,128)}, f32[32,512]{1,0:T(8,128)}, f32[8,512]{1,0:T(8,128)}, bf16[32,64,256]{2,1,0:T(8,128)(2,1)}) custom-call(bf16[22,16,128]{2,1,0:T(8,128)(2,1)} %get-tuple-element.13.sums_in, f32[8,512]{1,0:T(8,128)} %get-tuple-element.14.eg_in, bf16[32,64,256]{2,1,0:T(8,128)(2,1)} %get-tuple-element.15.pair_in), custom_call_target="tpu_custom_call" | custom-call | tf_op jit(solution)/shard_map/finish/pallas_call | solution.py:714

commit v15 on v13

--- a/solution.py
+++ b/solution.py
@@ -563,8 +563,8 @@
     def _():
         wait_bytes(r2, recv.at[12])
         fin[...] = jnp.sum(r2[...].astype(F32), axis=0).astype(BF16)
-        for k in (1, 0, *range(2, 32)):
-            pl.when(k1 != k)(lambda k=k: put(fin, *p.member(p.plane, k), sums_hbm.at[k1], 13))
+        for a, b, _ in p.group1:
+            put(fin, a, b, sums_hbm.at[k1], 13)
         pltpu.make_async_copy(fin, sums_hbm.at[k1], recv.at[13]).start()
 
     wait_bytes(gparts, recv.at[14])

time: 47 us -> 47.3 us (level)
  no operation moved by 1% of the time
where the time goes in v15:
time: 47.3 us; the launch traced here: 47.2 us
  Pallas kernels  46.6 us (99%)
  between operations  0.64 us (1%)
    pallas_call x1, Pallas kernels, shards(): pl.pallas_call(functools.partial(pair_kernel, nr, nc), out_shape=(jax.Sha...  44.4 us
    pallas_call x1, Pallas kernels, shards(): pl.pallas_call(functools.partial(finish_kernel, 32.0 / (8 * nr * nc)), ou...  2.16 us

profile of v15, /device:TPU:1, one launch (start us, length us, event | category | flops | bytes accessed | tf_op | source)
XLA Modules:
  0.0 47.2 jit_solution(13173436545795290928)
XLA Ops:
  0.6 44.4 %pair_kernel.1 = (bf16[32,64,256]{2,1,0:T(8,128)(2,1)}, bf16[22,16,128]{2,1,0:T(8,128)(2,1)}, f32[8,512]{1,0:T(8,128)}) custom-call(bf16[8,512]{1,0:T(8,128)(2,1)} %e_hbm.1, bf16[32,512]{1,0:T(8,128)(2,1)} %bitcast.4, bf16[32,512]{1,0:T(8,128)(2,1)} %bitcast.5, bf16[9,32,32]{2,1,0:T(8,128)(2,1)} %w_hbm.1, bf16[32,64,256]{2,1,0:T(8,128)(2,1)} %cot_hbm.1), custom_call_target="tpu_custom_call" | custom-call | tf_op jit(solution)/shard_map/pair_kernel/pallas_call | solution.py:647
  45.0 2.2 %finish.1 = (f32[9,32,32]{2,1,0:T(8,128)}, f32[32,512]{1,0:T(8,128)}, f32[32,512]{1,0:T(8,128)}, f32[8,512]{1,0:T(8,128)}, bf16[32,64,256]{2,1,0:T(8,128)(2,1)}) custom-call(bf16[22,16,128]{2,1,0:T(8,128)(2,1)} %get-tuple-element.13.sums_in, f32[8,512]{1,0:T(8,128)} %get-tuple-element.14.eg_in, bf16[32,64,256]{2,1,0:T(8,128)(2,1)} %get-tuple-element.15.pair_in), custom_call_target="tpu_custom_call" | custom-call | tf_op jit(solution)/shard_map/finish/pallas_call | solution.py:696
